TPU v7x, 32 devices: a whole 2x2x4 slice. The times are simulated.
32 devices in a mesh: pts: 8 (over z, y), fsdp: 4 (over x, core).
Axes of the slice: x: 2, y: 2, z: 4, core: 2. Of those that a mesh axis runs over, the one named last changes fastest.
Arguments:
- points: bfloat16 [65536, 256], P(('pts', 'fsdp')), may hold values from -6 to 6
- cotangent: bfloat16 [65536, 256], P(('pts', 'fsdp')), may hold values from -6 to 6
- surface_count: int32 [32, 16], P(('pts', 'fsdp')), may hold values from 8 to 16, as said below
- volume_count: int32 [32, 16], P(('pts', 'fsdp')), may hold values from 28 to 112, as said below
- attn_weight: float32 [3, 256, 256], P(None, 'fsdp')
- attn_first: float32 [3, 256, 256], P(None, 'fsdp'), may hold values from -0.015625 to 0.015625
- attn_second: float32 [3, 256, 256], P(None, 'fsdp'), may hold values from 6.879623e-07 to 5.5036985e-06
- attn_average: float32 [3, 256, 256], P(None, 'fsdp'), may hold values from -1 to 1
- mlp_weight: float32 [2, 256, 1024], P(None, 'fsdp')
- mlp_first: float32 [2, 256, 1024], P(None, 'fsdp'), may hold values from -0.015625 to 0.015625
- mlp_second: float32 [2, 256, 1024], P(None, 'fsdp'), may hold values from 6.879623e-07 to 5.5036985e-06
- mlp_average: float32 [2, 256, 1024], P(None, 'fsdp'), may hold values from -1 to 1
- small_weight: float32 [32, 160], replicated
- small_first: float32 [32, 160], replicated, may hold values from -0.015625 to 0.015625
- small_second: float32 [32, 160], replicated, may hold values from 6.879623e-07 to 5.5036985e-06
- small_average: float32 [32, 160], replicated, may hold values from -2.5 to 2.5
- vector_params: float32 [3, 256], replicated
- vector_first: float32 [3, 256], replicated, may hold values from -0.015625 to 0.015625
- vector_second: float32 [3, 256], replicated, may hold values from 6.879623e-07 to 5.5036985e-06
- vector_average: float32 [3, 256], replicated, may hold values from 0.5 to 1.5
Outputs:
- mixed: bfloat16 [65536, 256], P(('pts', 'fsdp'))
- points_grad: float32 [65536, 256], P(('pts', 'fsdp'))
- grad_norm: float32 [], replicated
- attn_new: float32 [3, 256, 256], P(None, 'fsdp')
- attn_first_new: float32 [3, 256, 256], P(None, 'fsdp')
- attn_second_new: float32 [3, 256, 256], P(None, 'fsdp')
- attn_average_new: float32 [3, 256, 256], P(None, 'fsdp')
- attn_copy: bfloat16 [3, 256, 256], P(None, 'fsdp')
- mlp_new: float32 [2, 256, 1024], P(None, 'fsdp')
- mlp_first_new: float32 [2, 256, 1024], P(None, 'fsdp')
- mlp_second_new: float32 [2, 256, 1024], P(None, 'fsdp')
- mlp_average_new: float32 [2, 256, 1024], P(None, 'fsdp')
- mlp_copy: bfloat16 [2, 256, 1024], P(None, 'fsdp')
- small_new: float32 [32, 160], replicated
- small_first_new: float32 [32, 160], replicated
- small_second_new: float32 [32, 160], replicated
- small_average_new: float32 [32, 160], replicated
- small_copy: bfloat16 [32, 160], replicated
- vector_new: float32 [3, 256], replicated
- vector_first_new: float32 [3, 256], replicated
- vector_second_new: float32 [3, 256], replicated
- vector_average_new: float32 [3, 256], replicated
- vector_copy: bfloat16 [3, 256], replicated
Inputs may be any that keep to these rules, and one draw needn't show every extreme that they name: `surface_count`: some device holds 16 surface points of every item. `volume_count`: some device holds 112 volume points of every item.
All inputs are finite; a program needn't handle non-finite values.
Results may differ from a plain program's by a relative error of at most 0.02.
Values may be sent and summed in bfloat16 or wider, within the bound.
A program may use at most 256 MiB of HBM per device.

v0:
```python
import math

import jax
import jax.numpy as jnp
from jax import lax
from jax.sharding import PartitionSpec as P

H = 8
DH = 32
G = 64
STEP = 5


HIGH = lax.Precision.HIGHEST
NORM_EPS = 1e-05
SLICE_EPS = 1e-05
CLIP = 1.0
BETA_ONE = 0.5
BETA_TWO = 0.5
ADAM_EPS = 1e-08
DECAY = 0.01
EMA_RATE = 0.6
RATE_ATTN = 0.04
RATE_MLP = 0.03
RATE_SMALL = 0.4
RATE_VECTOR = 0.3


def layout(surface_count, volume_count, rows):
    counted = surface_count + volume_count
    ends = jnp.cumsum(counted, axis=1)
    starts = ends - counted
    position = jnp.arange(rows, dtype=jnp.int32)[None, :, None]
    inside = (position >= starts[:, None, :]) & (position < ends[:, None, :])
    surface_end = (starts + surface_count)[:, None, :]
    onehot = inside.astype(jnp.float32)
    surface = jnp.sum((inside & (position < surface_end)).astype(jnp.float32), axis=2)
    return (onehot, surface)


def layer_norm(field, gain):
    row_mean = jnp.mean(field, axis=-1, keepdims=True)
    centred = field - row_mean
    row_var = jnp.mean(centred * centred, axis=-1, keepdims=True)
    return centred * lax.rsqrt(row_var + NORM_EPS) * gain


def slice_attention(sums, totals, small):
    tokens_slice = sums / (totals[..., None] + SLICE_EPS)
    queries = jnp.einsum("bhgd,de->bhge", tokens_slice, small[:, G : G + DH], precision=HIGH)
    key_rows = jnp.einsum(
        "bhgd,de->bhge", tokens_slice, small[:, G + DH : G + 2 * DH], precision=HIGH
    )
    value_rows = jnp.einsum("bhgd,de->bhge", tokens_slice, small[:, G + 2 * DH :], precision=HIGH)
    scores = jnp.einsum("bhge,bhke->bhgk", queries, key_rows, precision=HIGH) / math.sqrt(DH)
    weights = jax.nn.softmax(scores, axis=-1)
    return jnp.einsum("bhgk,bhke->bhge", weights, value_rows, precision=HIGH)


def adamw(weight, first, second, average, grad, factor, rate):
    clipped = grad * factor
    first_new = BETA_ONE * first + (1.0 - BETA_ONE) * clipped
    second_new = BETA_TWO * second + (1.0 - BETA_TWO) * clipped * clipped
    first_hat = first_new / (1.0 - BETA_ONE**STEP)
    second_hat = second_new / (1.0 - BETA_TWO**STEP)
    new_weight = weight - rate * (first_hat / (jnp.sqrt(second_hat) + ADAM_EPS) + DECAY * weight)
    average_new = EMA_RATE * average + (1.0 - EMA_RATE) * new_weight
    return (new_weight, first_new, second_new, average_new, new_weight.astype(jnp.bfloat16))


def contract_rows(left, right):
    return lax.dot_general(
        left, right, (((0,), (0,)), ((), ())), preferred_element_type=jnp.float32
    )


def contract_cols(left, right):
    return lax.dot_general(
        left, right, (((1,), (1,)), ((), ())), preferred_element_type=jnp.float32
    )


def body(
    points,
    cotangent,
    surface_count,
    volume_count,
    attn_weight,
    attn_first,
    attn_second,
    attn_average,
    mlp_weight,
    mlp_first,
    mlp_second,
    mlp_average,
    small_weight,
    small_first,
    small_second,
    small_average,
    vector_params,
    vector_first,
    vector_second,
    vector_average,
):
    rows, width = points.shape
    onehot_all, surface_all = layout(surface_count, volume_count, rows)
    onehot = onehot_all[0]
    surface = surface_all[0]
    attn_full, mlp_full = (
        lax.all_gather(attn_weight.astype(jnp.bfloat16), "fsdp", axis=1, tiled=True),
        lax.all_gather(mlp_weight.astype(jnp.bfloat16), "fsdp", axis=1, tiled=True),
    )
    weight_x = attn_full[0]
    weight_f = attn_full[1]
    weight_o = attn_full[2]
    weight_in = mlp_full[0]
    weight_out = mlp_full[1]
    weight_slice = small_weight[:, :G].astype(jnp.bfloat16)
    start = points.astype(jnp.float32) + surface[:, None] * vector_params[2]
    normed_full, norm_one_pull = jax.vjp(layer_norm, start, vector_params[0])
    normed = normed_full.astype(jnp.bfloat16)
    mid_x = jnp.dot(normed, weight_x, preferred_element_type=jnp.float32).astype(jnp.bfloat16)
    mid_f = jnp.dot(normed, weight_f, preferred_element_type=jnp.float32).astype(jnp.bfloat16)
    flat_x = mid_x.reshape(-1, DH)
    logits = jnp.dot(flat_x, weight_slice, preferred_element_type=jnp.float32).reshape(rows, H, G)
    slice_prob = jax.nn.softmax(logits, axis=-1)
    prob_low = slice_prob.astype(jnp.bfloat16)
    masked = onehot.astype(jnp.bfloat16)[:, :, None, None] * prob_low[:, None, :, :]
    features = mid_f.reshape(rows, H, DH)
    part_sums = jnp.einsum("nbhg,nhd->bhgd", masked, features, preferred_element_type=jnp.float32)
    part_totals = jnp.sum(masked, axis=0, dtype=jnp.float32)
    slice_sum, slice_total = lax.psum((part_sums, part_totals), ("pts", "fsdp"))
    slice_raw, slice_pull = jax.vjp(slice_attention, slice_sum, slice_total, small_weight)
    slice_out = slice_raw.astype(jnp.bfloat16)
    mixed_heads = (
        jnp.einsum("nbhg,bhgd->nhd", masked, slice_out, preferred_element_type=jnp.float32)
        .reshape(rows, width)
        .astype(jnp.bfloat16)
    )
    middle = start + jnp.dot(mixed_heads, weight_o, preferred_element_type=jnp.float32)
    normed_two_full, norm_two_pull = jax.vjp(layer_norm, middle, vector_params[1])
    normed_two = normed_two_full.astype(jnp.bfloat16)
    hidden = jnp.dot(normed_two, weight_in, preferred_element_type=jnp.float32)
    active_full, gelu_pull = jax.vjp(jax.nn.gelu, hidden)
    active = active_full.astype(jnp.bfloat16)
    mixed = (middle + contract_cols(active, weight_out)).astype(jnp.bfloat16)
    grad_out_w = contract_rows(cotangent, active)
    d_active = jnp.dot(cotangent, weight_out, preferred_element_type=jnp.float32)
    (d_hidden_full,) = gelu_pull(d_active)
    d_hidden = d_hidden_full.astype(jnp.bfloat16)
    grad_in_w = contract_rows(normed_two, d_hidden)
    d_normed_two = contract_cols(d_hidden, weight_in)
    d_middle_norm, grad_gain_two = norm_two_pull(d_normed_two)
    d_middle = cotangent.astype(jnp.float32) + d_middle_norm
    d_branch = d_middle.astype(jnp.bfloat16)
    grad_o_w = contract_rows(mixed_heads, d_branch)
    d_heads = contract_cols(d_branch, weight_o).astype(jnp.bfloat16).reshape(rows, H, DH)
    part_back = jnp.einsum("nbhg,nhd->bhgd", masked, d_heads, preferred_element_type=jnp.float32)
    d_slice_out = lax.psum(part_back, ("pts", "fsdp"))
    d_sum_full, d_total, grad_small_attn = slice_pull(d_slice_out)
    d_sum = d_sum_full.astype(jnp.bfloat16)
    d_masked = (
        jnp.einsum("nhd,bhgd->nbhg", d_heads, slice_out, preferred_element_type=jnp.float32)
        + jnp.einsum("nhd,bhgd->nbhg", features, d_sum, preferred_element_type=jnp.float32)
        + d_total[None]
    )
    d_prob = jnp.sum(d_masked * onehot[:, :, None, None], axis=1)
    d_logits = slice_prob * (d_prob - jnp.sum(slice_prob * d_prob, axis=-1, keepdims=True))
    flat_d = d_logits.astype(jnp.bfloat16).reshape(-1, G)
    grad_slice_w = contract_rows(flat_x, flat_d)
    d_mid_x = contract_cols(flat_d, weight_slice).reshape(rows, width).astype(jnp.bfloat16)
    d_mid_f = (
        jnp.einsum("nbhg,bhgd->nhd", masked, d_sum, preferred_element_type=jnp.float32)
        .reshape(rows, width)
        .astype(jnp.bfloat16)
    )
    grad_x_w = contract_rows(normed, d_mid_x)
    grad_f_w = contract_rows(normed, d_mid_f)
    d_normed = contract_cols(d_mid_x, weight_x) + contract_cols(d_mid_f, weight_f)
    d_start_norm, grad_gain_one = norm_one_pull(d_normed)
    points_grad = d_middle + d_start_norm
    grad_embed = jnp.sum(points_grad * surface[:, None], axis=0)
    grad_attn = jnp.stack([grad_x_w, grad_f_w, grad_o_w])
    grad_mlp = jnp.stack([grad_in_w, grad_out_w])
    grad_vector_local = jnp.stack([grad_gain_one, grad_gain_two, grad_embed])
    summed_attn, summed_mlp = lax.psum((grad_attn, grad_mlp), "pts")
    shard_attn, shard_mlp = (
        lax.psum_scatter(
            summed_attn.astype(jnp.bfloat16), "fsdp", scatter_dimension=1, tiled=True
        ).astype(jnp.float32),
        lax.psum_scatter(
            summed_mlp.astype(jnp.bfloat16), "fsdp", scatter_dimension=1, tiled=True
        ).astype(jnp.float32),
    )
    slice_grad_total, grad_vector = lax.psum((grad_slice_w, grad_vector_local), ("pts", "fsdp"))
    grad_small = grad_small_attn + jnp.pad(slice_grad_total, ((0, 0), (0, 3 * DH)))
    big_squares = jnp.sum(shard_attn * shard_attn) + jnp.sum(shard_mlp * shard_mlp)
    all_big = lax.psum(big_squares, "fsdp")
    grad_norm = jnp.sqrt(
        all_big + jnp.sum(grad_small * grad_small) + jnp.sum(grad_vector * grad_vector)
    )
    factor = jnp.minimum(1.0, CLIP / grad_norm)
    attn_state = adamw(
        attn_weight, attn_first, attn_second, attn_average, shard_attn, factor, RATE_ATTN
    )
    mlp_state = adamw(mlp_weight, mlp_first, mlp_second, mlp_average, shard_mlp, factor, RATE_MLP)
    small_state = adamw(
        small_weight, small_first, small_second, small_average, grad_small, factor, RATE_SMALL
    )
    vector_state = adamw(
        vector_params, vector_first, vector_second, vector_average, grad_vector, factor, RATE_VECTOR
    )
    return (
        mixed,
        points_grad,
        grad_norm,
        attn_state[0],
        attn_state[1],
        attn_state[2],
        attn_state[3],
        attn_state[4],
        mlp_state[0],
        mlp_state[1],
        mlp_state[2],
        mlp_state[3],
        mlp_state[4],
        small_state[0],
        small_state[1],
        small_state[2],
        small_state[3],
        small_state[4],
        vector_state[0],
        vector_state[1],
        vector_state[2],
        vector_state[3],
        vector_state[4],
    )


def solution(mesh):
    in_specs = (
        P(("pts", "fsdp"), None),
        P(("pts", "fsdp"), None),
        P(("pts", "fsdp"), None),
        P(("pts", "fsdp"), None),
        P(None, "fsdp", None),
        P(None, "fsdp", None),
        P(None, "fsdp", None),
        P(None, "fsdp", None),
        P(None, "fsdp", None),
        P(None, "fsdp", None),
        P(None, "fsdp", None),
        P(None, "fsdp", None),
        P(),
        P(),
        P(),
        P(),
        P(),
        P(),
        P(),
        P(),
    )
    out_specs = (
        P(("pts", "fsdp"), None),
        P(("pts", "fsdp"), None),
        P(),
        P(None, "fsdp", None),
        P(None, "fsdp", None),
        P(None, "fsdp", None),
        P(None, "fsdp", None),
        P(None, "fsdp", None),
        P(None, "fsdp", None),
        P(None, "fsdp", None),
        P(None, "fsdp", None),
        P(None, "fsdp", None),
        P(None, "fsdp", None),
        P(),
        P(),
        P(),
        P(),
        P(),
        P(),
        P(),
        P(),
        P(),
        P(),
    )
    return jax.shard_map(body, mesh=mesh, in_specs=in_specs, out_specs=out_specs, check_vma=False)
```

profile of v0, /device:TPU:0, one launch (start us, length us, event | category | flops | bytes accessed | tf_op | source)
XLA Modules:
  0.0 722.3 jit_solution(6349833401550390353)
XLA Ops:
  12.8 7.9 %all_gather.6 = bf16[3,256,256]{2,1,0:T(8,128)(2,1)S(1)} all-gather(bf16[3,64,256]{2,1,0:T(8,128)(2,1)S(1)} %convert_element_type.144), channel_id=1, replica_groups=mesh['pts'=8,'fsdp'=4] {'fsdp'}, dimensions={1}, use_global_device_ids=true | all-gather | bytes 491520 | tf_op jit(solution)/shard_map/all_gather | solution.py:110
  25.5 4.8 fusion.144
  34.4 17.4 %fusion.60 = f32[16,8,64,32]{2,3,0,1:T(8,128)} fusion(bf16[2048,8,32,1]{0,2,3,1:T(8,128)(2,1)S(1)} %bitcast.183, bf16[2048,8,64]{0,2,1:T(8,128)(2,1)S(1)} %fusion.131, bf16[2048,16]{0,1:T(8,128)(2,1)S(1)} %copy-done.74), kind=kOutput, calls=%fused_computation.88 | convolution fusion | flops 1140850688 | bytes 4259840 | tf_op jit(solution)/shard_map/nbhg,nhd->bhgd/dot_general | solution.py:130
  54.2 20.5 %convert_reduce_fusion = f32[16,8,64]{2,0,1:T(8,128)} fusion(bf16[2048,8,64]{0,2,1:T(8,128)(2,1)} %copy-done.12, bf16[2048,16]{0,1:T(8,128)(2,1)} %get-tuple-element.172), kind=kLoop, calls=%fused_computation.5 | loop fusion | flops 50323456 | bytes 2195456 | tf_op jit(solution)/shard_map/reduce_sum | solution.py:131
  76.2 3.3 reshape.370
  79.5 41.0 %psum.57 = f32[16,8,64]{2,0,1:T(8,128)S(1)} all-reduce(f32[16,8,64]{2,0,1:T(8,128)S(1)} %copy-done.79), channel_id=1, replica_groups=mesh['pts'=8,'fsdp'=4] {'pts','fsdp'}, use_global_device_ids=true, to_apply=%region_8.9 | all-reduce | flops 8192 | bytes 65536 | tf_op jit(solution)/shard_map/psum | solution.py:132
  121.1 67.5 %all-reduce.10.cloned.1.call-done = f32[16,8,64,32]{2,3,0,1:T(8,128)} async-done(((f32[16,8,64,32]{2,3,0,1:T(8,128)}), f32[16,8,64,32]{2,3,0,1:T(8,128)}) %all-reduce.10.cloned.1.call-update) | async-done | bytes 1048592 | tf_op jit(solution)/shard_map/psum | solution.py:132
  188.7 3.8 fusion.74
  195.5 7.0 multiply_reduce_fusion.2
  206.0 4.6 convolution_convert_fusion.4
  210.6 7.5 %fusion.37 = bf16[8,32,2048]{2,1,0:T(8,128)(2,1)S(1)} fusion(bf16[16,8,64,32]{2,3,1,0:T(8,128)(2,1)S(1)} %convolution_convert_fusion.4, bf16[2048,8,64]{0,2,1:T(8,128)(2,1)S(1)} %copy-done.13, bf16[2048,16]{0,1:T(8,128)(2,1)S(1)} %copy-done.75), kind=kOutput, calls=%fused_computation.50 | convolution fusion | flops 1091043328 | bytes 3735552 | tf_op jit(solution)/shard_map/nbhg,bhgd->nhd/dot_general | solution.py:136
  222.8 4.4 convolution_bitcast_fusion
  227.2 6.3 fusion.24
  239.7 17.4 %fusion.63 = f32[16,8,64,32]{2,3,0,1:T(8,128)} fusion(bf16[2048,8,32,1]{0,2,3,1:T(8,128)(2,1)S(1)} %bitcast.185, bf16[2048,8,64]{0,2,1:T(8,128)(2,1)S(1)} %copy-done.14, bf16[2048,16]{0,1:T(8,128)(2,1)S(1)} %copy-done.76), kind=kOutput, calls=%fused_computation.89 | convolution fusion | flops 1140850688 | bytes 4259840 | tf_op jit(solution)/shard_map/nbhg,nhd->bhgd/dot_general | solution.py:158
  257.1 24.6 %fusion.88 = f32[8,16,64,2048]{3,2,1,0:T(8,128)} fusion(bf16[2048,8,32,1]{0,2,3,1:T(8,128)(2,1)} %bitcast.186, bf16[16,8,64,32]{2,3,1,0:T(8,128)(2,1)} %copy-done.43), kind=kOutput, calls=%fused_computation.112 | convolution fusion | flops 1073741824 | bytes 68681728 | tf_op jit(solution)/shard_map/nhd,bhgd->nbhg/dot_general | solution.py:163
  282.2 7.8 %fusion.40 = bf16[2048,256]{0,1:T(8,128)(2,1)} fusion(f32[2048,256]{0,1:T(8,128)S(1)} %get-tuple-element.180, bf16[2,256,1024]{2,1,0:T(8,128)(2,1)} %all-gather.2.cloned.1.call-done, f32[2048,1024]{1,0:T(8,128)} %copy-done.6), kind=kOutput, calls=%fused_computation.51 | convolution fusion | flops 1093664768 | bytes 12058624 | tf_op jit(solution)/shard_map/dot_general | solution.py:78
  297.6 117.0 %all-reduce.12.cloned.1.call-done = f32[16,8,64,32]{2,3,0,1:T(8,128)} async-done(((f32[16,8,64,32]{2,3,0,1:T(8,128)}), f32[16,8,64,32]{2,3,0,1:T(8,128)}) %all-reduce.12.cloned.1.call-update) | async-done | bytes 1048592 | tf_op jit(solution)/shard_map/psum | solution.py:159
  414.7 10.0 %multiply_reduce_fusion.1 = (f32[16,8,64]{2,1,0:T(8,128)S(1)}, f32[16,8,64,64]{2,3,1,0:T(8,128)S(1)}) fusion(f32[16,8,64]{2,1,0:T(8,128)S(1)} %copy-done.72, f32[16,8,64]{2,1,0:T(8,128)S(1)} %copy-done.53, f32[16,8,64,64]{2,3,1,0:T(8,128)} %copy-done.2, f32[16,8,64,32]{2,3,1,0:T(8,128)S(1)} %copy-done.26, f32[16,8,64,32]{2,3,0,1:T(8,128)} %all-reduce.12.cloned.1.call-done), kind=kOutput, calls=%fused_computation.39 | convolution fusion | flops 203939840 | bytes 6389760 | tf_op jit(solution)/shard_map/transpose(jvp(bhgk,bhke->bhge))/dot_general | solution.py:57
  424.8 4.9 fusion.132
  429.7 8.0 %fusion.133 = f32[16,8,64,32]{2,3,1,0:T(8,128)S(1)} fusion(f32[16,8,64,32]{2,3,1,0:T(8,128)S(1)} %copy-done.40, f32[16,8,64,64]{2,3,1,0:T(8,128)S(1)} %get-tuple-element.183, f32[16,8,64]{2,1,0:T(8,128)S(1)} %neg.22, f32[16,8,64]{2,1,0:T(8,128)S(1)} %copy-done.71, f32[16,8,64]{2,1,0:T(8,128)S(1)} %copy-done.53, f32[16,8,64,64]{2,3,1,0:T(8,128)S(1)} %copy-done.3), kind=kOutput, calls=%fused_computation.204 | convolution fusion | flops 204472320 | bytes 6389760 | tf_op jit(solution)/shard_map/transpose(jvp(bhge,bhke->bhgk))/dot_general | solution.py:55
  441.6 7.4 %fusion.55 = f32[16,8,64,32]{2,3,1,0:T(8,128)S(1)} fusion(f32[16,8,64,32]{2,3,0,1:T(8,128)S(1)} %copy-done.27, f32[16,8,64]{2,1,0:T(8,128)S(1)} %copy-done.71, f32[16,8,64]{2,1,0:T(8,128)S(1)} %copy-done.53, f32[16,8,64,64]{2,3,1,0:T(8,128)S(1)} %copy-done.3), kind=kOutput, calls=%fused_computation.85 | convolution fusion | flops 202899456 | bytes 4259840 | tf_op jit(solution)/shard_map/transpose(jvp(bhgk,bhke->bhge))/dot_general | solution.py:57
  452.0 7.2 %fusion.41 = bf16[8,32,2048]{2,1,0:T(8,128)(2,1)} fusion(bf16[2048,8,64]{0,2,1:T(8,128)(2,1)S(1)} %copy-done.15, bf16[2048,16]{0,1:T(8,128)(2,1)S(1)} %copy-done.77, f32[16,8,64,32]{2,3,0,1:T(8,128)S(1)} %get-tuple-element.185, f32[16,8,64]{2,0,1:T(8,128)S(1)} %copy-done.68), kind=kOutput, calls=%fused_computation.55 | convolution fusion | flops 1091567616 | bytes 4292608 | tf_op jit(solution)/shard_map/nbhg,bhgd->nhd/dot_general | solution.py:173
  459.3 25.6 %fusion.3 = f32[2048,8,64]{0,2,1:T(8,128)} fusion(f32[8,16,64,2048]{3,2,1,0:T(8,128)} %fusion.88, f32[2048,16]{0,1:T(8,128)S(1)} %copy-done.9, f32[16,8,64]{2,0,1:T(8,128)S(1)} %neg.23, bf16[2048,8,32,1]{0,2,3,1:T(8,128)(2,1)S(1)} %bitcast.184, f32[16,8,64,32]{2,3,0,1:T(8,128)S(1)} %get-tuple-element.185, f32[16,8,64]{2,0,1:T(8,128)S(1)} %copy-done.68), kind=kOutput, calls=%fused_computation.4 | convolution fusion | flops 1140326400 | bytes 73596928 | tf_op jit(solution)/shard_map/nhd,bhgd->nbhg/dot_general | solution.py:164
  484.9 7.0 multiply_convert_fusion.1
  491.9 4.2 copy.220
  496.1 3.7 convolution_convert_fusion
  503.1 5.4 convert_element_type.166
  512.8 115.9 %all-reduce.13 = (bf16[3,256,256]{2,1,0:T(8,128)(2,1)}, bf16[2,256,1024]{2,1,0:T(8,128)(2,1)}) all-reduce(f32[3,256,256]{2,1,0:T(8,128)} %pad_maximum_fusion.1, f32[2,256,1024]{2,1,0:T(8,128)} %pad_maximum_fusion), channel_id=1, replica_groups=mesh['pts'=8,'fsdp'=4] {'pts'}, use_global_device_ids=true, to_apply=%region_22.23 | all-reduce | flops 720896 | bytes 4325376 | tf_op jit(solution)/shard_map/psum | solution.py:186
  634.3 4.8 fusion.25
  639.0 38.7 %all-reduce.4 = (f32[32,64]{1,0:T(8,128)S(1)}, f32[3,256]{1,0:T(4,128)S(1)}) all-reduce(f32[32,64]{1,0:T(8,128)S(1)} %fusion.25, f32[3,256]{1,0:T(4,128)S(1)} %pad_maximum_fusion.2), channel_id=1, replica_groups=mesh['pts'=8,'fsdp'=4] {'pts','fsdp'}, use_global_device_ids=true, to_apply=%region_29.30 | all-reduce | flops 2816 | bytes 22528 | tf_op jit(solution)/shard_map/psum | solution.py:195
  677.8 4.4 fusion.82
  694.0 6.6 psum.61
  (288 shorter events, 84.0 us)
Async XLA Ops:
  8.0 180.6 %all-reduce.10.cloned.1.call-start = ((), (), s32[]{:S(2)}) async-start(), calls=%async_computation.2 | async-start | bytes 4194304 | tf_op jit(solution)/shard_map/psum | solution.py:132
  11.0 12.3 %copy-start.91 = (f32[1,256]{1,0:T(1,128)}, f32[1,256]{1,0:T(1,128)S(1)}, u32[]{:S(2)}) copy-start(f32[1,256]{1,0:T(1,128)S(1)} %get-tuple-element.169) | copy-start | bytes 3076
  11.0 208.0 %copy-start.89 = (f32[1,256]{1,0:T(1,128)}, f32[1,256]{1,0:T(1,128)S(1)}, u32[]{:S(2)}) copy-start(f32[1,256]{1,0:T(1,128)S(1)} %get-tuple-element.170) | copy-start | bytes 3076
  11.9 207.1 %copy-start.54 = (f32[2048]{0:T(1024)}, f32[2048]{0:T(1024)S(1)}, u32[]{:S(2)}) copy-start(f32[2048]{0:T(1024)S(1)} %convert_reduce_fusion.1) | copy-start | bytes 24580
  20.7 216.5 %copy-start.23 = (bf16[3,256,256]{2,1,0:T(8,128)(2,1)}, bf16[3,256,256]{2,1,0:T(8,128)(2,1)S(1)}, u32[]{:S(2)}) copy-start(bf16[3,256,256]{2,1,0:T(8,128)(2,1)S(1)} %all_gather.6) | copy-start | bytes 1179652
  22.4 196.6 %copy-start = (bf16[2048,256]{0,1:T(8,128)(2,1)}, bf16[2048,256]{0,1:T(8,128)(2,1)S(1)}, u32[]{:S(2)}) copy-start(bf16[2048,256]{0,1:T(8,128)(2,1)S(1)} %copy.193) | copy-start | bytes 3145732
  51.9 168.0 %all-gather.2.cloned.1.call-start = ((), (), s32[]{:S(2)}) async-start(), calls=%async_computation.3 | async-start | bytes 1310720 | tf_op jit(solution)/shard_map/all_gather | solution.py:111
  53.7 361.0 %all-reduce.12.cloned.1.call-start = ((), (), s32[]{:S(2)}) async-start(), calls=%async_computation.4 | async-start | bytes 4194304 | tf_op jit(solution)/shard_map/psum | solution.py:159
  54.2 20.5 %copy-start.44 = (bf16[2048,256]{1,0:T(8,128)(2,1)S(1)}, bf16[2048,256]{1,0:T(8,128)(2,1)}, u32[]{:S(2)}) copy-start(bf16[2048,256]{1,0:T(8,128)(2,1)} %param.21) | copy-start | bytes 3145732
  76.2 112.5 %copy-start.59 = (f32[32,160]{1,0:T(8,128)S(1)}, f32[32,160]{1,0:T(8,128)}, u32[]{:S(2)}) copy-start(f32[32,160]{1,0:T(8,128)} %param.32) | copy-start | bytes 61444
  121.1 67.5 %copy-start.66 = (f32[16,8,64]{2,0,1:T(8,128)}, f32[16,8,64]{2,0,1:T(8,128)S(1)}, u32[]{:S(2)}) copy-start(f32[16,8,64]{2,0,1:T(8,128)S(1)} %get-tuple-element.167) | copy-start | bytes 98308
  204.0 14.2 %copy-start.70 = (f32[16,8,64]{2,1,0:T(8,128)}, f32[16,8,64]{2,1,0:T(8,128)S(1)}, u32[]{:S(2)}) copy-start(f32[16,8,64]{2,1,0:T(8,128)S(1)} %fusion.57) | copy-start | bytes 98308
  281.7 405.8 %reduce-scatter.3.cloned.1.call-start = ((), (), s32[]{:S(2)}) async-start(), calls=%async_computation.5 | async-start | bytes 491520 | tf_op jit(solution)/shard_map/reduce_scatter | solution.py:188
  296.4 118.2 %copy-start.26 = (f32[16,8,64,32]{2,3,1,0:T(8,128)S(1)}, f32[16,8,64,32]{2,3,1,0:T(8,128)}, u32[]{:S(2)}) copy-start(f32[16,8,64,32]{2,3,1,0:T(8,128)} %copy-done.25) | copy-start | bytes 3145732
  296.4 118.2 %copy-start.53 = (f32[16,8,64]{2,1,0:T(8,128)S(1)}, f32[16,8,64]{2,1,0:T(8,128)}, u32[]{:S(2)}) copy-start(f32[16,8,64]{2,1,0:T(8,128)} %copy-done.52) | copy-start | bytes 98308
  296.4 118.2 %copy-start.72 = (f32[16,8,64]{2,1,0:T(8,128)S(1)}, f32[16,8,64]{2,1,0:T(8,128)}, u32[]{:S(2)}) copy-start(f32[16,8,64]{2,1,0:T(8,128)} %copy.212) | copy-start | bytes 98308
  297.6 127.1 %copy-start.71 = (f32[16,8,64]{2,1,0:T(8,128)S(1)}, f32[16,8,64]{2,1,0:T(8,128)}, u32[]{:S(2)}) copy-start(f32[16,8,64]{2,1,0:T(8,128)} %copy-done.70) | copy-start | bytes 98308
  459.3 25.6 %copy-start.78 = (f32[2048,8]{0,1:T(8,128)S(1)}, f32[2048,8]{0,1:T(8,128)}, u32[]{:S(2)}) copy-start(f32[2048,8]{0,1:T(8,128)} %get-tuple-element.175) | copy-start | bytes 196612
  511.8 117.0 %copy-start.1 = (bf16[2048,256]{0,1:T(8,128)(2,1)S(1)}, bf16[2048,256]{0,1:T(8,128)(2,1)}, u32[]{:S(2)}) copy-start(bf16[2048,256]{0,1:T(8,128)(2,1)} %copy-done) | copy-start | bytes 3145732
  511.8 117.0 %copy-start.16 = (f32[2048,256]{0,1:T(8,128)S(1)}, f32[2048,256]{0,1:T(8,128)}, u32[]{:S(2)}) copy-start(f32[2048,256]{0,1:T(8,128)} %fusion.102) | copy-start | bytes 6291460
  511.8 117.0 %copy-start.55 = (f32[2048]{0:T(1024)S(1)}, f32[2048]{0:T(1024)}, u32[]{:S(2)}) copy-start(f32[2048]{0:T(1024)} %copy-done.54) | copy-start | bytes 24580
  511.8 117.0 %copy-start.65 = (f32[2048]{0:T(1024)S(1)}, f32[2048]{0:T(1024)}, u32[]{:S(2)}) copy-start(f32[2048]{0:T(1024)} %copy-done.64) | copy-start | bytes 24580
  628.8 60.3 %reduce-scatter.5.cloned.1.call-start = ((), (), s32[]{:S(2)}) async-start(), calls=%async_computation.6 | async-start | bytes 1310720 | tf_op jit(solution)/shard_map/reduce_scatter | solution.py:191
  634.3 43.5 %copy-start.69 = (f32[16,8,64]{2,0,1:T(8,128)S(1)}, f32[16,8,64]{2,0,1:T(8,128)}, u32[]{:S(2)}) copy-start(f32[16,8,64]{2,0,1:T(8,128)} %copy-done.66) | copy-start | bytes 98308
  692.1 12.5 %copy-start.62 = (f32[32,160]{1,0:T(8,128)S(1)}, f32[32,160]{1,0:T(8,128)}, u32[]{:S(2)}) copy-start(f32[32,160]{1,0:T(8,128)} %param.32) | copy-start | bytes 61444
  692.1 15.4 %copy-start.50 = (f32[3,64,256]{2,1,0:T(8,128)S(1)}, f32[3,64,256]{2,1,0:T(8,128)}, u32[]{:S(2)}) copy-start(f32[3,64,256]{2,1,0:T(8,128)} %param.24) | copy-start | bytes 589828
  692.1 15.3 %copy-start.63 = (bf16[3,64,256]{2,1,0:T(8,128)(2,1)S(1)}, bf16[3,64,256]{2,1,0:T(8,128)(2,1)}, u32[]{:S(2)}) copy-start(bf16[3,64,256]{2,1,0:T(8,128)(2,1)} %reduce-scatter.3.cloned.1.call-done) | copy-start | bytes 294916
  692.1 15.3 %copy-start.81 = (f32[3,64,256]{2,1,0:T(8,128)S(1)}, f32[3,64,256]{2,1,0:T(8,128)}, u32[]{:S(2)}) copy-start(f32[3,64,256]{2,1,0:T(8,128)} %param.25) | copy-start | bytes 589828
  694.0 17.1 %copy-start.33 = (f32[2,64,1024]{2,1,0:T(8,128)S(1)}, f32[2,64,1024]{2,1,0:T(8,128)}, u32[]{:S(2)}) copy-start(f32[2,64,1024]{2,1,0:T(8,128)} %param.28) | copy-start | bytes 1572868
  694.0 17.1 %copy-start.49 = (bf16[2,64,1024]{2,1,0:T(8,128)(2,1)S(1)}, bf16[2,64,1024]{2,1,0:T(8,128)(2,1)}, u32[]{:S(2)}) copy-start(bf16[2,64,1024]{2,1,0:T(8,128)(2,1)} %reduce-scatter.5.cloned.1.call-done) | copy-start | bytes 786436
  694.0 17.1 %copy-start.57 = (f32[2,64,1024]{2,1,0:T(8,128)S(1)}, f32[2,64,1024]{2,1,0:T(8,128)}, u32[]{:S(2)}) copy-start(f32[2,64,1024]{2,1,0:T(8,128)} %param.29) | copy-start | bytes 1572868
  694.0 17.1 %copy-start.58 = (f32[2,64,1024]{2,1,0:T(8,128)S(1)}, f32[2,64,1024]{2,1,0:T(8,128)}, u32[]{:S(2)}) copy-start(f32[2,64,1024]{2,1,0:T(8,128)} %param.30) | copy-start | bytes 1572868
  (75 other events, 294.2 us)
Sparse Core Ops, SparseCore 0:
  52.0 136.6 all-reduce.9
  281.9 132.7 all-reduce.11
Sparse Core Ops, SparseCore 1:
  54.6 17.8 all-gather.1
  628.8 19.1 reduce-scatter.2
  650.4 24.6 reduce-scatter.4
where the time goes:
time: 730 us; the launch traced here: 722 us
  matrix products  212 us (29%)
  blocking collectives  210 us (29%)
  waiting for transfers between devices  185 us (25%)
  other arithmetic  59.5 us (8%)
  local copies, waits for them, and re-layouts  33.4 us (5%)
  between operations  21.7 us (3%)
    psum x1, waiting for transfers between devices, body(): d_slice_out = lax.psum(part_back, ('pts', 'fsdp'))  117 us
    psum x1, blocking collectives, body(): summed_attn, summed_mlp = lax.psum((grad_attn, grad_mlp), 'pts')  116 us
    psum x1, waiting for transfers between devices, body(): slice_sum, slice_total = lax.psum((part_sums, part_totals), ('pts', 'fsdp'))  67.5 us
    psum x1, blocking collectives, body(): slice_sum, slice_total = lax.psum((part_sums, part_totals), ('pts', 'fsdp'))  41 us
    psum x1, blocking collectives, body(): lax.psum((grad_slice_w, grad_vector_local), ('pts', 'fsdp'))  38.7 us
    dot_general x1, matrix products, body(): jnp.einsum('nhd,bhgd->nbhg', features, d_sum, preferred_element_type=jnp....  25.6 us
    dot_general x1, matrix products, body(): jnp.einsum('nhd,bhgd->nbhg', d_heads, slice_out, preferred_element_type=j...  24.6 us
    dot_general x3, matrix products, slice_attention(): return jnp.einsum('bhgk,bhke->bhge', weights, value_rows, precision=HIGH)  22 us
  transfers between devices with their start and end apart: 5, of which 2 were waited for; matrix products, arithmetic and copies ran while one was open for 13% of the time, Pallas kernels for 0%

commit v1 on v0

v1 whole, which is shorter than its diff:
```python
import functools
import math

import jax
import jax.numpy as jnp
from jax import lax
from jax.experimental import pallas as pl
from jax.experimental.pallas import tpu as pltpu
from jax.sharding import PartitionSpec as P

C = 256
H = 8
DH = 32
G = 64
FF = 1024
ITEMS = 16
STEP = 5
W = 256
NORM_EPS = 1e-05
SLICE_EPS = 1e-05
CLIP = 1.0
BETA_ONE = 0.5
BETA_TWO = 0.5
ADAM_EPS = 1e-08
DECAY = 0.01
EMA_RATE = 0.6
RATE_ATTN = 0.04
RATE_MLP = 0.03
RATE_SMALL = 0.4
RATE_VECTOR = 0.3
ZO = 4
CH = 80
CB = 144
CL = 32
SM = 80
MESH = pl.DeviceIdType.MESH
HIGH = lax.Precision.HIGHEST
F32 = jnp.float32
BF = jnp.bfloat16
GELU_A = math.sqrt(2.0 / math.pi)
GELU_B = GELU_A * 0.044715


def nn(a, b, precision=None):
    return lax.dot_general(a, b, (((1,), (0,)), ((), ())), precision=precision, preferred_element_type=F32)


def nt(a, b, precision=None):
    return lax.dot_general(a, b, (((1,), (1,)), ((), ())), precision=precision, preferred_element_type=F32)


def tn(a, b, precision=None):
    return lax.dot_general(a, b, (((0,), (0,)), ((), ())), precision=precision, preferred_element_type=F32)


def iota(shape, dim):
    return lax.broadcasted_iota(jnp.int32, shape, dim)


def tile_of(i, width=W):
    return pl.ds(pl.multiple_of(i * width, width), width)


class Place:
    def __init__(self, zs):
        self.p = lax.axis_index("pts")
        self.f = lax.axis_index("fsdp")
        self.a = self.f % 2
        self.x = self.f // 2
        self.y = self.p % 2
        self.z = self.p // 2
        self.m = self.x * 2 + self.y
        self.zs = zs
        self.core = (self.p, self.f + 1 - 2 * self.a)
        self.xpeer = (self.p, (1 - self.x) * 2 + self.a)
        self.ypeer = (self.z * 2 + 1 - self.y, self.f)
        self.zown = self.z if zs == ZO else jnp.minimum(self.z, ZO - 1)

    def xy(self, k):
        mm = (self.m + k) % 4
        return mm, (self.z * 2 + mm % 2, (mm // 2) * 2 + self.a)

    def xy_other(self, k):
        mm = (self.m + k) % 4
        return mm, (self.z * 2 + mm % 2, (mm // 2) * 2 + 1 - self.a)

    def zl(self, k):
        zz = (self.z + k) % self.zs
        return zz, (zz * 2 + self.y, self.f)

    def barrier(self, crossed=False):
        b = pltpu.get_barrier_semaphore()
        peers = [self.core] + [self.xy(k)[1] for k in (1, 2, 3)] + [self.zl(k)[1] for k in range(1, self.zs)]
        if crossed:
            peers += [self.xy_other(k)[1] for k in (1, 2, 3)]
        for d in peers:
            pl.semaphore_signal(b, inc=1, device_id=d, device_id_type=MESH)
        pl.semaphore_wait(b, len(peers))

    def owned(self, z, fn):
        if self.zs == ZO:
            fn()
        else:
            pl.when(z < ZO)(fn)


def rcopy(src, dst, ss, rs, dev):
    return pltpu.make_async_remote_copy(
        src_ref=src, dst_ref=dst, send_sem=ss, recv_sem=rs, device_id=dev, device_id_type=MESH
    )


class Reduce:
    def __init__(self, g, src, bufs):
        self.g, self.src = g, src
        self.r1, self.s2, self.r2, self.s3, self.r3, self.sem = bufs
        self.c1, self.c2, self.c3 = {}, [], []

    @staticmethod
    def scratch(rows, zs):
        return [
            pltpu.VMEM((4, ZO, rows, 128), BF),
            pltpu.VMEM((3, ZO, rows, 128), BF),
            pltpu.VMEM((3, ZO, rows, 128), BF),
            pltpu.VMEM((ZO, rows, 128), BF),
            pltpu.VMEM((zs - 1, rows, 128), BF),
            pltpu.SemaphoreType.DMA((6, max(zs, 4))),
        ]

    def core(self, k):
        g = self.g
        mm = (g.m + k) % 4
        c = rcopy(self.src.at[1 - g.a, mm], self.r1.at[mm], self.sem.at[0, k], self.sem.at[1, k], g.core)
        c.start()
        self.c1[k] = c

    def pair(self, k):
        g = self.g
        self.c1[k].wait_recv()
        mm = (g.m + k) % 4
        return self.src[g.a, mm].astype(F32) + self.r1[mm].astype(F32)

    def square(self, k):
        g = self.g
        dev = g.xy(k)[1]
        self.s2[k - 1] = self.pair(k).astype(BF)
        c = rcopy(self.s2.at[k - 1], self.r2.at[k - 1], self.sem.at[2, k - 1], self.sem.at[3, k - 1], dev)
        c.start()
        self.c2.append(c)

    def line(self):
        g = self.g
        acc = self.pair(0)
        for k in (1, 2, 3):
            self.c2[k - 1].wait_recv()
            acc = acc + self.r2[k - 1].astype(F32)
        self.s3[...] = acc.astype(BF)
        for k in range(1, g.zs):
            zz, dev = g.zl(k)
            at = zz if g.zs == ZO else jnp.minimum(zz, ZO - 1)
            c = rcopy(self.s3.at[at], self.r3.at[k - 1], self.sem.at[4, k - 1], self.sem.at[5, k - 1], dev)
            g.owned(zz, c.start)
            self.c3.append(c)

    def result(self):
        g = self.g
        out = self.s3[g.zown].astype(F32)
        for k in range(1, g.zs):
            g.owned(g.z, self.c3[k - 1].wait_recv)
            out = out + self.r3[k - 1].astype(F32)
        return out

    def finish(self):
        g = self.g
        for c in self.c1.values():
            c.wait_send()
        for c in self.c2:
            c.wait_send()
        for k in range(1, g.zs):
            g.owned(g.zl(k)[0], self.c3[k - 1].wait_send)


class Gather:
    def __init__(self, g, out, sem):
        self.g, self.out, self.sem = g, out, sem
        self.cz, self.cxy, self.cc = [], {}, []

    @staticmethod
    def scratch(zs):
        return [pltpu.SemaphoreType.DMA((6, 4, max(zs, 4)))]

    def start(self):
        g = self.g
        own = self.out.at[g.a, g.m, g.zown]
        for k in range(1, g.zs):
            c = rcopy(own, own, self.sem.at[0, 0, k], self.sem.at[1, 0, k], g.zl(k)[1])
            g.owned(g.z, c.start)
            self.cz.append(c)
        self.fan(g.z, 0)

    def fan(self, z, k):
        g = self.g
        at = z if g.zs == ZO else jnp.minimum(z, ZO - 1)
        r = self.out.at[g.a, g.m, at]
        for j in (1, 2, 3):
            c = rcopy(r, r, self.sem.at[2, j, k], self.sem.at[3, j, k], g.xy(j)[1])
            g.owned(z, c.start)
            self.cxy[j, k] = (z, c)

    def line(self):
        g = self.g
        for k in range(1, g.zs):
            z = (g.z - k + g.zs) % g.zs
            g.owned(z, self.cz[k - 1].wait_recv)
            self.fan(z, k)

    def to_core(self, mm, i):
        r = self.out.at[self.g.a, mm]
        c = rcopy(r, r, self.sem.at[4, 0, i], self.sem.at[5, 0, i], self.g.core)
        c.start()
        self.cc.append(c)

    def square(self):
        g = self.g
        self.to_core(g.m, 0)
        for j in (1, 2, 3):
            for k in range(g.zs):
                z, c = self.cxy[j, k]
                g.owned(z, c.wait_recv)
            self.to_core((g.m - j + 4) % 4, j)

    def done(self):
        for c in self.cc:
            c.wait_recv()

    def finish(self):
        g = self.g
        for c in self.cz:
            g.owned(g.z, c.wait_send)
        for z, c in self.cxy.values():
            g.owned(z, c.wait_send)
        for c in self.cc:
            c.wait_send()


class Items:
    def __init__(self, surface, volume, bounds, rows):
        at = jnp.int32(0)
        self.starts, self.ends, self.surfs = [], [], []
        self.rows, self.bounds = rows, bounds
        for b in range(ITEMS):
            s = surface[0, b]
            self.starts.append(at)
            self.surfs.append(at + s)
            at = at + s + volume[0, b]
            self.ends.append(at)
            bounds[0, b] = self.starts[b]
            bounds[1, b] = self.ends[b]
            bounds[2, b] = jnp.minimum(lax.div(self.starts[b], jnp.int32(128)), rows // 128 - 2)

    def window(self, b):
        base = self.bounds[2, b]
        pos = iota((1, W), 1) + base * 128
        mask = (pos >= self.bounds[0, b]) & (pos < self.bounds[1, b])
        return base, mask.astype(F32).astype(BF)

    def surface(self):
        pos = iota((1, self.rows), 1)
        out = jnp.zeros((1, self.rows), F32)
        for b in range(ITEMS):
            out = out + ((pos >= self.starts[b]) & (pos < self.surfs[b])).astype(F32)
        return out

    def combine(self, t, buffers):
        first = jnp.int32(0)
        for b in range(ITEMS):
            first = first + (self.ends[b] <= t * 128).astype(jnp.int32)
        pos = iota((1, 128), 1) + t * 128
        outs = [None for _ in buffers]
        for k in range(5):
            b = jnp.minimum(first + k, ITEMS - 1)
            half = jnp.clip(t - self.bounds[2, b], 0, 1)
            low = jnp.where(first + k < ITEMS, self.bounds[0, b], self.rows)
            mask = ((pos >= low) & (pos < self.bounds[1, b])).astype(F32).astype(BF)
            for i, buf in enumerate(buffers):
                part = buf[2 * b + half] * mask
                outs[i] = part if outs[i] is None else outs[i] + part
        return outs


def pair(ref, base, rows):
    return jnp.concatenate([ref[base, rows, :], ref[base + 1, rows, :]], axis=1)


def put_pair(ref, i, rows, value):
    ref[2 * i, rows, :] = value[:, 0:128]
    ref[2 * i + 1, rows, :] = value[:, 128:256]


def column(row):
    return jnp.broadcast_to(row, (128, row.shape[1])).T


def wide(col):
    return jnp.concatenate([col, col], axis=1)


def norm_stats(v):
    mean = jnp.mean(v, axis=0, keepdims=True)
    centred = v - mean
    var = jnp.mean(centred * centred, axis=0, keepdims=True)
    scale = lax.rsqrt(var + NORM_EPS)
    return centred * scale, scale


def halves():
    lane = iota((1, 128), 1)
    return (lane < G).astype(F32).astype(BF), (lane >= G).astype(F32).astype(BF)


def spread_chunk(chunk):
    low, high = halves()
    zero = jnp.zeros((DH, 128), BF)
    one, two = chunk[0:DH], chunk[DH : 2 * DH]
    return jnp.concatenate(
        [
            jnp.concatenate([one * low, zero], axis=1),
            jnp.concatenate([one * high, zero], axis=1),
            jnp.concatenate([zero, two * low], axis=1),
            jnp.concatenate([zero, two * high], axis=1),
        ],
        axis=0,
    )


def take_chunk(full):
    low = iota((DH, 128), 1) < G
    one = jnp.where(low, full[0:DH, 0:128], full[DH : 2 * DH, 0:128])
    two = jnp.where(low, full[2 * DH : 3 * DH, 128:256], full[3 * DH : 4 * DH, 128:256])
    return one, two


def item_sums(probs, fields, mask):
    left = fields * mask
    left = jnp.concatenate([left, jnp.broadcast_to(mask, (16, W))], axis=0)
    full = nt(left, probs)
    one, two = take_chunk(full)
    return jnp.concatenate([one, two, full[128:136, 0:128], full[136:144, 128:256]], axis=0)


def slice_columns(small):
    low = small[:, 0:128].astype(BF)
    pick = (iota((H * G, 128), 0) % G == iota((H * G, 128), 1)).astype(F32).astype(BF)
    rows = nt(pick, low).astype(BF)
    place = (iota((DH, C), 1) % DH == iota((DH, C), 0)).astype(F32).astype(BF)
    full = nn(rows, place)
    keep = iota((H * G, C), 0) // G == iota((H * G, C), 1) // DH
    return jnp.where(keep, full, 0.0).astype(BF)


def same_head():
    return iota((4 * G, 4 * G), 0) // G == iota((4 * G, 4 * G), 1) // G


def first_kernel(
    zs, surface, volume, points, attn_w, mlp_w, small, vector,
    xt, normed, mid, probs, slice_out, saved, attention, wat, wml,
    bounds, surf, src, wxf, slicew, weight_sem, *sems,
):
    g = Place(zs)
    rows = points.shape[0]
    reduce = Reduce(g, src, sems[0:6])
    gather = Gather(g, slice_out, sems[6])
    own = pl.ds(pl.multiple_of(g.f * 64, 64), 64)
    other = pl.ds(pl.multiple_of(((1 - g.x) * 2 + g.a) * 64, 64), 64)
    wat[:, own, :] = attn_w[...].astype(BF)
    wml[:, own, :] = mlp_w[...].astype(BF)
    g.barrier()

    def weight(ref, at, i, dev):
        r = ref.at[:, at, :]
        return rcopy(r, r, weight_sem.at[0, i], weight_sem.at[1, i], dev)

    a_x, a_c = weight(wat, own, 0, g.xpeer), weight(wat, own, 1, g.core)
    m_x, m_c = weight(wml, own, 2, g.xpeer), weight(wml, own, 3, g.core)
    a_f, m_f = weight(wat, other, 4, g.core), weight(wml, other, 5, g.core)
    for c in (a_x, a_c, m_x, m_c):
        c.start()

    items = Items(surface, volume, bounds, rows)
    surf[...] = items.surface()
    gain = wide(column(vector[0:1, :]))
    embed = wide(column(vector[2:3, :]))

    def norm_tile(i, carry):
        at = tile_of(i)
        field = points[at, :].astype(F32).T
        xt[:, at] = field.astype(BF)
        unit, _ = norm_stats(field + embed * surf[:, at])
        normed[:, at] = (unit * gain).astype(BF)
        return carry

    lax.fori_loop(0, rows // W, norm_tile, 0)
    slicew[...] = slice_columns(small)
    a_x.wait_recv()
    a_f.start()
    a_c.wait_recv()
    a_f.wait_recv()
    wxf[0:C, :] = wat[0].astype(F32).T.astype(BF)
    wxf[C : 2 * C, :] = wat[1].astype(F32).T.astype(BF)

    def soft_tile(i, carry):
        at = tile_of(i)
        both = nn(wxf[...], normed[:, at]).astype(BF)
        put_pair(mid, i, slice(None), both)
        logits = nn(slicew[...], both[0:C]).reshape(H, G, W)
        top = jnp.max(logits, axis=1, keepdims=True)
        e = jnp.exp(logits - top)
        total = jnp.sum(e, axis=1, keepdims=True)
        put_pair(probs, i, slice(None), (e * (1.0 / total)).reshape(H * G, W).astype(BF))
        return carry

    lax.fori_loop(0, rows // W, soft_tile, 0)
    m_x.wait_recv()
    m_f.start()

    def item(half, mm, j):
        b = half * 8 + mm * 2 + j
        base, mask = items.window(b)
        for q in range(2):
            fields = pair(mid, base, slice(C + q * 128, C + q * 128 + 128))
            part = item_sums(pair(probs, base, slice(q * 256, q * 256 + 256)), fields, mask)
            src[half, mm, 2 * j + q] = part.astype(BF)

    for k in (1, 2, 3, 0):
        mm = (g.m + k) % 4
        for j in range(2):
            item(1 - g.a, mm, j)
        reduce.core(k)
    for k in (1, 2, 3, 0):
        mm = (g.m + k) % 4
        for j in range(2):
            item(g.a, mm, j)
        if k:
            reduce.square(k)
    reduce.line()
    chunk = reduce.result()

    sums = jnp.concatenate([chunk[0:DH], chunk[DH : 2 * DH]], axis=1)
    scale = jnp.concatenate([chunk[64:72], chunk[72:80]], axis=1) + SLICE_EPS
    token = sums / scale[0:1]
    maps = small[...]
    qkv = tn(maps, token, HIGH)
    query, key, value = qkv[64:96], qkv[96:128], qkv[128:160]
    scores = tn(key, query, HIGH) / math.sqrt(DH)
    scores = jnp.where(same_head(), scores, -jnp.inf)
    top = jnp.max(scores, axis=0, keepdims=True)
    e = jnp.exp(scores - top)
    weights = e / jnp.sum(e, axis=0, keepdims=True)
    out = nn(value, weights, HIGH)
    slice_out[g.a, g.m, g.zown] = jnp.concatenate([out[:, 0:128], out[:, 128:256]], axis=0).astype(BF)
    gather.start()
    saved[0:32] = token
    saved[32:128] = qkv[64:160]
    saved[128:160] = sums
    saved[160:168] = scale
    attention[...] = weights
    gather.line()
    gather.square()
    m_c.wait_recv()
    m_f.wait_recv()
    for c in (a_x, a_c, m_x, m_c, a_f, m_f):
        c.wait_send()
    gather.done()
    gather.finish()
    reduce.finish()


def second_kernel(
    zs, surface, volume, xt, probs, slice_out, saved, attention, wat, wml, small, vector, cotangent,
    mixed, d_mid, d_spread, d_slice, big, squares, small_part,
    bounds, surf, windows, spread, norm_two, active, d_hidden, cot_t, d_branch, wot, wint, woutt, gain_acc,
    src, src_big, red_big, big_sem, *sems,
):
    g = Place(zs)
    rows = cotangent.shape[0]
    reduce = Reduce(g, src, sems[0:6])
    reduce_big = Reduce(g, src_big, sems[6:12])
    gather = Gather(g, d_slice, sems[12])
    items = Items(surface, volume, bounds, rows)
    surf[...] = items.surface()
    gain = wide(column(vector[1:2, :]))
    embed = wide(column(vector[2:3, :]))
    g.barrier()

    def turned(v):
        return v.astype(F32).T.astype(BF)

    wot[...] = turned(wat[2])
    for j in range(FF // 256):
        wint[j * 256 : j * 256 + 256, :] = turned(wml[0, :, j * 256 : j * 256 + 256])
        woutt[j * 256 : j * 256 + 256, :] = turned(wml[1, :, j * 256 : j * 256 + 256])
    gain_acc[...] = jnp.zeros_like(gain_acc)

    def spread_item(b, carry):
        base, _ = items.window(b)
        for q in range(2):
            part = nn(spread_chunk(slice_out[2 * b + q]), pair(probs, base, slice(q * 256, q * 256 + 256))).astype(BF)
            windows[2 * b, q * 128 : q * 128 + 128, :] = part[:, 0:128]
            windows[2 * b + 1, q * 128 : q * 128 + 128, :] = part[:, 128:256]
        return carry

    lax.fori_loop(0, ITEMS, spread_item, 0)

    def mlp_tile(i, carry):
        at = tile_of(i)
        parts = [items.combine(2 * i + j, [windows])[0] for j in range(2)]
        sp = jnp.concatenate(parts, axis=1)
        spread[:, at] = sp
        middle = xt[:, at].astype(F32) + embed * surf[:, at] + nn(wot[...], sp)
        unit, scale = norm_stats(middle)
        two = (unit * gain).astype(BF)
        norm_two[:, at] = two
        ct = cotangent[at, :].astype(F32).T
        ctb = ct.astype(BF)
        cot_t[:, at] = ctb
        out = middle
        d_two = jnp.zeros((C, W), F32)
        for j in range(FF // 256):
            hid = pl.ds(j * 256, 256)
            x = nn(wint[hid, :], two)
            da = nn(woutt[hid, :], ctb)
            sq = x * x
            t = jnp.tanh(x * (GELU_A + GELU_B * sq))
            s = 0.5 + 0.5 * t
            act = (x * s).astype(BF)
            slope = s + (x * (s - s * s)) * (2.0 * GELU_A + 6.0 * GELU_B * sq)
            dh = (slope * da).astype(BF)
            active[hid, at] = act
            d_hidden[hid, at] = dh
            out = out + nn(wml[1, :, hid], act)
            d_two = d_two + nn(wml[0, :, hid], dh)
        mixed[at, :] = out.T.astype(BF)
        gs = d_two * unit
        gain_acc[...] += gs[:, 0:128] + gs[:, 128:256]
        du = d_two * gain
        m1 = jnp.mean(du, axis=0, keepdims=True)
        m2 = jnp.mean(du * unit, axis=0, keepdims=True)
        dm = ct + scale * (du - m1 - unit * m2)
        d_mid[:, at] = dm
        db = dm.astype(BF)
        d_branch[:, at] = db
        put_pair(d_spread, i, slice(None), nn(wat[2], db).astype(BF))
        return carry

    lax.fori_loop(0, rows // W, mlp_tile, 0)

    def item(half, mm, j):
        b = half * 8 + mm * 2 + j
        base, mask = items.window(b)
        for q in range(2):
            fields = pair(d_spread, base, slice(q * 128, q * 128 + 128))
            part = item_sums(pair(probs, base, slice(q * 256, q * 256 + 256)), fields, mask)
            src[half, mm, 2 * j + q] = part.astype(BF)

    for k in (1, 2, 3, 0):
        mm = (g.m + k) % 4
        for j in range(2):
            item(1 - g.a, mm, j)
        reduce.core(k)
    for k in (1, 2, 3, 0):
        mm = (g.m + k) % 4
        for j in range(2):
            item(g.a, mm, j)
        if k:
            reduce.square(k)

    def put(f, p, lo, value):
        src_big[f % 2, (f // 2) * 2 + p % 2, p // 2, lo : lo + value.shape[0], :] = value

    for which, (left, right) in enumerate(((norm_two, d_hidden), (cot_t, active))):
        for j in range(FF // 256):
            grad = nt(left[...], right[j * 256 : j * 256 + 256, :]).astype(BF)
            for f in range(4):
                for i in range(2):
                    put(f, 2 * j + i, which * 64, grad[f * 64 : f * 64 + 64, i * 128 : i * 128 + 128])
    grad = nt(spread[...], d_branch[...]).astype(BF)
    for f in range(4):
        for p in range(8):
            lo = f * 64 + (p % 4) * 16
            put(f, p, 128, grad[lo : lo + 16, (p // 4) * 128 : (p // 4) * 128 + 128])
    for k in (1, 2, 3, 0):
        reduce_big.core(k)

    reduce.line()
    chunk = reduce.result()
    d_out = jnp.concatenate([chunk[0:DH], chunk[DH : 2 * DH]], axis=1)
    token, query, key, value = saved[0:32], saved[32:64], saved[64:96], saved[96:128]
    sums, scale = saved[128:160], saved[160:161]
    weights = attention[...]
    d_value = nt(d_out, weights, HIGH)
    d_weights = tn(value, d_out, HIGH)
    d_scores = weights * (d_weights - jnp.sum(weights * d_weights, axis=0, keepdims=True))
    d_query = nn(key, d_scores, HIGH) / math.sqrt(DH)
    d_key = nt(query, d_scores, HIGH) / math.sqrt(DH)
    d_maps = jnp.concatenate([jnp.zeros((64, 256), F32), d_query, d_key, d_value], axis=0)
    d_token = nn(small[...], d_maps, HIGH)
    d_total = -jnp.sum(d_token * sums, axis=0, keepdims=True) / (scale * scale)
    d_sum = d_token / scale
    tot = jnp.broadcast_to(d_total, (8, 256))
    d_slice[g.a, g.m, g.zown] = jnp.concatenate(
        [d_sum[:, 0:128], d_sum[:, 128:256], tot[:, 0:128], tot[:, 128:256]], axis=0
    ).astype(BF)
    gather.start()
    grad_maps = nt(token, jnp.concatenate([d_maps, jnp.zeros((96, 256), F32)], axis=0), HIGH)
    if zs != ZO:
        grad_maps = jnp.where(g.z < ZO, grad_maps, 0.0)
    small_part[0:32, :] = grad_maps
    small_part[32:40, :] = nt(jnp.ones((8, 128), F32), gain_acc[...], HIGH)
    for k in (1, 2, 3):
        reduce_big.square(k)
    gather.line()
    gather.square()
    reduce_big.line()
    whole = reduce_big.result().astype(BF)
    red_big[...] = whole
    mine = whole.astype(F32)
    sq = jnp.sum((mine * mine).reshape(CB // 8, 8, 128), axis=0)
    squares[...] = sq if zs == ZO else jnp.where(g.z < ZO, sq, 0.0)
    big[g.zown, g.y] = whole
    part = big.at[g.zown, g.y]
    cz = []
    for k in range(1, zs):
        c = rcopy(part, part, big_sem.at[0, k], big_sem.at[1, k], g.zl(k)[1])
        g.owned(g.z, c.start)
        cz.append(c)
    cy = []

    def to_y(z, k):
        at = z if zs == ZO else jnp.minimum(z, ZO - 1)
        r = big.at[at, g.y]
        c = rcopy(r, r, big_sem.at[2, k], big_sem.at[3, k], g.ypeer)
        g.owned(z, c.start)
        cy.append((z, c))

    to_y(g.z, 0)
    for k in range(1, zs):
        z = (g.z - k + zs) % zs
        g.owned(z, cz[k - 1].wait_recv)
        to_y(z, k)
    gather.done()
    for z, c in cy:
        g.owned(z, c.wait_recv)
    gather.finish()
    reduce.finish()
    reduce_big.finish()
    for c in cz:
        g.owned(g.z, c.wait_send)
    for z, c in cy:
        g.owned(z, c.wait_send)


def adamw(state, new, sl, grad, factor, rate):
    weight, first, second, average = [r[sl] for r in state]
    clipped = grad * factor
    first_new = BETA_ONE * first + (1.0 - BETA_ONE) * clipped
    second_new = BETA_TWO * second + (1.0 - BETA_TWO) * clipped * clipped
    first_hat = first_new / (1.0 - BETA_ONE**STEP)
    second_hat = second_new / (1.0 - BETA_TWO**STEP)
    new_weight = weight - rate * (first_hat / (jnp.sqrt(second_hat) + ADAM_EPS) + DECAY * weight)
    average_new = EMA_RATE * average + (1.0 - EMA_RATE) * new_weight
    for r, v in zip(new, (new_weight, first_new, second_new, average_new, new_weight.astype(BF))):
        r[sl] = v


def third_kernel(zs, surface, volume, *refs):
    (xt, normed, mid, probs, slice_out, d_slice, d_mid, d_spread, wat, small_all, vector_all,
     big, squares, small_part) = refs[0:14]
    attn, mlp, small_s, vector_s = [refs[14 + 4 * i : 18 + 4 * i] for i in range(4)]
    points_grad, norm_out = refs[30:32]
    attn_new, mlp_new, small_new, vector_new = [refs[32 + 5 * i : 37 + 5 * i] for i in range(4)]
    (bounds, surf, windows_x, windows_f, d_both, slicet, slice_acc, gain_acc, embed_acc, src, late,
     small_src, small_sum, sr1, sr2, sr3, sqa, sqb, sem) = refs[52:71]
    sems = refs[71:]
    g = Place(zs)
    rows = xt.shape[1]
    reduce = Reduce(g, src, sems[0:6])
    items = Items(surface, volume, bounds, rows)
    surf[...] = items.surface()
    gain = wide(column(vector_all[0:1, :]))
    embed = wide(column(vector_all[2:3, :]))
    g.barrier(crossed=True)
    for r in (slice_acc, gain_acc, embed_acc):
        r[...] = jnp.zeros_like(r)
    slicet[...] = slice_columns(small_all).astype(F32).T.astype(BF)
    first_row = (iota((16, W), 0) == 0).astype(F32).astype(BF)

    def item(b, carry):
        base, mask = items.window(b)
        for q in range(2):
            four = slice(q * 128, q * 128 + 128)
            eight = slice(q * 256, q * 256 + 256)
            d_chunk = d_slice[2 * b + q]
            maps = spread_chunk(d_chunk[0:64])
            both = jnp.concatenate([spread_chunk(slice_out[2 * b + q]), maps], axis=0)
            fields = jnp.concatenate(
                [pair(d_spread, base, four), pair(mid, base, slice(C + q * 128, C + q * 128 + 128))], axis=0
            )
            tot = jnp.concatenate([d_chunk[64:72], d_chunk[72:80]], axis=1)
            tot = jnp.concatenate([tot, tot], axis=0)
            pb = pair(probs, base, eight)
            dp = (tn(both, fields) + tn(tot, first_row)).reshape(4, G, W)
            pf = pb.astype(F32).reshape(4, G, W)
            back = pf * (dp - jnp.sum(pf * dp, axis=1, keepdims=True))
            dl = back.reshape(4 * G, W).astype(BF) * mask
            dx = nn(slicet[four, eight], dl).astype(BF)
            df = nn(maps, pb).astype(BF)
            for half in range(2):
                windows_x[2 * b + half, four, :] = dx[:, half * 128 : half * 128 + 128]
                windows_f[2 * b + half, four, :] = df[:, half * 128 : half * 128 + 128]
            one, two = take_chunk(nt(pair(mid, base, four), dl))
            slice_acc[...] += one + two
        return carry

    lax.fori_loop(0, ITEMS, item, 0)

    def back_tile(i, carry):
        at = tile_of(i)
        parts = [items.combine(2 * i + j, [windows_x, windows_f]) for j in range(2)]
        dx = jnp.concatenate([parts[0][0], parts[1][0]], axis=1)
        df = jnp.concatenate([parts[0][1], parts[1][1]], axis=1)
        d_both[0:C, at] = dx
        d_both[C : 2 * C, at] = df
        d_norm = nn(wat[0], dx) + nn(wat[1], df)
        sf = surf[:, at]
        unit, scale = norm_stats(xt[:, at].astype(F32) + embed * sf)
        gs = d_norm * unit
        gain_acc[...] += gs[:, 0:128] + gs[:, 128:256]
        du = d_norm * gain
        m1 = jnp.mean(du, axis=0, keepdims=True)
        m2 = jnp.mean(du * unit, axis=0, keepdims=True)
        pg = d_mid[:, at] + scale * (du - m1 - unit * m2)
        es = pg * sf
        embed_acc[...] += es[:, 0:128] + es[:, 128:256]
        points_grad[at, :] = pg.T
        return carry

    lax.fori_loop(0, rows // W, back_tile, 0)

    grads = [nt(normed[...], d_both[i * C : i * C + C, :]).astype(BF) for i in range(2)]
    for f in range(4):
        for p in range(8):
            lo, col = f * 64 + (p % 4) * 16, (p // 4) * 128
            both = [v[lo : lo + 16, col : col + 128] for v in grads]
            src[f % 2, (f // 2) * 2 + p % 2, p // 2] = jnp.concatenate(both, axis=0)
    for k in (1, 2, 3, 0):
        reduce.core(k)

    ones = jnp.ones((8, 128), F32)
    rows_one = nt(ones, gain_acc[...], HIGH)
    rows_emb = nt(ones, embed_acc[...], HIGH)
    rows_two = small_part[32:40, :]
    fold = slice_acc[...]
    fold = jnp.where(iota((32, 128), 1) < G, fold + pltpu.roll(fold, G, 1), 0.0)
    pick = iota((8, 256), 0)
    vec = jnp.where(pick == 0, rows_one, jnp.where(pick == 1, rows_two, jnp.where(pick == 2, rows_emb, 0.0)))
    small_src[0:32] = (fold + small_part[0:32, 0:128]).astype(BF)
    small_src[32:64] = small_part[0:32, 128:256].astype(BF)
    small_src[64:80] = jnp.concatenate([vec[:, 0:128], vec[:, 128:256]], axis=0).astype(BF)
    cs = []
    c = rcopy(small_src, sr1, sem.at[0, 0], sem.at[1, 0], g.core)
    c.start()
    cs.append(c)
    for k in (1, 2, 3):
        reduce.square(k)
    c.wait_recv()
    sr2[g.m] = (small_src[...].astype(F32) + sr1[...].astype(F32)).astype(BF)
    for k in (1, 2, 3):
        c = rcopy(sr2.at[g.m], sr2.at[g.m], sem.at[0, k], sem.at[1, k], g.xy(k)[1])
        c.start()
        cs.append(c)
    reduce.line()
    for c in cs[1:4]:
        c.wait_recv()
    total = sr2[0].astype(F32)
    for m in range(1, 4):
        total = total + sr2[m].astype(F32)
    sr3[g.z] = total.astype(BF)
    for k in range(1, zs):
        c = rcopy(sr3.at[g.z], sr3.at[g.z], sem.at[2, k], sem.at[3, k], g.zl(k)[1])
        c.start()
        cs.append(c)

    whole = reduce.result().astype(BF)
    late[g.zown, g.y] = whole
    mine = whole.astype(F32)
    sq = jnp.sum((mine * mine).reshape(CL // 8, 8, 128), axis=0)
    if zs != ZO:
        sq = jnp.where(g.z < ZO, sq, 0.0)
    sqa[g.z] = sq + squares[...]
    part = late.at[g.zown, g.y]
    cz = []
    for k in range(1, zs):
        c = rcopy(part, part, sem.at[4, k], sem.at[5, k], g.zl(k)[1])
        g.owned(g.z, c.start)
        cz.append(c)
        c = rcopy(sqa.at[g.z], sqa.at[g.z], sem.at[6, k], sem.at[7, k], g.zl(k)[1])
        c.start()
        cs.append(c)
    cy = []

    def to_y(z, k):
        at = z if zs == ZO else jnp.minimum(z, ZO - 1)
        r = late.at[at, g.y]
        c = rcopy(r, r, sem.at[8, k], sem.at[9, k], g.ypeer)
        g.owned(z, c.start)
        cy.append((z, c))

    to_y(g.z, 0)
    for k in range(1, zs):
        cs[4 + zs - 2 + k].wait_recv()
    sq = sqa[0]
    for z in range(1, zs):
        sq = sq + sqa[z]
    here = g.a * 4 + g.m
    sqb[here] = sq
    for k in range(1, 8):
        dev = (g.core if k == 4 else g.xy(k)[1] if k < 4 else g.xy_other(k - 4)[1])
        c = rcopy(sqb.at[here], sqb.at[here], sem.at[10, k], sem.at[11, k], dev)
        c.start()
        cs.append(c)
    for k in range(1, zs):
        z = (g.z - k + zs) % zs
        g.owned(z, cz[k - 1].wait_recv)
        to_y(z, k)

    for k in range(1, zs):
        cs[3 + k].wait_recv()
    total = sr3[0].astype(F32)
    for z in range(1, zs):
        total = total + sr3[z].astype(F32)
    small_sum[...] = total
    for c in cs[-7:]:
        c.wait_recv()
    sq = sqb[0]
    for i in range(1, 8):
        sq = sq + sqb[i]
    norm = jnp.sqrt(jnp.sum(sq) + jnp.sum(total * total))
    norm_out[0, 0] = norm
    factor = jnp.minimum(1.0, CLIP / norm)
    everything = slice(None)
    gsmall = jnp.concatenate([total[0:32], total[32:64]], axis=1)[:, 0:160]
    adamw(small_s, small_new, (everything, everything), gsmall, factor, RATE_SMALL)
    gvec = jnp.concatenate([total[64:72], total[72:80]], axis=1)[0:3, :]
    adamw(vector_s, vector_new, (everything, everything), gvec, factor, RATE_VECTOR)
    for z in range(ZO):
        for y in range(2):
            p = z * 2 + y
            for i in range(2):
                grad = big[z, y, i * 64 : i * 64 + 64, :].astype(F32)
                adamw(mlp, mlp_new, (i, everything, slice(p * 128, p * 128 + 128)), grad, factor, RATE_MLP)
            lo, col = (p % 4) * 16, (p // 4) * 128
            grad = big[z, y, 128:144, :].astype(F32)
            adamw(attn, attn_new, (2, slice(lo, lo + 16), slice(col, col + 128)), grad, factor, RATE_ATTN)
    for z, c in cy:
        g.owned(z, c.wait_recv)
    for z in range(ZO):
        for y in range(2):
            p = z * 2 + y
            lo, col = (p % 4) * 16, (p // 4) * 128
            for i in range(2):
                grad = late[z, y, i * 16 : i * 16 + 16, :].astype(F32)
                adamw(attn, attn_new, (i, slice(lo, lo + 16), slice(col, col + 128)), grad, factor, RATE_ATTN)
    for c in cs:
        c.wait_send()
    for c in cz:
        g.owned(g.z, c.wait_send)
    for z, c in cy:
        g.owned(z, c.wait_send)
    reduce.finish()


def body(zs, points, cotangent, surface_count, volume_count, *state):
    attn, mlp, small, vector = [state[4 * i : 4 * i + 4] for i in range(4)]
    rows = points.shape[0]
    vmem = pl.BlockSpec(memory_space=pltpu.VMEM)
    smem = pl.BlockSpec(memory_space=pltpu.SMEM)
    sd = jax.ShapeDtypeStruct
    tall = pltpu.VMEM((C, rows), BF)

    def params(cid):
        return pltpu.CompilerParams(collective_id=cid, has_side_effects=True, vmem_limit_bytes=60 << 20)

    def tiles(features):
        return sd((rows // 128, features, 128), BF)

    chunks = sd((2, 4, ZO, 2 * DH, 128), BF)
    firsts = pl.pallas_call(
        functools.partial(first_kernel, zs),
        out_shape=[
            sd((C, rows), BF), sd((C, rows), BF), tiles(2 * C), tiles(H * G), chunks,
            sd((168, 256), F32), sd((256, 256), F32), sd((3, C, C), BF), sd((2, C, FF), BF),
        ],
        in_specs=[smem, smem] + [vmem] * 5,
        out_specs=[vmem] * 9,
        scratch_shapes=[
            pltpu.SMEM((3, ITEMS), jnp.int32), pltpu.VMEM((1, rows), F32), pltpu.VMEM((2, 4, ZO, CH, 128), BF),
            pltpu.VMEM((2 * C, C), BF), pltpu.VMEM((H * G, C), BF), pltpu.SemaphoreType.DMA((2, 6)),
        ] + Reduce.scratch(CH, zs) + Gather.scratch(zs),
        compiler_params=params(0),
        name="first",
    )(surface_count, volume_count, points, attn[0], mlp[0], small[0], vector[0])
    xt, normed, mid, probs, slice_out, saved, attention, wat, wml = firsts
    flat_out = slice_out.reshape(2 * ITEMS, 2 * DH, 128)

    seconds = pl.pallas_call(
        functools.partial(second_kernel, zs),
        out_shape=[
            sd((rows, C), BF), sd((C, rows), F32), tiles(C), sd((2, 4, ZO, CH, 128), BF),
            sd((ZO, 2, CB, 128), BF), sd((8, 128), F32), sd((40, 256), F32),
        ],
        in_specs=[smem, smem] + [vmem] * 10,
        out_specs=[vmem] * 7,
        scratch_shapes=[
            pltpu.SMEM((3, ITEMS), jnp.int32), pltpu.VMEM((1, rows), F32), pltpu.VMEM((2 * ITEMS, C, 128), BF),
            tall, tall, pltpu.VMEM((FF, rows), BF), pltpu.VMEM((FF, rows), BF), tall, tall,
            pltpu.VMEM((C, C), BF), pltpu.VMEM((FF, C), BF), pltpu.VMEM((FF, C), BF), pltpu.VMEM((C, 128), F32),
            pltpu.VMEM((2, 4, ZO, CH, 128), BF), pltpu.VMEM((2, 4, ZO, CB, 128), BF), pltpu.VMEM((CB, 128), BF),
            pltpu.SemaphoreType.DMA((4, max(zs, 4))),
        ] + Reduce.scratch(CH, zs) + Reduce.scratch(CB, zs) + Gather.scratch(zs),
        compiler_params=params(1),
        name="second",
    )(surface_count, volume_count, xt, probs, flat_out, saved, attention, wat, wml, small[0], vector[0], cotangent)
    mixed, d_mid, d_spread, d_slice, big, squares, small_part = seconds
    flat_d = d_slice.reshape(2 * ITEMS, CH, 128)

    def news(leaves):
        return [sd(leaves[0].shape, F32)] * 4 + [sd(leaves[0].shape, BF)]

    thirds = pl.pallas_call(
        functools.partial(third_kernel, zs),
        out_shape=[sd((rows, C), F32), sd((1, 1), F32)] + news(attn) + news(mlp) + news(small) + news(vector),
        in_specs=[smem, smem] + [vmem] * 30,
        out_specs=[vmem, smem] + [vmem] * 20,
        scratch_shapes=[
            pltpu.SMEM((3, ITEMS), jnp.int32), pltpu.VMEM((1, rows), F32), pltpu.VMEM((2 * ITEMS, C, 128), BF),
            pltpu.VMEM((2 * ITEMS, C, 128), BF), pltpu.VMEM((2 * C, rows), BF), pltpu.VMEM((C, H * G), BF),
            pltpu.VMEM((32, 128), F32), pltpu.VMEM((C, 128), F32), pltpu.VMEM((C, 128), F32),
            pltpu.VMEM((2, 4, ZO, CL, 128), BF), pltpu.VMEM((ZO, 2, CL, 128), BF),
            pltpu.VMEM((SM, 128), BF), pltpu.VMEM((SM, 128), F32), pltpu.VMEM((SM, 128), BF),
            pltpu.VMEM((4, SM, 128), BF), pltpu.VMEM((zs, SM, 128), BF),
            pltpu.VMEM((zs, 8, 128), F32), pltpu.VMEM((8, 8, 128), F32),
            pltpu.SemaphoreType.DMA((12, max(zs, 8))),
        ] + Reduce.scratch(CL, zs),
        compiler_params=params(2),
        name="third",
    )(surface_count, volume_count, xt, normed, mid, probs, flat_out, flat_d, d_mid, d_spread, wat, small[0], vector[0],
      big, squares, small_part, *attn, *mlp, *small, *vector)
    points_grad, norm = thirds[0:2]
    return (mixed, points_grad, norm.reshape(())) + tuple(thirds[2:])


def solution(mesh):
    rows = P(("pts", "fsdp"), None)
    split = P(None, "fsdp", None)
    in_specs = (rows,) * 4 + (split,) * 8 + (P(),) * 8
    out_specs = (rows, rows, P()) + (split,) * 10 + (P(),) * 10
    return jax.shard_map(
        functools.partial(body, mesh.shape["pts"] // 2),
        mesh=mesh, in_specs=in_specs, out_specs=out_specs, check_vma=False,
    )
```

time: 730 us -> 175 us (0.24)
  matrix products: 212 us -> 0 us
  blocking collectives: 210 us -> 0 us
  waiting for transfers between devices: 185 us -> 0 us
  Pallas kernels: 0 us -> 155 us
  other arithmetic: 59.5 us -> 0 us
  between operations: 21.7 us -> 2.68 us
  local copies, waits for them, and re-layouts: 33.4 us -> 16.6 us
    dot_general x38 -> x0, matrix products: 207 us -> none  [the longest x1 25.6 us: body(): jnp.einsum('nhd,bhgd->nbhg', features, d_sum, preferred_element_type=jnp....]
    psum x4 -> x0, blocking collectives: 202 us -> none  [the longest x1 116 us: body(): summed_attn, summed_mlp = lax.psum((grad_attn, grad_mlp), 'pts')]
    psum x2 -> x0, waiting for transfers between devices: 185 us -> none  [the longest x1 117 us: body(): d_slice_out = lax.psum(part_back, ('pts', 'fsdp'))]
    pallas_call x0 -> x3, Pallas kernels: none -> 155 us  [the longest x1 66.3 us: body(): pl.pallas_call(functools.partial(second_kernel, zs), out_shape=[sd((rows,...]
    reduce_sum x13 -> x0, other arithmetic: 31.1 us -> none  [the longest x1 20.5 us: body(): part_totals = jnp.sum(masked, axis=0, dtype=jnp.float32)]
    convert_element_type x4 -> x0, local copies, waits for them, and re-layouts: 13.4 us -> none  [the longest x2 8.66 us: body(): contract_cols(flat_d, weight_slice).reshape(rows, width)]
    convert_element_type x10 -> x0, other arithmetic: 11.4 us -> none  [the longest x4 5.31 us: adamw(): new_weight.astype(jnp.bfloat16)]
    all_gather x1 -> x0, blocking collectives: 7.91 us -> none  [body(): lax.all_gather(attn_weight.astype(jnp.bfloat16), 'fsdp', axis=1, tiled=True)]
  transfers between devices with their start and end apart: 5 -> 0, of which waited for: 2 -> 0; matrix products, arithmetic and copies ran while one was open for 13% -> 0% of each run, Pallas kernels for 0% -> 0%
where the time goes in v1:
time: 175 us
  Pallas kernels  155 us (89%)
  local copies, waits for them, and re-layouts  16.6 us (9%)
  between operations  2.68 us (2%)
    pallas_call x1, Pallas kernels, body(): pl.pallas_call(functools.partial(second_kernel, zs), out_shape=[sd((rows,...  66.3 us
    pallas_call x1, Pallas kernels, body(): pl.pallas_call(functools.partial(third_kernel, zs), out_shape=[sd((rows,...  45.1 us
    pallas_call x1, Pallas kernels, body(): pl.pallas_call(functools.partial(first_kernel, zs), out_shape=[sd((C, row...  43.9 us
    unnamed x66, local copies, waits for them, and re-layouts  16.6 us

profile of v1, /device:TPU:0, one launch (start us, length us, event | category | flops | bytes accessed | tf_op | source)
XLA Modules:
  0.0 174.6 jit_solution(10597778637757676893)
XLA Ops:
  0.7 43.9 %first.1 = (bf16[256,2048]{1,0:T(8,128)(2,1)}, bf16[256,2048]{1,0:T(8,128)(2,1)}, bf16[16,512,128]{2,1,0:T(8,128)(2,1)}, bf16[16,512,128]{2,1,0:T(8,128)(2,1)}, ...) custom-call(s32[1,16]{1,0:T(1,128)} %surface.5, ...), custom_call_target="tpu_custom_call" | custom-call | tf_op jit(solution)/shard_map/first/pallas_call | solution.py:898
  44.6 66.3 %second.1 = (bf16[2048,256]{1,0:T(8,128)(2,1)}, f32[256,2048]{1,0:T(8,128)}, bf16[16,256,128]{2,1,0:T(8,128)(2,1)}, bf16[2,4,4,80,128]{4,3,2,1,0:T(8,128)(2,1)},...) custom-call(s32[1,16]{1,0:T(1,128)} %surface.5, s32[1,16]{1,0:T(1,128)} %volume.5, ...), custom_call_target="tpu_custom_call" | custom-call | tf_op jit(solution)/shard_map/second/pallas_call | solution.py:916
  110.9 0.0 copy-start.1
  110.9 45.1 %third.1 = (f32[2048,256]{1,0:T(8,128)}, f32[1,1]{1,0:T(1,128)}, f32[3,64,256]{2,1,0:T(8,128)}, f32[3,64,256]{2,1,0:T(8,128)}, f32[3,64,256]{2,1,0:T(8,128)}, /*...) custom-call(s32[1,16]{1,0:T(1,128)} %surface.5, ...), custom_call_target="tpu_custom_call" | custom-call | tf_op jit(solution)/shard_map/third/pallas_call | solution.py:940
  156.0 1.0 copy.66
  157.0 1.0 copy-done
  158.0 1.3 copy.67
  160.0 0.7 copy.69
  160.7 0.7 copy.70
  161.4 0.7 copy.71
  162.1 0.7 copy.72
  162.8 0.6 copy.73
  163.4 0.0 copy-done.5
  163.4 0.8 copy.74
  164.2 0.0 copy-done.4
  164.2 0.0 copy-start.12
  164.2 0.0 copy-start.16
  164.2 0.0 copy-start.20
  164.3 0.8 copy.75
  165.1 0.8 copy.76
  165.9 0.8 copy.77
  166.7 0.7 copy.78
  167.4 0.6 copy.79
  168.0 0.6 copy.80
  168.6 0.6 copy.81
  169.2 0.6 copy.82
  169.9 0.6 copy.83
  170.5 0.6 copy.84
  171.1 0.6 copy.85
  171.7 0.6 copy.86
  172.2 0.6 copy.87
  172.8 0.6 copy.88
  (37 shorter events, 0.1 us)
Async XLA Ops:
  110.9 45.1 %copy-start.1 = (bf16[2048,256]{1,0:T(8,128)(2,1)S(1)}, bf16[2048,256]{1,0:T(8,128)(2,1)}, u32[]{:S(2)}) copy-start(bf16[2048,256]{1,0:T(8,128)(2,1)} %get-tuple-element.122) | copy-start | bytes 3145732
  156.0 2.0 %copy-start = (f32[2048,256]{1,0:T(8,128)S(1)}, f32[2048,256]{1,0:T(8,128)}, u32[]{:S(2)}) copy-start(f32[2048,256]{1,0:T(8,128)} %get-tuple-element.123) | copy-start | bytes 6291460
  157.9 2.1 %copy-start.10 = (f32[3,64,256]{2,1,0:T(8,128)S(1)}, f32[3,64,256]{2,1,0:T(8,128)}, u32[]{:S(2)}) copy-start(f32[3,64,256]{2,1,0:T(8,128)} %get-tuple-element.125) | copy-start | bytes 589828
  157.9 2.8 %copy-start.9 = (f32[3,64,256]{2,1,0:T(8,128)S(1)}, f32[3,64,256]{2,1,0:T(8,128)}, u32[]{:S(2)}) copy-start(f32[3,64,256]{2,1,0:T(8,128)} %get-tuple-element.126) | copy-start | bytes 589828
  157.9 3.5 %copy-start.8 = (f32[3,64,256]{2,1,0:T(8,128)S(1)}, f32[3,64,256]{2,1,0:T(8,128)}, u32[]{:S(2)}) copy-start(f32[3,64,256]{2,1,0:T(8,128)} %get-tuple-element.127) | copy-start | bytes 589828
  157.9 4.1 %copy-start.7 = (f32[3,64,256]{2,1,0:T(8,128)S(1)}, f32[3,64,256]{2,1,0:T(8,128)}, u32[]{:S(2)}) copy-start(f32[3,64,256]{2,1,0:T(8,128)} %get-tuple-element.128) | copy-start | bytes 589828
  158.0 4.8 %copy-start.11 = (bf16[3,64,256]{2,1,0:T(8,128)(2,1)S(1)}, bf16[3,64,256]{2,1,0:T(8,128)(2,1)}, u32[]{:S(2)}) copy-start(bf16[3,64,256]{2,1,0:T(8,128)(2,1)} %get-tuple-element.129) | copy-start | bytes 294916
  158.0 5.4 %copy-start.5 = (f32[2,64,1024]{2,1,0:T(8,128)S(1)}, f32[2,64,1024]{2,1,0:T(8,128)}, u32[]{:S(2)}) copy-start(f32[2,64,1024]{2,1,0:T(8,128)} %get-tuple-element.130) | copy-start | bytes 1572868
  159.3 4.9 %copy-start.4 = (f32[2,64,1024]{2,1,0:T(8,128)S(1)}, f32[2,64,1024]{2,1,0:T(8,128)}, u32[]{:S(2)}) copy-start(f32[2,64,1024]{2,1,0:T(8,128)} %get-tuple-element.131) | copy-start | bytes 1572868
  159.3 5.8 %copy-start.3 = (f32[2,64,1024]{2,1,0:T(8,128)S(1)}, f32[2,64,1024]{2,1,0:T(8,128)}, u32[]{:S(2)}) copy-start(f32[2,64,1024]{2,1,0:T(8,128)} %get-tuple-element.132) | copy-start | bytes 1572868
  161.4 4.5 %copy-start.2 = (f32[2,64,1024]{2,1,0:T(8,128)S(1)}, f32[2,64,1024]{2,1,0:T(8,128)}, u32[]{:S(2)}) copy-start(f32[2,64,1024]{2,1,0:T(8,128)} %get-tuple-element.133) | copy-start | bytes 1572868
  163.4 3.3 %copy-start.6 = (bf16[2,64,1024]{2,1,0:T(8,128)(2,1)S(1)}, bf16[2,64,1024]{2,1,0:T(8,128)(2,1)}, u32[]{:S(2)}) copy-start(bf16[2,64,1024]{2,1,0:T(8,128)(2,1)} %get-tuple-element.134) | copy-start | bytes 786436
  164.2 3.2 %copy-start.15 = (f32[32,160]{1,0:T(8,128)S(1)}, f32[32,160]{1,0:T(8,128)}, u32[]{:S(2)}) copy-start(f32[32,160]{1,0:T(8,128)} %get-tuple-element.135) | copy-start | bytes 61444
  164.2 3.8 %copy-start.14 = (f32[32,160]{1,0:T(8,128)S(1)}, f32[32,160]{1,0:T(8,128)}, u32[]{:S(2)}) copy-start(f32[32,160]{1,0:T(8,128)} %get-tuple-element.136) | copy-start | bytes 61444
  164.2 4.4 %copy-start.13 = (f32[32,160]{1,0:T(8,128)S(1)}, f32[32,160]{1,0:T(8,128)}, u32[]{:S(2)}) copy-start(f32[32,160]{1,0:T(8,128)} %get-tuple-element.137) | copy-start | bytes 61444
  164.2 5.0 %copy-start.12 = (f32[32,160]{1,0:T(8,128)S(1)}, f32[32,160]{1,0:T(8,128)}, u32[]{:S(2)}) copy-start(f32[32,160]{1,0:T(8,128)} %get-tuple-element.138) | copy-start | bytes 61444
  164.2 5.6 %copy-start.16 = (bf16[32,160]{1,0:T(8,128)(2,1)S(1)}, bf16[32,160]{1,0:T(8,128)(2,1)}, u32[]{:S(2)}) copy-start(bf16[32,160]{1,0:T(8,128)(2,1)} %get-tuple-element.139) | copy-start | bytes 30724
  164.2 6.2 %copy-start.20 = (f32[3,256]{1,0:T(4,128)S(1)}, f32[3,256]{1,0:T(4,128)}, u32[]{:S(2)}) copy-start(f32[3,256]{1,0:T(4,128)} %get-tuple-element.140) | copy-start | bytes 9220
  164.2 6.8 %copy-start.19 = (f32[3,256]{1,0:T(4,128)S(1)}, f32[3,256]{1,0:T(4,128)}, u32[]{:S(2)}) copy-start(f32[3,256]{1,0:T(4,128)} %get-tuple-element.141) | copy-start | bytes 9220
  164.3 7.4 %copy-start.18 = (f32[3,256]{1,0:T(4,128)S(1)}, f32[3,256]{1,0:T(4,128)}, u32[]{:S(2)}) copy-start(f32[3,256]{1,0:T(4,128)} %get-tuple-element.142) | copy-start | bytes 9220
  164.3 8.0 %copy-start.17 = (f32[3,256]{1,0:T(4,128)S(1)}, f32[3,256]{1,0:T(4,128)}, u32[]{:S(2)}) copy-start(f32[3,256]{1,0:T(4,128)} %get-tuple-element.143) | copy-start | bytes 9220
  164.3 8.6 %copy-start.21 = (bf16[3,256]{1,0:T(4,128)(2,1)S(1)}, bf16[3,256]{1,0:T(4,128)(2,1)}, u32[]{:S(2)}) copy-start(bf16[3,256]{1,0:T(4,128)(2,1)} %get-tuple-element.144) | copy-start | bytes 4612

commit v2 on v1

v2 whole, which is shorter than its diff:
```python
import functools
import math

import jax
import jax.numpy as jnp
from jax import lax
from jax.experimental import pallas as pl
from jax.experimental.pallas import tpu as pltpu
from jax.sharding import PartitionSpec as P

C = 256
H = 8
DH = 32
G = 64
FF = 1024
ITEMS = 16
STEP = 5
W = 256
T = 128
BATCH = 8
NORM_EPS = 1e-05
SLICE_EPS = 1e-05
CLIP = 1.0
BETA_ONE = 0.5
BETA_TWO = 0.5
ADAM_EPS = 1e-08
DECAY = 0.01
EMA_RATE = 0.6
RATE_ATTN = 0.04
RATE_MLP = 0.03
RATE_SMALL = 0.4
RATE_VECTOR = 0.3
ZO = 4
UN = 48
CB = 144
CL = 32
SM = 80
MESH = pl.DeviceIdType.MESH
HIGH = lax.Precision.HIGHEST
F32 = jnp.float32
BF = jnp.bfloat16
GELU_A = math.sqrt(2.0 / math.pi)
GELU_B = GELU_A * 0.044715


def nn(a, b, precision=None):
    return lax.dot_general(a, b, (((1,), (0,)), ((), ())), precision=precision, preferred_element_type=F32)


def nt(a, b, precision=None):
    return lax.dot_general(a, b, (((1,), (1,)), ((), ())), precision=precision, preferred_element_type=F32)


def tn(a, b, precision=None):
    return lax.dot_general(a, b, (((0,), (0,)), ((), ())), precision=precision, preferred_element_type=F32)


def iota(shape, dim):
    return lax.broadcasted_iota(jnp.int32, shape, dim)


def tile_of(i, width=W):
    return pl.ds(pl.multiple_of(i * width, width), width)


class Place:
    def __init__(self, zs):
        self.p = lax.axis_index("pts")
        self.f = lax.axis_index("fsdp")
        self.a = self.f % 2
        self.x = self.f // 2
        self.y = self.p % 2
        self.z = self.p // 2
        self.m = self.x * 2 + self.y
        self.zs = zs
        self.core = (self.p, self.f + 1 - 2 * self.a)
        self.xpeer = (self.p, (1 - self.x) * 2 + self.a)
        self.ypeer = (self.z * 2 + 1 - self.y, self.f)
        self.zown = self.z if zs == ZO else jnp.minimum(self.z, ZO - 1)

    def xy(self, k):
        mm = (self.m + k) % 4
        return mm, (self.z * 2 + mm % 2, (mm // 2) * 2 + self.a)

    def xy_other(self, k):
        mm = (self.m + k) % 4
        return mm, (self.z * 2 + mm % 2, (mm // 2) * 2 + 1 - self.a)

    def zl(self, k):
        zz = (self.z + k) % self.zs
        return zz, (zz * 2 + self.y, self.f)

    def barrier(self, crossed=False):
        b = pltpu.get_barrier_semaphore()
        peers = [self.core] + [self.xy(k)[1] for k in (1, 2, 3)] + [self.zl(k)[1] for k in range(1, self.zs)]
        if crossed:
            peers += [self.xy_other(k)[1] for k in (1, 2, 3)]
        for d in peers:
            pl.semaphore_signal(b, inc=1, device_id=d, device_id_type=MESH)
        pl.semaphore_wait(b, len(peers))

    def owned(self, z, fn):
        if self.zs == ZO:
            fn()
        else:
            pl.when(z < ZO)(fn)


def rcopy(src, dst, ss, rs, dev):
    return pltpu.make_async_remote_copy(
        src_ref=src, dst_ref=dst, send_sem=ss, recv_sem=rs, device_id=dev, device_id_type=MESH
    )


class Reduce:
    def __init__(self, g, src, bufs):
        self.g, self.src = g, src
        self.r1, self.s2, self.r2, self.s3, self.r3, self.sem = bufs
        self.c1, self.c2, self.c3 = {}, [], []

    @staticmethod
    def scratch(rows, zs):
        return [
            pltpu.VMEM((4, ZO, rows, 128), BF),
            pltpu.VMEM((3, ZO, rows, 128), BF),
            pltpu.VMEM((3, ZO, rows, 128), BF),
            pltpu.VMEM((ZO, rows, 128), BF),
            pltpu.VMEM((zs - 1, rows, 128), BF),
            pltpu.SemaphoreType.DMA((6, max(zs, 4))),
        ]

    def core(self, k):
        g = self.g
        mm = (g.m + k) % 4
        c = rcopy(self.src.at[1 - g.a, mm], self.r1.at[mm], self.sem.at[0, k], self.sem.at[1, k], g.core)
        c.start()
        self.c1[k] = c

    def pair(self, k):
        g = self.g
        self.c1[k].wait_recv()
        mm = (g.m + k) % 4
        return self.src[g.a, mm].astype(F32) + self.r1[mm].astype(F32)

    def square(self, k):
        g = self.g
        dev = g.xy(k)[1]
        self.s2[k - 1] = self.pair(k).astype(BF)
        c = rcopy(self.s2.at[k - 1], self.r2.at[k - 1], self.sem.at[2, k - 1], self.sem.at[3, k - 1], dev)
        c.start()
        self.c2.append(c)

    def line(self):
        g = self.g
        acc = self.pair(0)
        for k in (1, 2, 3):
            self.c2[k - 1].wait_recv()
            acc = acc + self.r2[k - 1].astype(F32)
        self.s3[...] = acc.astype(BF)
        for k in range(1, g.zs):
            zz, dev = g.zl(k)
            at = zz if g.zs == ZO else jnp.minimum(zz, ZO - 1)
            c = rcopy(self.s3.at[at], self.r3.at[k - 1], self.sem.at[4, k - 1], self.sem.at[5, k - 1], dev)
            g.owned(zz, c.start)
            self.c3.append(c)

    def result(self):
        g = self.g
        out = self.s3[g.zown].astype(F32)
        for k in range(1, g.zs):
            g.owned(g.z, self.c3[k - 1].wait_recv)
            out = out + self.r3[k - 1].astype(F32)
        return out

    def finish(self):
        g = self.g
        for c in self.c1.values():
            c.wait_send()
        for c in self.c2:
            c.wait_send()
        for k in range(1, g.zs):
            g.owned(g.zl(k)[0], self.c3[k - 1].wait_send)


class Gather:
    def __init__(self, g, out, sem):
        self.g, self.out, self.sem = g, out, sem
        self.cz, self.cxy, self.cc = [], [], []

    @staticmethod
    def scratch(zs):
        return [pltpu.SemaphoreType.DMA((6, max(zs, 4)))]

    def start(self):
        g = self.g
        own = self.out.at[g.a, g.m, g.zown]
        for k in range(1, g.zs):
            c = rcopy(own, own, self.sem.at[0, k], self.sem.at[1, k], g.zl(k)[1])
            g.owned(g.z, c.start)
            self.cz.append(c)

    def line(self):
        g = self.g
        for k in range(1, g.zs):
            g.owned((g.z - k + g.zs) % g.zs, self.cz[k - 1].wait_recv)
        r = self.out.at[g.a, g.m]
        for j in (1, 2, 3):
            c = rcopy(r, r, self.sem.at[2, j], self.sem.at[3, j], g.xy(j)[1])
            c.start()
            self.cxy.append(c)
        self.to_core(g.m, 0)

    def to_core(self, mm, i):
        r = self.out.at[self.g.a, mm]
        c = rcopy(r, r, self.sem.at[4, i], self.sem.at[5, i], self.g.core)
        c.start()
        self.cc.append(c)

    def square(self):
        g = self.g
        for j in (1, 2, 3):
            self.cxy[j - 1].wait_recv()
            self.to_core((g.m - j + 4) % 4, j)

    def done(self):
        for c in self.cc:
            c.wait_recv()

    def finish(self):
        g = self.g
        for c in self.cz:
            g.owned(g.z, c.wait_send)
        for c in self.cxy + self.cc:
            c.wait_send()


def counts(surface, volume):
    at = jnp.int32(0)
    starts, surfs, sizes = [], [], []
    for b in range(ITEMS):
        starts.append(at)
        surfs.append(surface[0, b])
        sizes.append(surface[0, b] + volume[0, b])
        at = at + sizes[b]
    return starts, surfs, sizes, at


def column(row):
    return jnp.broadcast_to(row, (128, row.shape[1])).T


def wide(col):
    return jnp.concatenate([col, col], axis=1)


def norm_stats(v):
    mean = jnp.mean(v, axis=0, keepdims=True)
    centred = v - mean
    var = jnp.mean(centred * centred, axis=0, keepdims=True)
    scale = lax.rsqrt(var + NORM_EPS)
    return centred * scale, scale


def halves():
    lane = iota((1, 128), 1)
    return (lane < G).astype(F32).astype(BF), (lane >= G).astype(F32).astype(BF)


def spread_units(one, two):
    low, high = halves()
    zero = jnp.zeros((DH, 128), BF)
    return jnp.concatenate(
        [
            jnp.concatenate([one * low, zero], axis=1),
            jnp.concatenate([one * high, zero], axis=1),
            jnp.concatenate([zero, two * low], axis=1),
            jnp.concatenate([zero, two * high], axis=1),
        ],
        axis=0,
    )


def take_units(full):
    low = iota((DH, 128), 1) < G
    one = jnp.where(low, full[0:DH, 0:128], full[DH : 2 * DH, 0:128])
    two = jnp.where(low, full[2 * DH : 3 * DH, 128:256], full[3 * DH : 4 * DH, 128:256])
    return one, two


def item_units(fields, probs):
    left = jnp.concatenate([fields, jnp.ones((16, T), BF)], axis=0)
    full = nt(left, probs)
    one, two = take_units(full)
    one = jnp.concatenate([one, full[128:144, 0:128]], axis=0)
    two = jnp.concatenate([two, full[128:144, 128:256]], axis=0)
    return one.astype(BF), two.astype(BF)


def slice_columns(small):
    low = small[:, 0:128].astype(BF)
    pick = (iota((H * G, 128), 0) % G == iota((H * G, 128), 1)).astype(F32).astype(BF)
    rows = nt(pick, low).astype(BF)
    place = (iota((DH, C), 1) % DH == iota((DH, C), 0)).astype(F32).astype(BF)
    full = nn(rows, place)
    keep = iota((H * G, C), 0) // G == iota((H * G, C), 1) // DH
    return jnp.where(keep, full, 0.0).astype(BF)


def same_head():
    return iota((2 * G, 2 * G), 0) // G == iota((2 * G, 2 * G), 1) // G


def main_kernel(
    zs, surface, volume, points, cotangent, attn_w, mlp_w, small, vector,
    mixed, points_grad, big, late, small_sum, norm_out,
    bounds, surf, keep, xt, cot_t, normed, mid, probs, spread, norm_two, active, d_hidden, d_branch, d_spread, d_mid,
    d_both, wat, wml, wxf, slicew, slicet, wot, wint, woutt, gain_one, gain_two, embed_acc, slice_acc,
    src, src_big, src_late, slice_out, d_slice, saved, attention, maps_acc,
    small_src, sr1, sr2, sr3, sqa, sqb, weight_sem, big_sem, sem, *sems,
):
    g = Place(zs)
    rows = ITEMS * T
    red = [Reduce(g, src.at[i], sems[6 * i : 6 * i + 6]) for i in range(4)]
    red_big = Reduce(g, src_big, sems[24:30])
    red_late = Reduce(g, src_late, sems[30:36])
    gat = [Gather(g, slice_out.at[i], sems[36 + i]) for i in range(2)]
    gat += [Gather(g, d_slice.at[i], sems[38 + i]) for i in range(2)]

    own = pl.ds(pl.multiple_of(g.f * 64, 64), 64)
    other = pl.ds(pl.multiple_of(((1 - g.x) * 2 + g.a) * 64, 64), 64)
    wat[:, own, :] = attn_w[...].astype(BF)
    g.barrier(crossed=True)

    def weight(ref, at, i, dev):
        r = ref.at[:, at, :]
        return rcopy(r, r, weight_sem.at[0, i], weight_sem.at[1, i], dev)

    a_x, a_c = weight(wat, own, 0, g.xpeer), weight(wat, own, 1, g.core)
    m_x, m_c = weight(wml, own, 2, g.xpeer), weight(wml, own, 3, g.core)
    a_f, m_f = weight(wat, other, 4, g.core), weight(wml, other, 5, g.core)
    a_x.start()
    a_c.start()
    wml[:, own, :] = mlp_w[...].astype(BF)
    m_x.start()
    m_c.start()

    starts, surfs, sizes, total = counts(surface, volume)
    lane = iota((1, T), 1)
    for b in range(ITEMS):
        shift = total + b * T - starts[b] - sizes[b]
        bounds[0, b] = starts[b]
        bounds[1, b] = sizes[b]
        bounds[2, b] = shift
        bounds[3, b] = jnp.minimum(lax.div(starts[b], jnp.int32(T)), ITEMS - 2)
        bounds[4, b] = jnp.minimum(lax.div(shift, jnp.int32(T)), ITEMS - 2)
        surf[:, b * T : b * T + T] = (lane < surfs[b]).astype(F32)
        keep[:, b * T : b * T + T] = (lane < sizes[b]).astype(F32)
    gain_a = column(vector[0:1, :])
    gain_b = wide(column(vector[1:2, :]))
    embed = column(vector[2:3, :])
    embed2 = wide(embed)

    def pack_item(b, carry):
        at = tile_of(b, T)
        t, u, size = bounds[3, b], bounds[4, b], bounds[1, b]
        both = [
            jnp.concatenate([ref[i] for i in (t, t + 1, u, u + 1)], axis=0) for ref in (points, cotangent)
        ]
        to, row = iota((T, 2 * T), 0), iota((T, 2 * T), 1)
        one = (row + t * T == to + bounds[0, b]) & (to < size)
        two = (row + u * T == to + bounds[2, b]) & (to >= size)
        pick = jnp.concatenate([one.astype(F32).astype(BF), two.astype(F32).astype(BF)], axis=1)
        field = nn(pick, both[0]).T
        cot_t[:, at] = nn(pick, both[1]).T.astype(BF)
        xt[:, at] = field.astype(BF)
        unit, _ = norm_stats(field + embed * surf[:, at])
        normed[:, at] = (unit * gain_a).astype(BF)
        return carry

    lax.fori_loop(0, ITEMS, pack_item, 0)
    slicew[...] = slice_columns(small)
    for r in (gain_one, gain_two, embed_acc, slice_acc, maps_acc):
        r[...] = jnp.zeros_like(r)

    def turned(v):
        return v.astype(F32).T.astype(BF)

    a_x.wait_recv()
    a_f.start()
    a_c.wait_recv()
    a_f.wait_recv()
    wxf[0:C, :] = turned(wat[0])
    wxf[C : 2 * C, :] = turned(wat[1])

    def soft_tile(i, carry):
        at = tile_of(i)
        both = nn(wxf[...], normed[:, at]).astype(BF)
        mid[:, at] = both
        logits = nn(slicew[...], both[0:C]).reshape(H, G, W)
        top = jnp.max(logits, axis=1, keepdims=True)
        e = jnp.exp(logits - top)
        scale = keep[:, at] / jnp.sum(e, axis=1, keepdims=True)
        probs[:, at] = (e * scale).reshape(H * G, W).astype(BF)
        return carry

    def sums(r, batch, fields, off):
        for half in range(2):
            for k in (1, 2, 3, 0):
                mm = (g.m + k) % 4
                core = (1 - g.a) if half == 0 else g.a
                at = tile_of(batch * BATCH + core * 4 + mm, T)
                for q in range(2):
                    both = item_units(fields[off + q * 128 : off + q * 128 + 128, at], probs[q * 256 : q * 256 + 256, at])
                    for i in range(2):
                        r.src[core, mm, 2 * q + i] = both[i]
                if half == 0:
                    r.core(k)

    def attend(batch):
        unit = red[batch].result()
        raw, scale = unit[0:DH], unit[DH : DH + 8] + SLICE_EPS
        token = raw / scale[0:1]
        qkv = tn(small[...], token, HIGH)
        query, key, value = qkv[64:96], qkv[96:128], qkv[128:160]
        scores = tn(key, query, HIGH) / math.sqrt(DH)
        scores = jnp.where(same_head(), scores, -jnp.inf)
        top = jnp.max(scores, axis=0, keepdims=True)
        e = jnp.exp(scores - top)
        weights = e / jnp.sum(e, axis=0, keepdims=True)
        slice_out[batch, g.a, g.m, g.zown] = nn(value, weights, HIGH).astype(BF)
        gat[batch].start()
        saved[batch, 0:32] = token
        saved[batch, 32:128] = qkv[64:160]
        saved[batch, 128:160] = raw
        saved[batch, 160:168] = scale
        attention[batch] = weights

    def attend_back(batch):
        unit = red[2 + batch].result()
        d_out = unit[0:DH]
        s = saved.at[batch]
        token, query, key, value = s[0:32], s[32:64], s[64:96], s[96:128]
        raw, scale = s[128:160], s[160:161]
        weights = attention[batch]
        d_value = nt(d_out, weights, HIGH)
        d_weights = tn(value, d_out, HIGH)
        d_scores = weights * (d_weights - jnp.sum(weights * d_weights, axis=0, keepdims=True))
        d_query = nn(key, d_scores, HIGH) / math.sqrt(DH)
        d_key = nt(query, d_scores, HIGH) / math.sqrt(DH)
        d_maps = jnp.concatenate([jnp.zeros((64, T), F32), d_query, d_key, d_value], axis=0)
        d_token = nn(small[...], d_maps, HIGH)
        d_total = -jnp.sum(d_token * raw, axis=0, keepdims=True) / (scale * scale)
        tot = jnp.broadcast_to(d_total, (16, T))
        d_slice[batch, g.a, g.m, g.zown] = jnp.concatenate([d_token / scale, tot], axis=0).astype(BF)
        gat[2 + batch].start()
        part = nt(token, jnp.concatenate([d_maps, jnp.zeros((96, T), F32)], axis=0), HIGH)
        if zs != ZO:
            part = jnp.where(g.z < ZO, part, 0.0)
        maps_acc[...] += part

    lax.fori_loop(0, 4, soft_tile, 0)
    sums(red[0], 0, mid, C)
    lax.fori_loop(4, 6, soft_tile, 0)
    for k in (1, 2, 3):
        red[0].square(k)
    lax.fori_loop(6, 8, soft_tile, 0)
    sums(red[1], 1, mid, C)
    red[0].line()
    for k in (1, 2, 3):
        red[1].square(k)
    m_x.wait_recv()
    m_f.start()
    wot[...] = turned(wat[2])
    attend(0)
    red[1].line()
    slicet[...] = turned(slicew[...])
    gat[0].line()
    m_c.wait_recv()
    m_f.wait_recv()
    attend(1)
    gat[0].square()
    for j in range(FF // 256):
        wint[j * 256 : j * 256 + 256, :] = turned(wml[0, :, j * 256 : j * 256 + 256])
        woutt[j * 256 : j * 256 + 256, :] = turned(wml[1, :, j * 256 : j * 256 + 256])
    gat[1].line()
    gat[0].done()

    def spread_item(b, carry):
        at = tile_of(b, T)
        batch = b // BATCH
        core = (b % BATCH) // 4
        for q in range(2):
            units = [slice_out[batch, core, b % 4, 2 * q + i] for i in range(2)]
            part = nn(spread_units(*units), probs[q * 256 : q * 256 + 256, at])
            spread[q * 128 : q * 128 + 128, at] = part.astype(BF)
        return carry

    def mlp_tile(i, carry):
        at = tile_of(i)
        middle = xt[:, at].astype(F32) + embed2 * surf[:, at] + nn(wot[...], spread[:, at])
        unit, scale = norm_stats(middle)
        two = (unit * gain_b).astype(BF)
        norm_two[:, at] = two
        ctb = cot_t[:, at]
        out = middle
        d_two = jnp.zeros((C, W), F32)
        for j in range(FF // 256):
            hid = pl.ds(j * 256, 256)
            x = nn(wint[hid, :], two)
            da = nn(woutt[hid, :], ctb)
            sq = x * x
            t = jnp.tanh(x * (GELU_A + GELU_B * sq))
            s = 0.5 + 0.5 * t
            act = (x * s).astype(BF)
            slope = s + (x * (s - s * s)) * (2.0 * GELU_A + 6.0 * GELU_B * sq)
            dh = (slope * da).astype(BF)
            active[hid, at] = act
            d_hidden[hid, at] = dh
            out = out + nn(wml[1, :, hid], act)
            d_two = d_two + nn(wml[0, :, hid], dh)
        mixed[:, at] = out.astype(BF)
        gs = d_two * unit
        gain_two[...] += gs[:, 0:128] + gs[:, 128:256]
        du = d_two * gain_b
        m1 = jnp.mean(du, axis=0, keepdims=True)
        m2 = jnp.mean(du * unit, axis=0, keepdims=True)
        dm = ctb.astype(F32) + scale * (du - m1 - unit * m2)
        d_mid[:, at] = dm
        db = dm.astype(BF)
        d_branch[:, at] = db
        d_spread[:, at] = nn(wat[2], db).astype(BF)
        return carry

    lax.fori_loop(0, BATCH, spread_item, 0)
    lax.fori_loop(0, 2, mlp_tile, 0)
    gat[1].square()
    lax.fori_loop(2, 4, mlp_tile, 0)
    sums(red[2], 0, d_spread, 0)
    gat[1].done()
    lax.fori_loop(BATCH, ITEMS, spread_item, 0)
    lax.fori_loop(4, 5, mlp_tile, 0)
    for k in (1, 2, 3):
        red[2].square(k)
    lax.fori_loop(5, 7, mlp_tile, 0)
    red[2].line()
    lax.fori_loop(7, 8, mlp_tile, 0)
    sums(red[3], 1, d_spread, 0)
    attend_back(0)

    def put(f, p, lo, value):
        src_big[f % 2, (f // 2) * 2 + p % 2, p // 2, lo : lo + value.shape[0], :] = value

    def grad_mlp(which, left, right):
        for j in range(FF // 256):
            grad = nt(left[...], right[j * 256 : j * 256 + 256, :]).astype(BF)
            for f in range(4):
                for i in range(2):
                    put(f, 2 * j + i, which * 64, grad[f * 64 : f * 64 + 64, i * 128 : i * 128 + 128])

    grad_mlp(0, norm_two, d_hidden)
    for k in (1, 2, 3):
        red[3].square(k)
    gat[2].line()
    grad_mlp(1, cot_t, active)
    grad = nt(spread[...], d_branch[...]).astype(BF)
    for f in range(4):
        for p in range(8):
            lo = f * 64 + (p % 4) * 16
            put(f, p, 128, grad[lo : lo + 16, (p // 4) * 128 : (p // 4) * 128 + 128])
    for k in (1, 2, 3, 0):
        red_big.core(k)
    red[3].line()
    gat[2].square()
    attend_back(1)
    for k in (1, 2, 3):
        red_big.square(k)
    gat[2].done()
    first_row = (iota((16, T), 0) == 0).astype(F32).astype(BF)

    def back_item(b, carry):
        at = tile_of(b, T)
        batch = b // BATCH
        core = (b % BATCH) // 4
        for q in range(2):
            four = slice(q * 128, q * 128 + 128)
            eight = slice(q * 256, q * 256 + 256)
            outs = [slice_out[batch, core, b % 4, 2 * q + i] for i in range(2)]
            ds = [d_slice[batch, core, b % 4, 2 * q + i] for i in range(2)]
            maps = spread_units(ds[0][0:DH], ds[1][0:DH])
            both = jnp.concatenate([spread_units(*outs), maps], axis=0)
            fields = jnp.concatenate([d_spread[four, at], mid[C + q * 128 : C + q * 128 + 128, at]], axis=0)
            tot = jnp.concatenate([ds[0][DH:UN], ds[1][DH:UN]], axis=1)
            pb = probs[eight, at]
            dp = (tn(both, fields) + tn(tot, first_row)).reshape(4, G, T)
            pf = pb.astype(F32).reshape(4, G, T)
            back = pf * (dp - jnp.sum(pf * dp, axis=1, keepdims=True))
            dl = back.reshape(4 * G, T).astype(BF)
            d_both[four, at] = nn(slicet[four, eight], dl).astype(BF)
            d_both[C + q * 128 : C + q * 128 + 128, at] = nn(maps, pb).astype(BF)
            one, two = take_units(nt(mid[four, at], dl))
            slice_acc[...] += one + two
        return carry

    def back_tile(i, carry):
        at = tile_of(i)
        d_norm = nn(wat[0], d_both[0:C, at]) + nn(wat[1], d_both[C : 2 * C, at])
        sf = surf[:, at]
        unit, scale = norm_stats(xt[:, at].astype(F32) + embed2 * sf)
        gs = d_norm * unit
        gain_one[...] += gs[:, 0:128] + gs[:, 128:256]
        du = d_norm * wide(gain_a)
        m1 = jnp.mean(du, axis=0, keepdims=True)
        m2 = jnp.mean(du * unit, axis=0, keepdims=True)
        pg = d_mid[:, at] + scale * (du - m1 - unit * m2)
        es = pg * sf
        embed_acc[...] += es[:, 0:128] + es[:, 128:256]
        points_grad[:, at] = pg
        return carry

    lax.fori_loop(0, 4, back_item, 0)
    gat[3].line()
    lax.fori_loop(4, BATCH, back_item, 0)
    red_big.line()
    gat[3].square()
    lax.fori_loop(0, 4, back_tile, 0)
    gat[3].done()
    lax.fori_loop(BATCH, ITEMS, back_item, 0)

    grads = [nt(normed[...], d_both[i * C : i * C + C, :]).astype(BF) for i in range(2)]
    for f in range(4):
        for p in range(8):
            lo, col = f * 64 + (p % 4) * 16, (p // 4) * 128
            both = [v[lo : lo + 16, col : col + 128] for v in grads]
            src_late[f % 2, (f // 2) * 2 + p % 2, p // 2] = jnp.concatenate(both, axis=0)
    for k in (1, 2, 3, 0):
        red_late.core(k)
    whole = red_big.result().astype(BF)
    big[g.zown, g.y] = whole
    mine = whole.astype(F32)
    squares = jnp.sum((mine * mine).reshape(CB // 8, 8, 128), axis=0)

    def share(ref, base):
        part = ref.at[g.zown, g.y]
        cz, cy = [], []
        for k in range(1, zs):
            c = rcopy(part, part, big_sem.at[base, k], big_sem.at[base + 1, k], g.zl(k)[1])
            g.owned(g.z, c.start)
            cz.append(c)

        def to_y(z, k):
            at = z if zs == ZO else jnp.minimum(z, ZO - 1)
            r = ref.at[at, g.y]
            c = rcopy(r, r, big_sem.at[base + 2, k], big_sem.at[base + 3, k], g.ypeer)
            g.owned(z, c.start)
            cy.append((z, c))

        to_y(g.z, 0)

        def rest():
            for k in range(1, zs):
                z = (g.z - k + zs) % zs
                g.owned(z, cz[k - 1].wait_recv)
                to_y(z, k)

        def done():
            for z, c in cy:
                g.owned(z, c.wait_recv)

        def finish():
            for c in cz:
                g.owned(g.z, c.wait_send)
            for z, c in cy:
                g.owned(z, c.wait_send)

        return rest, done, finish

    big_rest, big_done, big_finish = share(big, 0)
    lax.fori_loop(4, 8, back_tile, 0)

    ones = jnp.ones((8, 128), F32)
    line = [nt(ones, r[...], HIGH) for r in (gain_one, gain_two, embed_acc)]
    fold = slice_acc[...]
    fold = jnp.where(iota((32, 128), 1) < G, fold + pltpu.roll(fold, G, 1), 0.0)
    pick = iota((8, 256), 0)
    vec = jnp.where(pick == 0, line[0], jnp.where(pick == 1, line[1], jnp.where(pick == 2, line[2], 0.0)))
    small_src[0:32] = (fold + maps_acc[:, 0:128]).astype(BF)
    small_src[32:64] = maps_acc[:, 128:256].astype(BF)
    small_src[64:80] = jnp.concatenate([vec[:, 0:128], vec[:, 128:256]], axis=0).astype(BF)
    cs = [rcopy(small_src, sr1, sem.at[0, 0], sem.at[1, 0], g.core)]
    cs[0].start()
    for k in (1, 2, 3):
        red_late.square(k)
    cs[0].wait_recv()
    sr2[g.m] = (small_src[...].astype(F32) + sr1[...].astype(F32)).astype(BF)
    for k in (1, 2, 3):
        c = rcopy(sr2.at[g.m], sr2.at[g.m], sem.at[0, k], sem.at[1, k], g.xy(k)[1])
        c.start()
        cs.append(c)
    big_rest()
    red_late.line()
    for c in cs[1:4]:
        c.wait_recv()
    total = sr2[0].astype(F32)
    for m in range(1, 4):
        total = total + sr2[m].astype(F32)
    sr3[g.z] = total.astype(BF)
    for k in range(1, zs):
        c = rcopy(sr3.at[g.z], sr3.at[g.z], sem.at[2, k], sem.at[3, k], g.zl(k)[1])
        c.start()
        cs.append(c)
    whole = red_late.result().astype(BF)
    late[g.zown, g.y] = whole
    mine = whole.astype(F32)
    squares = squares + jnp.sum((mine * mine).reshape(CL // 8, 8, 128), axis=0)
    if zs != ZO:
        squares = jnp.where(g.z < ZO, squares, 0.0)
    sqa[g.z] = squares
    late_rest, late_done, late_finish = share(late, 4)
    for k in range(1, zs):
        c = rcopy(sqa.at[g.z], sqa.at[g.z], sem.at[6, k], sem.at[7, k], g.zl(k)[1])
        c.start()
        cs.append(c)
    for k in range(1, zs):
        cs[3 + k].wait_recv()
    total = sr3[0].astype(F32)
    for z in range(1, zs):
        total = total + sr3[z].astype(F32)
    small_sum[...] = total
    late_rest()
    for k in range(1, zs):
        cs[2 + zs + k].wait_recv()
    sq = sqa[0]
    for z in range(1, zs):
        sq = sq + sqa[z]
    here = g.a * 4 + g.m
    sqb[here] = sq
    for k in range(1, 8):
        dev = g.core if k == 4 else g.xy(k)[1] if k < 4 else g.xy_other(k - 4)[1]
        c = rcopy(sqb.at[here], sqb.at[here], sem.at[10, k], sem.at[11, k], dev)
        c.start()
        cs.append(c)
    big_done()
    late_done()
    for c in cs[-7:]:
        c.wait_recv()
    sq = sqb[0]
    for i in range(1, 8):
        sq = sq + sqb[i]
    norm_out[0, 0] = jnp.sqrt(jnp.sum(sq) + jnp.sum(total * total))

    for c in cs + [a_x, a_c, m_x, m_c, a_f, m_f]:
        c.wait_send()
    big_finish()
    late_finish()
    for r in red + [red_big, red_late] + gat:
        r.finish()


def adamw(state, new, sl, grad, factor, rate):
    weight, first, second, average = [r[sl] for r in state]
    clipped = grad * factor
    first_new = BETA_ONE * first + (1.0 - BETA_ONE) * clipped
    second_new = BETA_TWO * second + (1.0 - BETA_TWO) * clipped * clipped
    first_hat = first_new / (1.0 - BETA_ONE**STEP)
    second_hat = second_new / (1.0 - BETA_TWO**STEP)
    new_weight = weight - rate * (first_hat / (jnp.sqrt(second_hat) + ADAM_EPS) + DECAY * weight)
    average_new = EMA_RATE * average + (1.0 - EMA_RATE) * new_weight
    for r, v in zip(new, (new_weight, first_new, second_new, average_new, new_weight.astype(BF))):
        r[sl] = v


def last_kernel(surface, volume, mixed_t, grad_t, big, late, small_sum, norm, *refs):
    attn, mlp, small_s, vector_s = [refs[4 * i : 4 * i + 4] for i in range(4)]
    mixed, points_grad = refs[16:18]
    attn_new, mlp_new, small_new, vector_new = [refs[18 + 5 * i : 23 + 5 * i] for i in range(4)]
    wide_mixed = refs[38]
    rows = mixed.shape[0]
    starts, _, sizes, total = counts(surface, volume)
    span = T + 8
    at = iota((span, 1), 0)
    for b in range(ITEMS):
        shift = total + b * T - starts[b] - sizes[b]
        tile = slice(b * T, b * T + T)
        zero = jnp.zeros((8, C), F32)
        for out, value in ((points_grad, grad_t[:, tile]), (wide_mixed, mixed_t[:, tile].astype(F32))):
            turned = jnp.concatenate([value.T, zero], axis=0)
            for base, low, high in ((starts[b], 0, sizes[b]), (shift, sizes[b], T)):
                first = jnp.minimum(lax.div(base, jnp.int32(8)) * 8, rows - span)
                off = base - first
                moved = pltpu.roll(turned, off, 0)
                here = pl.ds(pl.multiple_of(first, 8), span)
                out[here, :] = jnp.where((at >= low + off) & (at < high + off), moved, out[here, :])
    mixed[...] = wide_mixed[...].astype(BF)

    factor = jnp.minimum(1.0, CLIP / norm[0, 0])
    everything = slice(None)
    both = (everything, everything)
    gsmall = jnp.concatenate([small_sum[0:32, :], small_sum[32:64, :]], axis=1)[:, 0:160]
    adamw(small_s, small_new, both, gsmall, factor, RATE_SMALL)
    gvec = jnp.concatenate([small_sum[64:72, :], small_sum[72:80, :]], axis=1)[0:3, :]
    adamw(vector_s, vector_new, both, gvec, factor, RATE_VECTOR)
    for z in range(ZO):
        for y in range(2):
            p = z * 2 + y
            for i in range(2):
                grad = big[z, y, i * 64 : i * 64 + 64, :].astype(F32)
                adamw(mlp, mlp_new, (i, everything, slice(p * 128, p * 128 + 128)), grad, factor, RATE_MLP)
            lo, col = (p % 4) * 16, (p // 4) * 128
            place = (slice(lo, lo + 16), slice(col, col + 128))
            grad = big[z, y, 128:144, :].astype(F32)
            adamw(attn, attn_new, (2,) + place, grad, factor, RATE_ATTN)
            for i in range(2):
                grad = late[z, y, i * 16 : i * 16 + 16, :].astype(F32)
                adamw(attn, attn_new, (i,) + place, grad, factor, RATE_ATTN)


def body(zs, points, cotangent, surface_count, volume_count, *state):
    attn, mlp, small, vector = [state[4 * i : 4 * i + 4] for i in range(4)]
    rows = points.shape[0]
    vmem = pl.BlockSpec(memory_space=pltpu.VMEM)
    smem = pl.BlockSpec(memory_space=pltpu.SMEM)
    sd = jax.ShapeDtypeStruct

    def tall(features, dtype=BF):
        return pltpu.VMEM((features, rows), dtype)

    def units(n, depth):
        return pltpu.VMEM((n, 2, 4, ZO, depth, 128), BF)

    line = max(zs, 8)
    scratch = [
        pltpu.SMEM((5, ITEMS), jnp.int32), tall(1, F32), tall(1, F32),
        tall(C), tall(C), tall(C), tall(2 * C), tall(H * G), tall(C), tall(C), tall(FF), tall(FF), tall(C), tall(C),
        tall(C, F32), tall(2 * C),
        pltpu.VMEM((3, C, C), BF), pltpu.VMEM((2, C, FF), BF), pltpu.VMEM((2 * C, C), BF),
        pltpu.VMEM((H * G, C), BF), pltpu.VMEM((C, H * G), BF), pltpu.VMEM((C, C), BF),
        pltpu.VMEM((FF, C), BF), pltpu.VMEM((FF, C), BF),
        pltpu.VMEM((C, 128), F32), pltpu.VMEM((C, 128), F32), pltpu.VMEM((C, 128), F32), pltpu.VMEM((DH, 128), F32),
        units(4, UN), pltpu.VMEM((2, 4, ZO, CB, 128), BF), pltpu.VMEM((2, 4, ZO, CL, 128), BF),
        units(2, DH), units(2, UN), pltpu.VMEM((2, 168, 128), F32), pltpu.VMEM((2, 128, 128), F32),
        pltpu.VMEM((DH, 256), F32),
        pltpu.VMEM((SM, 128), BF), pltpu.VMEM((SM, 128), BF), pltpu.VMEM((4, SM, 128), BF), pltpu.VMEM((zs, SM, 128), BF),
        pltpu.VMEM((zs, 8, 128), F32), pltpu.VMEM((8, 8, 128), F32),
        pltpu.SemaphoreType.DMA((2, 6)), pltpu.SemaphoreType.DMA((8, line)), pltpu.SemaphoreType.DMA((12, line)),
    ]
    for depth in (UN, UN, UN, UN, CB, CL):
        scratch += Reduce.scratch(depth, zs)
    for _ in range(4):
        scratch += Gather.scratch(zs)
    mixed_t, grad_t, big, late, small_sum, norm = pl.pallas_call(
        functools.partial(main_kernel, zs),
        out_shape=[
            sd((C, rows), BF), sd((C, rows), F32), sd((ZO, 2, CB, 128), BF), sd((ZO, 2, CL, 128), BF),
            sd((SM, 128), F32), sd((1, 1), F32),
        ],
        in_specs=[smem, smem] + [vmem] * 6,
        out_specs=[vmem] * 5 + [smem],
        scratch_shapes=scratch,
        compiler_params=pltpu.CompilerParams(collective_id=0, has_side_effects=True, vmem_limit_bytes=60 << 20),
        name="main",
    )(surface_count, volume_count, points.reshape(-1, T, C), cotangent.reshape(-1, T, C), attn[0], mlp[0], small[0], vector[0])

    def news(leaves):
        return [sd(leaves[0].shape, F32)] * 4 + [sd(leaves[0].shape, BF)]

    outs = pl.pallas_call(
        last_kernel,
        out_shape=[sd((rows, C), BF), sd((rows, C), F32)] + news(attn) + news(mlp) + news(small) + news(vector),
        in_specs=[smem, smem] + [vmem] * 5 + [smem] + [vmem] * 16,
        out_specs=[vmem] * 22,
        scratch_shapes=[pltpu.VMEM((rows, C), F32)],
        compiler_params=pltpu.CompilerParams(vmem_limit_bytes=60 << 20),
        name="last",
    )(surface_count, volume_count, mixed_t, grad_t, big, late, small_sum, norm, *attn, *mlp, *small, *vector)
    return tuple(outs[0:2]) + (norm.reshape(()),) + tuple(outs[2:])


def solution(mesh):
    rows = P(("pts", "fsdp"), None)
    split = P(None, "fsdp", None)
    in_specs = (rows,) * 4 + (split,) * 8 + (P(),) * 8
    out_specs = (rows, rows, P()) + (split,) * 10 + (P(),) * 10
    return jax.shard_map(
        functools.partial(body, mesh.shape["pts"] // 2),
        mesh=mesh, in_specs=in_specs, out_specs=out_specs, check_vma=False,
    )
```

time: 175 us -> 125 us (0.71)
  Pallas kernels: 155 us -> 122 us
  local copies, waits for them, and re-layouts: 16.6 us -> 0 us
    pallas_call x3 -> x2, Pallas kernels: 155 us -> 122 us  [the longest x1 110 us: body(): pl.pallas_call(functools.partial(main_kernel, zs), out_shape=[sd((C, rows...]
    unnamed x66 -> x0, local copies, waits for them, and re-layouts: 16.6 us -> none
where the time goes in v2:
time: 125 us; the launch traced here: 124 us
  Pallas kernels  122 us (98%)
  between operations  2.43 us (2%)
    pallas_call x1, Pallas kernels, body(): pl.pallas_call(functools.partial(main_kernel, zs), out_shape=[sd((C, rows...  110 us
    pallas_call x1, Pallas kernels, body(): pl.pallas_call(last_kernel, out_shape=[sd((rows, C), BF), sd((rows, C), F...  11.8 us

profile of v2, /device:TPU:0, one launch (start us, length us, event | category | flops | bytes accessed | tf_op | source)
XLA Modules:
  0.0 124.4 jit_solution(1167857076978933434)
XLA Ops:
  0.7 110.1 %main.1 = (bf16[256,2048]{1,0:T(8,128)(2,1)}, f32[256,2048]{1,0:T(8,128)}, bf16[4,2,144,128]{3,2,1,0:T(8,128)(2,1)}, bf16[4,2,32,128]{3,2,1,0:T(8,128)(2,1)}, f32[80,128]{1,0:T(8,128)}, /*index=5*/f32[1,1]{1,0:T(1,128)}) custom-call(s32[1,16]{1,0:T(1,128)} %surface.3, s32[1,16]{1,0:T(1,128)} %volume.3, bf16[16,128,256]{2,1,0:T(8,128)(2,1)} %bitcast.3, ...), custom_call_target="tpu_custom_call" | custom-call | tf_op jit(solution)/shard_map/main/pallas_call | solution.py:850
  110.8 11.8 %last.1 = (bf16[2048,256]{1,0:T(8,128)(2,1)}, f32[2048,256]{1,0:T(8,128)}, f32[3,64,256]{2,1,0:T(8,128)}, f32[3,64,256]{2,1,0:T(8,128)}, f32[3,64,256]{2,1,0:T(8...) custom-call(s32[1,16]{1,0:T(1,128)} %surface.3, ...), custom_call_target="tpu_custom_call" | custom-call | tf_op jit(solution)/shard_map/last/pallas_call | solution.py:866

commit v3 on v2

--- a/solution.py
+++ b/solution.py
@@ -86,15 +86,21 @@
         mm = (self.m + k) % 4
         return mm, (self.z * 2 + mm % 2, (mm // 2) * 2 + 1 - self.a)
 
+    def chips(self):
+        return [(k, j) for j in range(self.zs - 1, -1, -1) for k in (3, 2, 1, 0) if k or j]
+
+    def chip(self, k, j):
+        mm, zz = (self.m + k) % 4, (self.z + j) % self.zs
+        return mm, zz, (zz * 2 + mm % 2, (mm // 2) * 2 + self.a)
+
     def zl(self, k):
         zz = (self.z + k) % self.zs
         return zz, (zz * 2 + self.y, self.f)
 
-    def barrier(self, crossed=False):
+    def barrier(self):
         b = pltpu.get_barrier_semaphore()
-        peers = [self.core] + [self.xy(k)[1] for k in (1, 2, 3)] + [self.zl(k)[1] for k in range(1, self.zs)]
-        if crossed:
-            peers += [self.xy_other(k)[1] for k in (1, 2, 3)]
+        peers = [self.core] + [self.chip(k, j)[2] for k, j in self.chips()]
+        peers += [self.xy_other(k)[1] for k in (1, 2, 3)]
         for d in peers:
             pl.semaphore_signal(b, inc=1, device_id=d, device_id_type=MESH)
         pl.semaphore_wait(b, len(peers))
@@ -182,45 +188,85 @@
             g.owned(g.zl(k)[0], self.c3[k - 1].wait_send)
 
 
+class Direct:
+    def __init__(self, g, src, bufs):
+        self.g, self.src = g, src
+        self.r1, self.s2, self.r2, self.core_sem, self.chip_sem = bufs
+        self.c1, self.c2 = {}, {}
+
+    @staticmethod
+    def scratch(rows, zs):
+        return [
+            pltpu.VMEM((4, ZO, rows, 128), BF),
+            pltpu.VMEM((4, ZO, rows, 128), BF),
+            pltpu.VMEM((4, zs, rows, 128), BF),
+            pltpu.SemaphoreType.DMA((2, 4)),
+            pltpu.SemaphoreType.DMA((2, 4, zs)),
+        ]
+
+    def core(self, k):
+        g = self.g
+        mm = (g.m + k) % 4
+        c = rcopy(self.src.at[1 - g.a, mm], self.r1.at[mm], self.core_sem.at[0, k], self.core_sem.at[1, k], g.core)
+        c.start()
+        self.c1[k] = c
+
+    def chips(self):
+        g = self.g
+        for k in (3, 2, 1, 0):
+            self.c1[k].wait_recv()
+            mm = (g.m + k) % 4
+            self.s2[k] = (self.src[g.a, mm].astype(F32) + self.r1[mm].astype(F32)).astype(BF)
+        for k, j in g.chips():
+            _, zz, dev = g.chip(k, j)
+            at = zz if g.zs == ZO else jnp.minimum(zz, ZO - 1)
+            c = rcopy(self.s2.at[k, at], self.r2.at[k, j], self.chip_sem.at[0, k, j], self.chip_sem.at[1, k, j], dev)
+            g.owned(zz, c.start)
+            self.c2[k, j] = (zz, c)
+
+    def result(self):
+        g = self.g
+        out = self.s2[0, g.zown].astype(F32)
+        for k, j in reversed(g.chips()):
+            g.owned(g.z, self.c2[k, j][1].wait_recv)
+            out = out + self.r2[k, j].astype(F32)
+        return out
+
+    def finish(self):
+        for c in self.c1.values():
+            c.wait_send()
+        for zz, c in self.c2.values():
+            self.g.owned(zz, c.wait_send)
+
+
 class Gather:
-    def __init__(self, g, out, sem):
-        self.g, self.out, self.sem = g, out, sem
-        self.cz, self.cxy, self.cc = [], [], []
+    def __init__(self, g, out, bufs):
+        self.g, self.out = g, out
+        self.chip_sem, self.core_sem = bufs
+        self.cz, self.cc = {}, []
 
     @staticmethod
     def scratch(zs):
-        return [pltpu.SemaphoreType.DMA((6, max(zs, 4)))]
+        return [pltpu.SemaphoreType.DMA((2, 4, zs)), pltpu.SemaphoreType.DMA((2, 4))]
 
     def start(self):
         g = self.g
         own = self.out.at[g.a, g.m, g.zown]
-        for k in range(1, g.zs):
-            c = rcopy(own, own, self.sem.at[0, k], self.sem.at[1, k], g.zl(k)[1])
+        for k, j in g.chips():
+            c = rcopy(own, own, self.chip_sem.at[0, k, j], self.chip_sem.at[1, k, j], g.chip(k, j)[2])
             g.owned(g.z, c.start)
-            self.cz.append(c)
-
-    def line(self):
-        g = self.g
-        for k in range(1, g.zs):
-            g.owned((g.z - k + g.zs) % g.zs, self.cz[k - 1].wait_recv)
-        r = self.out.at[g.a, g.m]
-        for j in (1, 2, 3):
-            c = rcopy(r, r, self.sem.at[2, j], self.sem.at[3, j], g.xy(j)[1])
+            self.cz[k, j] = c
+
+    def to_core(self):
+        g = self.g
+        for k in range(4):
+            for j in range(g.zs):
+                if k or j:
+                    g.owned((g.z - j + g.zs) % g.zs, self.cz[k, j].wait_recv)
+            r = self.out.at[g.a, (g.m - k + 4) % 4]
+            c = rcopy(r, r, self.core_sem.at[0, k], self.core_sem.at[1, k], g.core)
             c.start()
-            self.cxy.append(c)
-        self.to_core(g.m, 0)
-
-    def to_core(self, mm, i):
-        r = self.out.at[self.g.a, mm]
-        c = rcopy(r, r, self.sem.at[4, i], self.sem.at[5, i], self.g.core)
-        c.start()
-        self.cc.append(c)
-
-    def square(self):
-        g = self.g
-        for j in (1, 2, 3):
-            self.cxy[j - 1].wait_recv()
-            self.to_core((g.m - j + 4) % 4, j)
+            self.cc.append(c)
 
     def done(self):
         for c in self.cc:
@@ -228,14 +274,14 @@
 
     def finish(self):
         g = self.g
-        for c in self.cz:
+        for c in self.cz.values():
             g.owned(g.z, c.wait_send)
-        for c in self.cxy + self.cc:
+        for c in self.cc:
             c.wait_send()
 
 
 def counts(surface, volume):
-    at = jnp.int32(0)
+    at = surface[0, 0] * 0
     starts, surfs, sizes = [], [], []
     for b in range(ITEMS):
         starts.append(at)
@@ -266,18 +312,9 @@
     return (lane < G).astype(F32).astype(BF), (lane >= G).astype(F32).astype(BF)
 
 
-def spread_units(one, two):
+def spread_unit(unit):
     low, high = halves()
-    zero = jnp.zeros((DH, 128), BF)
-    return jnp.concatenate(
-        [
-            jnp.concatenate([one * low, zero], axis=1),
-            jnp.concatenate([one * high, zero], axis=1),
-            jnp.concatenate([zero, two * low], axis=1),
-            jnp.concatenate([zero, two * high], axis=1),
-        ],
-        axis=0,
-    )
+    return jnp.concatenate([unit * low, unit * high], axis=0)
 
 
 def take_units(full):
@@ -311,38 +348,42 @@
 
 
 def main_kernel(
-    zs, surface, volume, points, cotangent, attn_w, mlp_w, small, vector,
-    mixed, points_grad, big, late, small_sum, norm_out,
+    zs, surface, volume, points_hbm, cot_hbm, attn_w, mlp_w, small, vector,
+    mixed_hbm, grad_hbm, big, late, small_sum, norm_out, points, cotangent, mixed, points_grad, load_sem,
     bounds, surf, keep, xt, cot_t, normed, mid, probs, spread, norm_two, active, d_hidden, d_branch, d_spread, d_mid,
-    d_both, wat, wml, wxf, slicew, slicet, wot, wint, woutt, gain_one, gain_two, embed_acc, slice_acc,
+    d_both, d_logits, wat, wml, wxf, slicew, slicet, wot, wint, woutt, gain_one, gain_two, embed_acc,
     src, src_big, src_late, slice_out, d_slice, saved, attention, maps_acc,
-    small_src, sr1, sr2, sr3, sqa, sqb, weight_sem, big_sem, sem, *sems,
+    small_src, sr1, sr2, sr3, line_late, sqb, weight_sem, big_sem, y_sem, sem, *sems,
 ):
     g = Place(zs)
     rows = ITEMS * T
-    red = [Reduce(g, src.at[i], sems[6 * i : 6 * i + 6]) for i in range(4)]
-    red_big = Reduce(g, src_big, sems[24:30])
-    red_late = Reduce(g, src_late, sems[30:36])
-    gat = [Gather(g, slice_out.at[i], sems[36 + i]) for i in range(2)]
-    gat += [Gather(g, d_slice.at[i], sems[38 + i]) for i in range(2)]
+    red = [Direct(g, src.at[i], sems[5 * i : 5 * i + 5]) for i in range(4)]
+    red_big = Reduce(g, src_big, sems[20:26])
+    red_late = Reduce(g, src_late, sems[26:32])
+    gat = [Gather(g, slice_out.at[i], sems[32 + 2 * i : 34 + 2 * i]) for i in range(2)]
+    gat += [Gather(g, d_slice.at[i], sems[36 + 2 * i : 38 + 2 * i]) for i in range(2)]
 
     own = pl.ds(pl.multiple_of(g.f * 64, 64), 64)
     other = pl.ds(pl.multiple_of(((1 - g.x) * 2 + g.a) * 64, 64), 64)
     wat[:, own, :] = attn_w[...].astype(BF)
-    g.barrier(crossed=True)
-
-    def weight(ref, at, i, dev):
-        r = ref.at[:, at, :]
+    load_points = pltpu.make_async_copy(points_hbm, points, load_sem.at[0])
+    load_cot = pltpu.make_async_copy(cot_hbm, cotangent, load_sem.at[1])
+    load_points.start()
+    g.barrier()
+
+    def weight(ref, lead, at, i, dev):
+        r = ref.at[lead, at, :]
         return rcopy(r, r, weight_sem.at[0, i], weight_sem.at[1, i], dev)
 
-    a_x, a_c = weight(wat, own, 0, g.xpeer), weight(wat, own, 1, g.core)
-    m_x, m_c = weight(wml, own, 2, g.xpeer), weight(wml, own, 3, g.core)
-    a_f, m_f = weight(wat, other, 4, g.core), weight(wml, other, 5, g.core)
+    two, three, all_mlp = pl.ds(0, 2), pl.ds(2, 1), pl.ds(0, 2)
+    a_x, a_c, a_f = weight(wat, two, own, 0, g.xpeer), weight(wat, two, own, 1, g.core), weight(wat, two, other, 2, g.core)
+    o_x, o_c, o_f = weight(wat, three, own, 3, g.xpeer), weight(wat, three, own, 4, g.core), weight(wat, three, other, 5, g.core)
+    m_x, m_c, m_f = weight(wml, all_mlp, own, 6, g.xpeer), weight(wml, all_mlp, own, 7, g.core), weight(wml, all_mlp, other, 8, g.core)
     a_x.start()
     a_c.start()
+    load_cot.start()
     wml[:, own, :] = mlp_w[...].astype(BF)
-    m_x.start()
-    m_c.start()
+    load_points.wait()
 
     starts, surfs, sizes, total = counts(surface, volume)
     lane = iota((1, T), 1)
@@ -360,33 +401,38 @@
     embed = column(vector[2:3, :])
     embed2 = wide(embed)
 
-    def pack_item(b, carry):
-        at = tile_of(b, T)
+    def packed(ref, b):
         t, u, size = bounds[3, b], bounds[4, b], bounds[1, b]
-        both = [
-            jnp.concatenate([ref[i] for i in (t, t + 1, u, u + 1)], axis=0) for ref in (points, cotangent)
-        ]
         to, row = iota((T, 2 * T), 0), iota((T, 2 * T), 1)
         one = (row + t * T == to + bounds[0, b]) & (to < size)
         two = (row + u * T == to + bounds[2, b]) & (to >= size)
         pick = jnp.concatenate([one.astype(F32).astype(BF), two.astype(F32).astype(BF)], axis=1)
-        field = nn(pick, both[0]).T
-        cot_t[:, at] = nn(pick, both[1]).T.astype(BF)
+        return nn(pick, jnp.concatenate([ref[i] for i in (t, t + 1, u, u + 1)], axis=0)).T
+
+    def pack_item(b, carry):
+        at = tile_of(b, T)
+        field = packed(points, b)
         xt[:, at] = field.astype(BF)
         unit, _ = norm_stats(field + embed * surf[:, at])
         normed[:, at] = (unit * gain_a).astype(BF)
         return carry
 
-    lax.fori_loop(0, ITEMS, pack_item, 0)
+    def pack_cot(b, carry):
+        cot_t[:, tile_of(b, T)] = packed(cotangent, b).astype(BF)
+        return carry
+
+    lax.fori_loop(0, ITEMS, pack_item, 0, unroll=8)
+    a_x.wait_recv()
+    a_f.start()
+    for c in (m_x, o_x, m_c, o_c):
+        c.start()
     slicew[...] = slice_columns(small)
-    for r in (gain_one, gain_two, embed_acc, slice_acc, maps_acc):
+    for r in (gain_one, gain_two, embed_acc, maps_acc):
         r[...] = jnp.zeros_like(r)
 
     def turned(v):
         return v.astype(F32).T.astype(BF)
 
-    a_x.wait_recv()
-    a_f.start()
     a_c.wait_recv()
     a_f.wait_recv()
     wxf[0:C, :] = turned(wat[0])
@@ -458,41 +504,39 @@
             part = jnp.where(g.z < ZO, part, 0.0)
         maps_acc[...] += part
 
-    lax.fori_loop(0, 4, soft_tile, 0)
+    lax.fori_loop(0, 4, soft_tile, 0, unroll=2)
     sums(red[0], 0, mid, C)
-    lax.fori_loop(4, 6, soft_tile, 0)
-    for k in (1, 2, 3):
-        red[0].square(k)
-    lax.fori_loop(6, 8, soft_tile, 0)
+    lax.fori_loop(4, 6, soft_tile, 0, unroll=2)
+    red[0].chips()
+    lax.fori_loop(6, 8, soft_tile, 0, unroll=2)
     sums(red[1], 1, mid, C)
-    red[0].line()
-    for k in (1, 2, 3):
-        red[1].square(k)
+    red[1].chips()
     m_x.wait_recv()
     m_f.start()
+    o_x.wait_recv()
+    o_f.start()
+    load_cot.wait()
+    slicet[...] = turned(slicew[...])
+    attend(0)
+    for c in (m_c, o_c, m_f, o_f):
+        c.wait_recv()
     wot[...] = turned(wat[2])
-    attend(0)
-    red[1].line()
-    slicet[...] = turned(slicew[...])
-    gat[0].line()
-    m_c.wait_recv()
-    m_f.wait_recv()
-    attend(1)
-    gat[0].square()
     for j in range(FF // 256):
         wint[j * 256 : j * 256 + 256, :] = turned(wml[0, :, j * 256 : j * 256 + 256])
+    attend(1)
+    for j in range(FF // 256):
         woutt[j * 256 : j * 256 + 256, :] = turned(wml[1, :, j * 256 : j * 256 + 256])
-    gat[1].line()
+    gat[0].to_core()
+    lax.fori_loop(0, ITEMS, pack_cot, 0, unroll=4)
     gat[0].done()
 
     def spread_item(b, carry):
         at = tile_of(b, T)
         batch = b // BATCH
         core = (b % BATCH) // 4
-        for q in range(2):
-            units = [slice_out[batch, core, b % 4, 2 * q + i] for i in range(2)]
-            part = nn(spread_units(*units), probs[q * 256 : q * 256 + 256, at])
-            spread[q * 128 : q * 128 + 128, at] = part.astype(BF)
+        for i in range(4):
+            part = nn(spread_unit(slice_out[batch, core, b % 4, i]), probs[i * 128 : i * 128 + 128, at])
+            spread[i * 64 : i * 64 + 64, at] = part.astype(BF)
         return carry
 
     def mlp_tile(i, carry):
@@ -502,8 +546,6 @@
         two = (unit * gain_b).astype(BF)
         norm_two[:, at] = two
         ctb = cot_t[:, at]
-        out = middle
-        d_two = jnp.zeros((C, W), F32)
         for j in range(FF // 256):
             hid = pl.ds(j * 256, 256)
             x = nn(wint[hid, :], two)
@@ -516,9 +558,8 @@
             dh = (slope * da).astype(BF)
             active[hid, at] = act
             d_hidden[hid, at] = dh
-            out = out + nn(wml[1, :, hid], act)
-            d_two = d_two + nn(wml[0, :, hid], dh)
-        mixed[:, at] = out.astype(BF)
+        d_two = nn(wml[0], d_hidden[:, at])
+        mixed[at, :] = (middle + nn(wml[1], active[:, at])).T.astype(BF)
         gs = d_two * unit
         gain_two[...] += gs[:, 0:128] + gs[:, 128:256]
         du = d_two * gain_b
@@ -531,21 +572,21 @@
         d_spread[:, at] = nn(wat[2], db).astype(BF)
         return carry
 
-    lax.fori_loop(0, BATCH, spread_item, 0)
-    lax.fori_loop(0, 2, mlp_tile, 0)
-    gat[1].square()
-    lax.fori_loop(2, 4, mlp_tile, 0)
+    lax.fori_loop(0, BATCH, spread_item, 0, unroll=8)
+    gat[1].to_core()
+    lax.fori_loop(0, 2, mlp_tile, 0, unroll=2)
+    lax.fori_loop(2, 4, mlp_tile, 0, unroll=2)
     sums(red[2], 0, d_spread, 0)
     gat[1].done()
-    lax.fori_loop(BATCH, ITEMS, spread_item, 0)
-    lax.fori_loop(4, 5, mlp_tile, 0)
-    for k in (1, 2, 3):
-        red[2].square(k)
-    lax.fori_loop(5, 7, mlp_tile, 0)
-    red[2].line()
-    lax.fori_loop(7, 8, mlp_tile, 0)
+    lax.fori_loop(BATCH, ITEMS, spread_item, 0, unroll=8)
+    red[2].chips()
+    lax.fori_loop(4, 6, mlp_tile, 0, unroll=2)
+    lax.fori_loop(6, 8, mlp_tile, 0, unroll=2)
     sums(red[3], 1, d_spread, 0)
+    stores = [pltpu.make_async_copy(mixed, mixed_hbm, load_sem.at[2])]
+    stores[0].start()
     attend_back(0)
+    red[3].chips()
 
     def put(f, p, lo, value):
         src_big[f % 2, (f // 2) * 2 + p % 2, p // 2, lo : lo + value.shape[0], :] = value
@@ -558,9 +599,6 @@
                     put(f, 2 * j + i, which * 64, grad[f * 64 : f * 64 + 64, i * 128 : i * 128 + 128])
 
     grad_mlp(0, norm_two, d_hidden)
-    for k in (1, 2, 3):
-        red[3].square(k)
-    gat[2].line()
     grad_mlp(1, cot_t, active)
     grad = nt(spread[...], d_branch[...]).astype(BF)
     for f in range(4):
@@ -569,36 +607,41 @@
             put(f, p, 128, grad[lo : lo + 16, (p // 4) * 128 : (p // 4) * 128 + 128])
     for k in (1, 2, 3, 0):
         red_big.core(k)
-    red[3].line()
-    gat[2].square()
+    gat[2].to_core()
     attend_back(1)
     for k in (1, 2, 3):
         red_big.square(k)
     gat[2].done()
-    first_row = (iota((16, T), 0) == 0).astype(F32).astype(BF)
+    block = iota((1, 2 * T), 1)
+    block = jnp.where(block < T, block // DH % 2, jnp.where(block == T, 0, jnp.where(block == T + 16, 1, 2)))
+    even, odd = [(block == i).astype(F32).astype(BF) for i in range(2)]
+    ones_rows = jnp.ones((T, T), BF)
+    blank = jnp.zeros((T - 32, T), BF)
 
     def back_item(b, carry):
         at = tile_of(b, T)
         batch = b // BATCH
         core = (b % BATCH) // 4
         for q in range(2):
-            four = slice(q * 128, q * 128 + 128)
-            eight = slice(q * 256, q * 256 + 256)
             outs = [slice_out[batch, core, b % 4, 2 * q + i] for i in range(2)]
             ds = [d_slice[batch, core, b % 4, 2 * q + i] for i in range(2)]
-            maps = spread_units(ds[0][0:DH], ds[1][0:DH])
-            both = jnp.concatenate([spread_units(*outs), maps], axis=0)
-            fields = jnp.concatenate([d_spread[four, at], mid[C + q * 128 : C + q * 128 + 128, at]], axis=0)
-            tot = jnp.concatenate([ds[0][DH:UN], ds[1][DH:UN]], axis=1)
-            pb = probs[eight, at]
-            dp = (tn(both, fields) + tn(tot, first_row)).reshape(4, G, T)
-            pf = pb.astype(F32).reshape(4, G, T)
-            back = pf * (dp - jnp.sum(pf * dp, axis=1, keepdims=True))
-            dl = back.reshape(4 * G, T).astype(BF)
-            d_both[four, at] = nn(slicet[four, eight], dl).astype(BF)
-            d_both[C + q * 128 : C + q * 128 + 128, at] = nn(maps, pb).astype(BF)
-            one, two = take_units(nt(mid[four, at], dl))
-            slice_acc[...] += one + two
+            parts = outs + [d[0:DH] for d in ds] + [d[DH:UN] for d in ds] + [blank]
+            turn = jnp.concatenate(parts, axis=0).T
+            for one in range(2):
+                rows_of = [4 * q + one, 4 * q + 2 + one]
+                left = turn[one * G : one * G + G]
+                left = jnp.concatenate([left * even, left * odd], axis=0)
+                fields = [d_spread[h * DH : h * DH + DH, at] for h in rows_of]
+                fields += [mid[C + h * DH : C + h * DH + DH, at] for h in rows_of]
+                dp = nn(left, jnp.concatenate(fields + [ones_rows], axis=0)).reshape(2, G, T)
+                pf = jnp.stack([probs[h * G : h * G + G, at] for h in rows_of]).astype(F32)
+                back = pf * (dp - jnp.sum(pf * dp, axis=1, keepdims=True))
+                for i, h in enumerate(rows_of):
+                    d_logits[h * G : h * G + G, at] = back[i].astype(BF)
+            for i in range(2):
+                k = 2 * q + i
+                part = nn(spread_unit(ds[i][0:DH]), probs[k * 128 : k * 128 + 128, at])
+                d_both[C + k * 64 : C + k * 64 + 64, at] = part.astype(BF)
         return carry
 
     def back_tile(i, carry):
@@ -614,17 +657,52 @@
         pg = d_mid[:, at] + scale * (du - m1 - unit * m2)
         es = pg * sf
         embed_acc[...] += es[:, 0:128] + es[:, 128:256]
-        points_grad[:, at] = pg
+        points_grad[at, :] = pg.T
         return carry
 
-    lax.fori_loop(0, 4, back_item, 0)
-    gat[3].line()
-    lax.fori_loop(4, BATCH, back_item, 0)
+    def mid_tile(i, carry):
+        at = tile_of(i)
+        d_both[0:C, at] = nn(slicet[...], d_logits[:, at]).astype(BF)
+        return carry
+
+    lax.fori_loop(0, BATCH, back_item, 0, unroll=4)
     red_big.line()
-    gat[3].square()
-    lax.fori_loop(0, 4, back_tile, 0)
+    gat[3].to_core()
+    lax.fori_loop(0, 4, mid_tile, 0, unroll=4)
+    lax.fori_loop(0, 4, back_tile, 0, unroll=4)
+    half_rows = [pl.ds(0, rows // 2), pl.ds(rows // 2, rows // 2)]
+
+    def store_half(i):
+        c = pltpu.make_async_copy(points_grad.at[half_rows[i], :], grad_hbm.at[half_rows[i], :], load_sem.at[3 + i])
+        c.start()
+        stores.append(c)
+
+    store_half(0)
+    whole = red_big.result().astype(BF)
+    big[g.zown, g.y] = whole
+
+    def copies(ref, base):
+        part = ref.at[g.zown, g.y]
+        cz = []
+        for k in range(1, zs):
+            c = rcopy(part, part, big_sem.at[base, k], big_sem.at[base + 1, k], g.zl(k)[1])
+            g.owned(g.z, c.start)
+            cz.append(c)
+        return cz
+
+    def to_y(ref, sem):
+        cy = []
+        for z in range(ZO):
+            r = ref.at[z, g.y]
+            c = rcopy(r, r, sem.at[0, z], sem.at[1, z], g.ypeer)
+            c.start()
+            cy.append(c)
+        return cy
+
+    big_z = copies(big, 0)
     gat[3].done()
-    lax.fori_loop(BATCH, ITEMS, back_item, 0)
+    lax.fori_loop(BATCH, ITEMS, back_item, 0, unroll=4)
+    lax.fori_loop(4, 8, mid_tile, 0, unroll=4)
 
     grads = [nt(normed[...], d_both[i * C : i * C + C, :]).astype(BF) for i in range(2)]
     for f in range(4):
@@ -634,53 +712,21 @@
             src_late[f % 2, (f // 2) * 2 + p % 2, p // 2] = jnp.concatenate(both, axis=0)
     for k in (1, 2, 3, 0):
         red_late.core(k)
-    whole = red_big.result().astype(BF)
-    big[g.zown, g.y] = whole
-    mine = whole.astype(F32)
-    squares = jnp.sum((mine * mine).reshape(CB // 8, 8, 128), axis=0)
-
-    def share(ref, base):
-        part = ref.at[g.zown, g.y]
-        cz, cy = [], []
-        for k in range(1, zs):
-            c = rcopy(part, part, big_sem.at[base, k], big_sem.at[base + 1, k], g.zl(k)[1])
-            g.owned(g.z, c.start)
-            cz.append(c)
-
-        def to_y(z, k):
-            at = z if zs == ZO else jnp.minimum(z, ZO - 1)
-            r = ref.at[at, g.y]
-            c = rcopy(r, r, big_sem.at[base + 2, k], big_sem.at[base + 3, k], g.ypeer)
-            g.owned(z, c.start)
-            cy.append((z, c))
-
-        to_y(g.z, 0)
-
-        def rest():
-            for k in range(1, zs):
-                z = (g.z - k + zs) % zs
-                g.owned(z, cz[k - 1].wait_recv)
-                to_y(z, k)
-
-        def done():
-            for z, c in cy:
-                g.owned(z, c.wait_recv)
-
-        def finish():
-            for c in cz:
-                g.owned(g.z, c.wait_send)
-            for z, c in cy:
-                g.owned(z, c.wait_send)
-
-        return rest, done, finish
-
-    big_rest, big_done, big_finish = share(big, 0)
-    lax.fori_loop(4, 8, back_tile, 0)
+    fold = jnp.zeros((DH, 128), F32)
+    for i in range(4):
+        part = nt(mid[i * 64 : i * 64 + 64, :], d_logits[i * 128 : i * 128 + 128, :])
+        fold = fold + jnp.where(iota((DH, 128), 1) < G, part[0:DH], part[DH : 2 * DH])
+    fold = jnp.where(iota((32, 128), 1) < G, fold + pltpu.roll(fold, G, 1), 0.0)
+    for k in (1, 2, 3):
+        red_late.square(k)
+    for k in range(1, zs):
+        g.owned((g.z - k + zs) % zs, big_z[k - 1].wait_recv)
+    big_y = to_y(big, y_sem.at[0])
+    lax.fori_loop(4, 8, back_tile, 0, unroll=4)
+    store_half(1)
 
     ones = jnp.ones((8, 128), F32)
     line = [nt(ones, r[...], HIGH) for r in (gain_one, gain_two, embed_acc)]
-    fold = slice_acc[...]
-    fold = jnp.where(iota((32, 128), 1) < G, fold + pltpu.roll(fold, G, 1), 0.0)
     pick = iota((8, 256), 0)
     vec = jnp.where(pick == 0, line[0], jnp.where(pick == 1, line[1], jnp.where(pick == 2, line[2], 0.0)))
     small_src[0:32] = (fold + maps_acc[:, 0:128]).astype(BF)
@@ -688,16 +734,42 @@
     small_src[64:80] = jnp.concatenate([vec[:, 0:128], vec[:, 128:256]], axis=0).astype(BF)
     cs = [rcopy(small_src, sr1, sem.at[0, 0], sem.at[1, 0], g.core)]
     cs[0].start()
+
+    acc = red_late.pair(0)
     for k in (1, 2, 3):
-        red_late.square(k)
+        red_late.c2[k - 1].wait_recv()
+        acc = acc + red_late.r2[k - 1].astype(F32)
+    line_late[g.z] = acc.astype(BF)
+    line_copies = []
+    for k in range(1, zs):
+        c = rcopy(line_late.at[g.z], line_late.at[g.z], sem.at[4, k], sem.at[5, k], g.zl(k)[1])
+        c.start()
+        line_copies.append(c)
     cs[0].wait_recv()
     sr2[g.m] = (small_src[...].astype(F32) + sr1[...].astype(F32)).astype(BF)
     for k in (1, 2, 3):
         c = rcopy(sr2.at[g.m], sr2.at[g.m], sem.at[0, k], sem.at[1, k], g.xy(k)[1])
         c.start()
         cs.append(c)
-    big_rest()
-    red_late.line()
+    bigs = big[:, g.y].astype(F32).reshape(ZO * CB // 8, 8, 128)
+    squares = jnp.sum(bigs * bigs, axis=0)
+    for c in line_copies:
+        c.wait_recv()
+    acc = line_late[0].astype(F32)
+    for z in range(1, zs):
+        acc = acc + line_late[z].astype(F32)
+    acc = acc.astype(BF)
+    late[:, g.y] = acc
+    mine = acc.astype(F32).reshape(ZO * CL // 8, 8, 128)
+    here = g.a * 4 + g.m
+    sqb[here] = squares + jnp.sum(mine * mine, axis=0)
+    sq_copies = []
+    for k in range(1, 8):
+        dev = g.core if k == 4 else g.xy(k)[1] if k < 4 else g.xy_other(k - 4)[1]
+        c = rcopy(sqb.at[here], sqb.at[here], sem.at[10, k], sem.at[11, k], dev)
+        c.start()
+        sq_copies.append(c)
+    late_y = to_y(late, y_sem.at[1])
     for c in cs[1:4]:
         c.wait_recv()
     total = sr2[0].astype(F32)
@@ -708,51 +780,30 @@
         c = rcopy(sr3.at[g.z], sr3.at[g.z], sem.at[2, k], sem.at[3, k], g.zl(k)[1])
         c.start()
         cs.append(c)
-    whole = red_late.result().astype(BF)
-    late[g.zown, g.y] = whole
-    mine = whole.astype(F32)
-    squares = squares + jnp.sum((mine * mine).reshape(CL // 8, 8, 128), axis=0)
-    if zs != ZO:
-        squares = jnp.where(g.z < ZO, squares, 0.0)
-    sqa[g.z] = squares
-    late_rest, late_done, late_finish = share(late, 4)
-    for k in range(1, zs):
-        c = rcopy(sqa.at[g.z], sqa.at[g.z], sem.at[6, k], sem.at[7, k], g.zl(k)[1])
-        c.start()
-        cs.append(c)
-    for k in range(1, zs):
-        cs[3 + k].wait_recv()
+    for c in big_y + late_y + cs[4:]:
+        c.wait_recv()
     total = sr3[0].astype(F32)
     for z in range(1, zs):
         total = total + sr3[z].astype(F32)
     small_sum[...] = total
-    late_rest()
-    for k in range(1, zs):
-        cs[2 + zs + k].wait_recv()
-    sq = sqa[0]
-    for z in range(1, zs):
-        sq = sq + sqa[z]
-    here = g.a * 4 + g.m
-    sqb[here] = sq
-    for k in range(1, 8):
-        dev = g.core if k == 4 else g.xy(k)[1] if k < 4 else g.xy_other(k - 4)[1]
-        c = rcopy(sqb.at[here], sqb.at[here], sem.at[10, k], sem.at[11, k], dev)
-        c.start()
-        cs.append(c)
-    big_done()
-    late_done()
-    for c in cs[-7:]:
+    for c in sq_copies:
         c.wait_recv()
     sq = sqb[0]
     for i in range(1, 8):
         sq = sq + sqb[i]
     norm_out[0, 0] = jnp.sqrt(jnp.sum(sq) + jnp.sum(total * total))
 
-    for c in cs + [a_x, a_c, m_x, m_c, a_f, m_f]:
+    for c in cs + line_copies + sq_copies + big_y + late_y + [a_x, a_c, a_f, o_x, o_c, o_f, m_x, m_c, m_f]:
         c.wait_send()
-    big_finish()
-    late_finish()
-    for r in red + [red_big, red_late] + gat:
+    for c in stores:
+        c.wait()
+    for c in big_z:
+        g.owned(g.z, c.wait_send)
+    for c in red_late.c1.values():
+        c.wait_send()
+    for c in red_late.c2:
+        c.wait_send()
+    for r in red + [red_big] + gat:
         r.finish()
 
 
@@ -769,49 +820,86 @@
         r[sl] = v
 
 
-def last_kernel(surface, volume, mixed_t, grad_t, big, late, small_sum, norm, *refs):
-    attn, mlp, small_s, vector_s = [refs[4 * i : 4 * i + 4] for i in range(4)]
-    mixed, points_grad = refs[16:18]
-    attn_new, mlp_new, small_new, vector_new = [refs[18 + 5 * i : 23 + 5 * i] for i in range(4)]
-    wide_mixed = refs[38]
-    rows = mixed.shape[0]
+def last_kernel(surface, volume, norm, mixed_p, grad_p, big, late, small_sum, *refs):
+    hbm_states, hbm_outs = refs[0:16], refs[16:38]
+    states, news = refs[38:54], refs[54:74]
+    rows_in, mixed_rows, mixed_low, grad_rows, in_sem, out_sem = refs[74:]
+    rows = mixed_low.shape[0]
+    ins = [pltpu.make_async_copy(h, v, in_sem.at[i]) for i, (h, v) in enumerate(zip(hbm_states, states))]
+    gp = pltpu.make_async_copy(grad_p, rows_in, in_sem.at[16])
+    gp.start()
+    for c in ins:
+        c.start()
     starts, _, sizes, total = counts(surface, volume)
-    span = T + 8
-    at = iota((span, 1), 0)
-    for b in range(ITEMS):
-        shift = total + b * T - starts[b] - sizes[b]
-        tile = slice(b * T, b * T + T)
-        zero = jnp.zeros((8, C), F32)
-        for out, value in ((points_grad, grad_t[:, tile]), (wide_mixed, mixed_t[:, tile].astype(F32))):
-            turned = jnp.concatenate([value.T, zero], axis=0)
-            for base, low, high in ((starts[b], 0, sizes[b]), (shift, sizes[b], T)):
-                first = jnp.minimum(lax.div(base, jnp.int32(8)) * 8, rows - span)
-                off = base - first
-                moved = pltpu.roll(turned, off, 0)
-                here = pl.ds(pl.multiple_of(first, 8), span)
-                out[here, :] = jnp.where((at >= low + off) & (at < high + off), moved, out[here, :])
-    mixed[...] = wide_mixed[...].astype(BF)
-
+
+    row = iota((T + 8, 1), 0)
+
+    def place(source, out):
+        blank = jnp.zeros((8, C), F32)
+
+        def moved(b, base):
+            first = pl.multiple_of(lax.div(base, jnp.int32(8)) * 8, 8)
+            tile = jnp.concatenate([source[b * T : b * T + T, :].astype(F32), blank], axis=0)
+            return first, base - first, pltpu.roll(tile, base - first, 0)
+
+        for b in range(ITEMS):
+            first, off, tile = moved(b, starts[b])
+            head = pl.ds(first, 8)
+            out[head, :] = jnp.where(row[0:8] >= off, tile[0:8], out[head, :])
+            out[pl.ds(pl.multiple_of(first + 8, 8), T), :] = tile[8:]
+        for b in range(ITEMS):
+            first, off, tile = moved(b, total + b * T - starts[b] - sizes[b])
+            here = pl.ds(first, T + 8)
+            out[here, :] = jnp.where(row >= sizes[b] + off, tile, out[here, :])
+
+    gp.wait()
+    place(rows_in, grad_rows)
+    outs = [pltpu.make_async_copy(grad_rows.at[pl.ds(0, rows), :], hbm_outs[1], out_sem.at[1])]
+    outs[0].start()
+    place(mixed_p, mixed_rows)
+    mixed_low[...] = mixed_rows[0:rows, :].astype(BF)
+    outs.append(pltpu.make_async_copy(mixed_low, hbm_outs[0], out_sem.at[0]))
+    outs[1].start()
+
+    attn, mlp, small_s, vector_s = [states[4 * i : 4 * i + 4] for i in range(4)]
+    attn_new, mlp_new, small_new, vector_new = [news[5 * i : 5 * i + 5] for i in range(4)]
     factor = jnp.minimum(1.0, CLIP / norm[0, 0])
     everything = slice(None)
     both = (everything, everything)
-    gsmall = jnp.concatenate([small_sum[0:32, :], small_sum[32:64, :]], axis=1)[:, 0:160]
-    adamw(small_s, small_new, both, gsmall, factor, RATE_SMALL)
-    gvec = jnp.concatenate([small_sum[64:72, :], small_sum[72:80, :]], axis=1)[0:3, :]
-    adamw(vector_s, vector_new, both, gvec, factor, RATE_VECTOR)
+    for c in ins:
+        c.wait()
     for z in range(ZO):
         for y in range(2):
             p = z * 2 + y
             for i in range(2):
                 grad = big[z, y, i * 64 : i * 64 + 64, :].astype(F32)
                 adamw(mlp, mlp_new, (i, everything, slice(p * 128, p * 128 + 128)), grad, factor, RATE_MLP)
+
+    def send(first, count):
+        for i in range(first, first + count):
+            c = pltpu.make_async_copy(news[i], hbm_outs[2 + i], out_sem.at[2 + i])
+            c.start()
+            outs.append(c)
+
+    send(5, 5)
+    for z in range(ZO):
+        for y in range(2):
+            p = z * 2 + y
             lo, col = (p % 4) * 16, (p // 4) * 128
-            place = (slice(lo, lo + 16), slice(col, col + 128))
+            at = (slice(lo, lo + 16), slice(col, col + 128))
             grad = big[z, y, 128:144, :].astype(F32)
-            adamw(attn, attn_new, (2,) + place, grad, factor, RATE_ATTN)
+            adamw(attn, attn_new, (2,) + at, grad, factor, RATE_ATTN)
             for i in range(2):
                 grad = late[z, y, i * 16 : i * 16 + 16, :].astype(F32)
-                adamw(attn, attn_new, (i,) + place, grad, factor, RATE_ATTN)
+                adamw(attn, attn_new, (i,) + at, grad, factor, RATE_ATTN)
+    send(0, 5)
+    gsmall = jnp.concatenate([small_sum[0:32, :], small_sum[32:64, :]], axis=1)[:, 0:160]
+    adamw(small_s, small_new, both, gsmall, factor, RATE_SMALL)
+    gvec = jnp.concatenate([small_sum[64:72, :], small_sum[72:80, :]], axis=1)[0:3, :]
+    adamw(vector_s, vector_new, both, gvec, factor, RATE_VECTOR)
+    send(10, 10)
+    for c in outs:
+        c.wait()
 
 
 def body(zs, points, cotangent, surface_count, volume_count, *state):
@@ -819,6 +907,7 @@
     rows = points.shape[0]
     vmem = pl.BlockSpec(memory_space=pltpu.VMEM)
     smem = pl.BlockSpec(memory_space=pltpu.SMEM)
+    hbm = pl.BlockSpec(memory_space=pl.ANY)
     sd = jax.ShapeDtypeStruct
 
     def tall(features, dtype=BF):
@@ -829,32 +918,37 @@
 
     line = max(zs, 8)
     scratch = [
+        pltpu.VMEM((rows // T, T, C), BF), pltpu.VMEM((rows // T, T, C), BF), pltpu.VMEM((rows, C), BF),
+        pltpu.VMEM((rows, C), F32), pltpu.SemaphoreType.DMA((5,)),
         pltpu.SMEM((5, ITEMS), jnp.int32), tall(1, F32), tall(1, F32),
         tall(C), tall(C), tall(C), tall(2 * C), tall(H * G), tall(C), tall(C), tall(FF), tall(FF), tall(C), tall(C),
-        tall(C, F32), tall(2 * C),
+        tall(C, F32), tall(2 * C), tall(H * G),
         pltpu.VMEM((3, C, C), BF), pltpu.VMEM((2, C, FF), BF), pltpu.VMEM((2 * C, C), BF),
         pltpu.VMEM((H * G, C), BF), pltpu.VMEM((C, H * G), BF), pltpu.VMEM((C, C), BF),
         pltpu.VMEM((FF, C), BF), pltpu.VMEM((FF, C), BF),
-        pltpu.VMEM((C, 128), F32), pltpu.VMEM((C, 128), F32), pltpu.VMEM((C, 128), F32), pltpu.VMEM((DH, 128), F32),
+        pltpu.VMEM((C, 128), F32), pltpu.VMEM((C, 128), F32), pltpu.VMEM((C, 128), F32),
         units(4, UN), pltpu.VMEM((2, 4, ZO, CB, 128), BF), pltpu.VMEM((2, 4, ZO, CL, 128), BF),
         units(2, DH), units(2, UN), pltpu.VMEM((2, 168, 128), F32), pltpu.VMEM((2, 128, 128), F32),
         pltpu.VMEM((DH, 256), F32),
         pltpu.VMEM((SM, 128), BF), pltpu.VMEM((SM, 128), BF), pltpu.VMEM((4, SM, 128), BF), pltpu.VMEM((zs, SM, 128), BF),
-        pltpu.VMEM((zs, 8, 128), F32), pltpu.VMEM((8, 8, 128), F32),
-        pltpu.SemaphoreType.DMA((2, 6)), pltpu.SemaphoreType.DMA((8, line)), pltpu.SemaphoreType.DMA((12, line)),
+        pltpu.VMEM((zs, ZO, CL, 128), BF), pltpu.VMEM((8, 8, 128), F32),
+        pltpu.SemaphoreType.DMA((2, 9)), pltpu.SemaphoreType.DMA((2, line)), pltpu.SemaphoreType.DMA((2, 2, ZO)),
+        pltpu.SemaphoreType.DMA((12, line)),
     ]
-    for depth in (UN, UN, UN, UN, CB, CL):
+    for _ in range(4):
+        scratch += Direct.scratch(UN, zs)
+    for depth in (CB, CL):
         scratch += Reduce.scratch(depth, zs)
     for _ in range(4):
         scratch += Gather.scratch(zs)
-    mixed_t, grad_t, big, late, small_sum, norm = pl.pallas_call(
+    mixed_p, grad_p, big, late, small_sum, norm = pl.pallas_call(
         functools.partial(main_kernel, zs),
         out_shape=[
-            sd((C, rows), BF), sd((C, rows), F32), sd((ZO, 2, CB, 128), BF), sd((ZO, 2, CL, 128), BF),
+            sd((rows, C), BF), sd((rows, C), F32), sd((ZO, 2, CB, 128), BF), sd((ZO, 2, CL, 128), BF),
             sd((SM, 128), F32), sd((1, 1), F32),
         ],
-        in_specs=[smem, smem] + [vmem] * 6,
-        out_specs=[vmem] * 5 + [smem],
+        in_specs=[smem, smem, hbm, hbm] + [vmem] * 4,
+        out_specs=[hbm, hbm] + [vmem] * 3 + [smem],
         scratch_shapes=scratch,
         compiler_params=pltpu.CompilerParams(collective_id=0, has_side_effects=True, vmem_limit_bytes=60 << 20),
         name="main",
@@ -863,15 +957,21 @@
     def news(leaves):
         return [sd(leaves[0].shape, F32)] * 4 + [sd(leaves[0].shape, BF)]
 
+    everything = news(attn) + news(mlp) + news(small) + news(vector)
     outs = pl.pallas_call(
         last_kernel,
-        out_shape=[sd((rows, C), BF), sd((rows, C), F32)] + news(attn) + news(mlp) + news(small) + news(vector),
-        in_specs=[smem, smem] + [vmem] * 5 + [smem] + [vmem] * 16,
-        out_specs=[vmem] * 22,
-        scratch_shapes=[pltpu.VMEM((rows, C), F32)],
+        out_shape=[sd((rows, C), BF), sd((rows, C), F32)] + everything,
+        in_specs=[smem, smem, smem, vmem, hbm, vmem, vmem, vmem] + [hbm] * 16,
+        out_specs=[hbm] * 22,
+        scratch_shapes=[pltpu.VMEM(v.shape, v.dtype) for v in state]
+        + [pltpu.VMEM(v.shape, v.dtype) for v in everything]
+        + [
+            pltpu.VMEM((rows, C), F32), pltpu.VMEM((rows + T, C), F32), pltpu.VMEM((rows, C), BF),
+            pltpu.VMEM((rows + T, C), F32), pltpu.SemaphoreType.DMA((17,)), pltpu.SemaphoreType.DMA((22,)),
+        ],
         compiler_params=pltpu.CompilerParams(vmem_limit_bytes=60 << 20),
         name="last",
-    )(surface_count, volume_count, mixed_t, grad_t, big, late, small_sum, norm, *attn, *mlp, *small, *vector)
+    )(surface_count, volume_count, norm, mixed_p, grad_p, big, late, small_sum, *state)
     return tuple(outs[0:2]) + (norm.reshape(()),) + tuple(outs[2:])
 
 

time: 125 us -> 109 us (0.87)
  Pallas kernels: 122 us -> 107 us
    pallas_call x1, Pallas kernels: 110 us -> 95.7 us  [body(): pl.pallas_call(functools.partial(main_kernel, zs), out_shape=[sd((rows, C...]
where the time goes in v3:
time: 109 us
  Pallas kernels  107 us (98%)
  between operations  2.42 us (2%)
    pallas_call x1, Pallas kernels, body(): pl.pallas_call(functools.partial(main_kernel, zs), out_shape=[sd((rows, C...  95.7 us
    pallas_call x1, Pallas kernels, body(): pl.pallas_call(last_kernel, out_shape=[sd((rows, C), BF), sd((rows, C), F...  10.9 us

profile of v3, /device:TPU:0, one launch (start us, length us, event | category | flops | bytes accessed | tf_op | source)
XLA Modules:
  0.0 109.0 jit_solution(17580187778165166889)
XLA Ops:
  0.7 95.7 %main.1 = (bf16[2048,256]{1,0:T(8,128)(2,1)}, f32[2048,256]{1,0:T(8,128)}, bf16[4,2,144,128]{3,2,1,0:T(8,128)(2,1)}, bf16[4,2,32,128]{3,2,1,0:T(8,128)(2,1)}, f32[80,128]{1,0:T(8,128)}, /*index=5*/f32[1,1]{1,0:T(1,128)}) custom-call(s32[1,16]{1,0:T(1,128)} %surface.3, s32[1,16]{1,0:T(1,128)} %volume.3, bf16[16,128,256]{2,1,0:T(8,128)(2,1)} %bitcast.3, ...), custom_call_target="tpu_custom_call" | custom-call | tf_op jit(solution)/shard_map/main/pallas_call | solution.py:944
  96.4 10.9 %last.1 = (bf16[2048,256]{1,0:T(8,128)(2,1)}, f32[2048,256]{1,0:T(8,128)}, f32[3,64,256]{2,1,0:T(8,128)}, f32[3,64,256]{2,1,0:T(8,128)}, f32[3,64,256]{2,1,0:T(8...) custom-call(s32[1,16]{1,0:T(1,128)} %surface.3, ...), custom_call_target="tpu_custom_call" | custom-call | tf_op jit(solution)/shard_map/last/pallas_call | solution.py:961

commit v4 on v3

--- a/solution.py
+++ b/solution.py
@@ -353,15 +353,15 @@
     bounds, surf, keep, xt, cot_t, normed, mid, probs, spread, norm_two, active, d_hidden, d_branch, d_spread, d_mid,
     d_both, d_logits, wat, wml, wxf, slicew, slicet, wot, wint, woutt, gain_one, gain_two, embed_acc,
     src, src_big, src_late, slice_out, d_slice, saved, attention, maps_acc,
-    small_src, sr1, sr2, sr3, line_late, sqb, weight_sem, big_sem, y_sem, sem, *sems,
+    small_src, sr1, sr2, sr3, line_late, sqb, weight_sem, big_sem, y_sem, sem, sq_sem, *sems,
 ):
     g = Place(zs)
     rows = ITEMS * T
-    red = [Direct(g, src.at[i], sems[5 * i : 5 * i + 5]) for i in range(4)]
-    red_big = Reduce(g, src_big, sems[20:26])
-    red_late = Reduce(g, src_late, sems[26:32])
-    gat = [Gather(g, slice_out.at[i], sems[32 + 2 * i : 34 + 2 * i]) for i in range(2)]
-    gat += [Gather(g, d_slice.at[i], sems[36 + 2 * i : 38 + 2 * i]) for i in range(2)]
+    red = [Direct(g, src.at[i], sems[3 * i : 3 * i + 3] + sems[12 + 2 * (i % 2) : 14 + 2 * (i % 2)]) for i in range(4)]
+    red_big = Reduce(g, src_big, sems[16:22])
+    red_late = Reduce(g, src_late, sems[22:28])
+    gat = [Gather(g, slice_out.at[i], sems[28 + 2 * i : 30 + 2 * i]) for i in range(2)]
+    gat += [Gather(g, d_slice.at[i], sems[28 + 2 * i : 30 + 2 * i]) for i in range(2)]
 
     own = pl.ds(pl.multiple_of(g.f * 64, 64), 64)
     other = pl.ds(pl.multiple_of(((1 - g.x) * 2 + g.a) * 64, 64), 64)
@@ -473,7 +473,7 @@
         top = jnp.max(scores, axis=0, keepdims=True)
         e = jnp.exp(scores - top)
         weights = e / jnp.sum(e, axis=0, keepdims=True)
-        slice_out[batch, g.a, g.m, g.zown] = nn(value, weights, HIGH).astype(BF)
+        slice_out[batch, g.a, g.m, g.zown] = nn(value.astype(BF), weights.astype(BF)).astype(BF)
         gat[batch].start()
         saved[batch, 0:32] = token
         saved[batch, 32:128] = qkv[64:160]
@@ -488,18 +488,21 @@
         token, query, key, value = s[0:32], s[32:64], s[64:96], s[96:128]
         raw, scale = s[128:160], s[160:161]
         weights = attention[batch]
-        d_value = nt(d_out, weights, HIGH)
-        d_weights = tn(value, d_out, HIGH)
+        low = weights.astype(BF)
+        d_low, query, key, value = [v.astype(BF) for v in (d_out, query, key, value)]
+        d_value = nt(d_low, low)
+        d_weights = tn(value, d_low)
         d_scores = weights * (d_weights - jnp.sum(weights * d_weights, axis=0, keepdims=True))
-        d_query = nn(key, d_scores, HIGH) / math.sqrt(DH)
-        d_key = nt(query, d_scores, HIGH) / math.sqrt(DH)
-        d_maps = jnp.concatenate([jnp.zeros((64, T), F32), d_query, d_key, d_value], axis=0)
-        d_token = nn(small[...], d_maps, HIGH)
+        d_scores = (d_scores / math.sqrt(DH)).astype(BF)
+        d_query = nn(key, d_scores)
+        d_key = nt(query, d_scores)
+        d_maps = jnp.concatenate([jnp.zeros((64, T), F32), d_query, d_key, d_value], axis=0).astype(BF)
+        d_token = nn(small[...].astype(BF), d_maps)
         d_total = -jnp.sum(d_token * raw, axis=0, keepdims=True) / (scale * scale)
         tot = jnp.broadcast_to(d_total, (16, T))
         d_slice[batch, g.a, g.m, g.zown] = jnp.concatenate([d_token / scale, tot], axis=0).astype(BF)
         gat[2 + batch].start()
-        part = nt(token, jnp.concatenate([d_maps, jnp.zeros((96, T), F32)], axis=0), HIGH)
+        part = nt(token.astype(BF), jnp.concatenate([d_maps, jnp.zeros((96, T), BF)], axis=0))
         if zs != ZO:
             part = jnp.where(g.z < ZO, part, 0.0)
         maps_acc[...] += part
@@ -576,17 +579,20 @@
     gat[1].to_core()
     lax.fori_loop(0, 2, mlp_tile, 0, unroll=2)
     lax.fori_loop(2, 4, mlp_tile, 0, unroll=2)
+    red[0].finish()
     sums(red[2], 0, d_spread, 0)
     gat[1].done()
+    red[1].finish()
     lax.fori_loop(BATCH, ITEMS, spread_item, 0, unroll=8)
     red[2].chips()
     lax.fori_loop(4, 6, mlp_tile, 0, unroll=2)
     lax.fori_loop(6, 8, mlp_tile, 0, unroll=2)
+    gat[0].finish()
+    gat[1].finish()
+    attend_back(0)
     sums(red[3], 1, d_spread, 0)
     stores = [pltpu.make_async_copy(mixed, mixed_hbm, load_sem.at[2])]
     stores[0].start()
-    attend_back(0)
-    red[3].chips()
 
     def put(f, p, lo, value):
         src_big[f % 2, (f // 2) * 2 + p % 2, p // 2, lo : lo + value.shape[0], :] = value
@@ -599,18 +605,14 @@
                     put(f, 2 * j + i, which * 64, grad[f * 64 : f * 64 + 64, i * 128 : i * 128 + 128])
 
     grad_mlp(0, norm_two, d_hidden)
+    red[3].chips()
     grad_mlp(1, cot_t, active)
+    gat[2].to_core()
     grad = nt(spread[...], d_branch[...]).astype(BF)
     for f in range(4):
         for p in range(8):
             lo = f * 64 + (p % 4) * 16
             put(f, p, 128, grad[lo : lo + 16, (p // 4) * 128 : (p // 4) * 128 + 128])
-    for k in (1, 2, 3, 0):
-        red_big.core(k)
-    gat[2].to_core()
-    attend_back(1)
-    for k in (1, 2, 3):
-        red_big.square(k)
     gat[2].done()
     block = iota((1, 2 * T), 1)
     block = jnp.where(block < T, block // DH % 2, jnp.where(block == T, 0, jnp.where(block == T + 16, 1, 2)))
@@ -665,11 +667,16 @@
         d_both[0:C, at] = nn(slicet[...], d_logits[:, at]).astype(BF)
         return carry
 
-    lax.fori_loop(0, BATCH, back_item, 0, unroll=4)
-    red_big.line()
-    gat[3].to_core()
+    lax.fori_loop(0, 4, back_item, 0, unroll=4)
+    attend_back(1)
+    for k in (1, 2, 3, 0):
+        red_big.core(k)
+    lax.fori_loop(4, BATCH, back_item, 0, unroll=4)
+    for k in (1, 2, 3):
+        red_big.square(k)
     lax.fori_loop(0, 4, mid_tile, 0, unroll=4)
     lax.fori_loop(0, 4, back_tile, 0, unroll=4)
+    gat[3].to_core()
     half_rows = [pl.ds(0, rows // 2), pl.ds(rows // 2, rows // 2)]
 
     def store_half(i):
@@ -678,9 +685,6 @@
         stores.append(c)
 
     store_half(0)
-    whole = red_big.result().astype(BF)
-    big[g.zown, g.y] = whole
-
     def copies(ref, base):
         part = ref.at[g.zown, g.y]
         cz = []
@@ -699,9 +703,10 @@
             cy.append(c)
         return cy
 
-    big_z = copies(big, 0)
     gat[3].done()
-    lax.fori_loop(BATCH, ITEMS, back_item, 0, unroll=4)
+    lax.fori_loop(BATCH, BATCH + 4, back_item, 0, unroll=4)
+    red_big.line()
+    lax.fori_loop(BATCH + 4, ITEMS, back_item, 0, unroll=4)
     lax.fori_loop(4, 8, mid_tile, 0, unroll=4)
 
     grads = [nt(normed[...], d_both[i * C : i * C + C, :]).astype(BF) for i in range(2)]
@@ -717,12 +722,14 @@
         part = nt(mid[i * 64 : i * 64 + 64, :], d_logits[i * 128 : i * 128 + 128, :])
         fold = fold + jnp.where(iota((DH, 128), 1) < G, part[0:DH], part[DH : 2 * DH])
     fold = jnp.where(iota((32, 128), 1) < G, fold + pltpu.roll(fold, G, 1), 0.0)
+    big[g.zown, g.y] = red_big.result().astype(BF)
+    big_z = copies(big, 0)
     for k in (1, 2, 3):
         red_late.square(k)
+    lax.fori_loop(4, 8, back_tile, 0, unroll=4)
     for k in range(1, zs):
         g.owned((g.z - k + zs) % zs, big_z[k - 1].wait_recv)
     big_y = to_y(big, y_sem.at[0])
-    lax.fori_loop(4, 8, back_tile, 0, unroll=4)
     store_half(1)
 
     ones = jnp.ones((8, 128), F32)
@@ -766,7 +773,7 @@
     sq_copies = []
     for k in range(1, 8):
         dev = g.core if k == 4 else g.xy(k)[1] if k < 4 else g.xy_other(k - 4)[1]
-        c = rcopy(sqb.at[here], sqb.at[here], sem.at[10, k], sem.at[11, k], dev)
+        c = rcopy(sqb.at[here], sqb.at[here], sq_sem.at[0, k], sq_sem.at[1, k], dev)
         c.start()
         sq_copies.append(c)
     late_y = to_y(late, y_sem.at[1])
@@ -803,7 +810,7 @@
         c.wait_send()
     for c in red_late.c2:
         c.wait_send()
-    for r in red + [red_big] + gat:
+    for r in red[2:] + [red_big] + gat[2:]:
         r.finish()
 
 
@@ -823,24 +830,25 @@
 def last_kernel(surface, volume, norm, mixed_p, grad_p, big, late, small_sum, *refs):
     hbm_states, hbm_outs = refs[0:16], refs[16:38]
     states, news = refs[38:54], refs[54:74]
-    rows_in, mixed_rows, mixed_low, grad_rows, in_sem, out_sem = refs[74:]
+    rows_in, mixed_in, mixed_rows, mixed_low, grad_rows, in_sem, out_sem = refs[74:]
     rows = mixed_low.shape[0]
     ins = [pltpu.make_async_copy(h, v, in_sem.at[i]) for i, (h, v) in enumerate(zip(hbm_states, states))]
     gp = pltpu.make_async_copy(grad_p, rows_in, in_sem.at[16])
-    gp.start()
-    for c in ins:
+    mp = pltpu.make_async_copy(mixed_p, mixed_in, in_sem.at[17])
+    for c in ins[4:8] + ins[0:4] + ins[8:] + [gp, mp]:
         c.start()
     starts, _, sizes, total = counts(surface, volume)
 
     row = iota((T + 8, 1), 0)
+    sub = iota((1, 8, 1), 1)
 
     def place(source, out):
-        blank = jnp.zeros((8, C), F32)
-
         def moved(b, base):
             first = pl.multiple_of(lax.div(base, jnp.int32(8)) * 8, 8)
-            tile = jnp.concatenate([source[b * T : b * T + T, :].astype(F32), blank], axis=0)
-            return first, base - first, pltpu.roll(tile, base - first, 0)
+            off = base - first
+            turn = pltpu.roll(source[b * T : b * T + T, :].astype(F32).reshape(T // 8, 8, C), off, 1)
+            later = jnp.where(sub >= off, turn[1:], turn[:-1])
+            return first, off, jnp.concatenate([turn[0:1], later, turn[-1:]], axis=0).reshape(T + 8, C)
 
         for b in range(ITEMS):
             first, off, tile = moved(b, starts[b])
@@ -852,21 +860,13 @@
             here = pl.ds(first, T + 8)
             out[here, :] = jnp.where(row >= sizes[b] + off, tile, out[here, :])
 
-    gp.wait()
-    place(rows_in, grad_rows)
-    outs = [pltpu.make_async_copy(grad_rows.at[pl.ds(0, rows), :], hbm_outs[1], out_sem.at[1])]
-    outs[0].start()
-    place(mixed_p, mixed_rows)
-    mixed_low[...] = mixed_rows[0:rows, :].astype(BF)
-    outs.append(pltpu.make_async_copy(mixed_low, hbm_outs[0], out_sem.at[0]))
-    outs[1].start()
-
+    outs = []
     attn, mlp, small_s, vector_s = [states[4 * i : 4 * i + 4] for i in range(4)]
     attn_new, mlp_new, small_new, vector_new = [news[5 * i : 5 * i + 5] for i in range(4)]
     factor = jnp.minimum(1.0, CLIP / norm[0, 0])
     everything = slice(None)
     both = (everything, everything)
-    for c in ins:
+    for c in ins[4:8]:
         c.wait()
     for z in range(ZO):
         for y in range(2):
@@ -882,6 +882,8 @@
             outs.append(c)
 
     send(5, 5)
+    for c in ins[0:4] + ins[8:]:
+        c.wait()
     for z in range(ZO):
         for y in range(2):
             p = z * 2 + y
@@ -898,6 +900,15 @@
     gvec = jnp.concatenate([small_sum[64:72, :], small_sum[72:80, :]], axis=1)[0:3, :]
     adamw(vector_s, vector_new, both, gvec, factor, RATE_VECTOR)
     send(10, 10)
+    gp.wait()
+    place(rows_in, grad_rows)
+    outs.append(pltpu.make_async_copy(grad_rows.at[pl.ds(0, rows), :], hbm_outs[1], out_sem.at[1]))
+    outs[-1].start()
+    mp.wait()
+    place(mixed_in, mixed_rows)
+    mixed_low[...] = mixed_rows[0:rows, :].astype(BF)
+    outs.append(pltpu.make_async_copy(mixed_low, hbm_outs[0], out_sem.at[0]))
+    outs[-1].start()
     for c in outs:
         c.wait()
 
@@ -916,7 +927,6 @@
     def units(n, depth):
         return pltpu.VMEM((n, 2, 4, ZO, depth, 128), BF)
 
-    line = max(zs, 8)
     scratch = [
         pltpu.VMEM((rows // T, T, C), BF), pltpu.VMEM((rows // T, T, C), BF), pltpu.VMEM((rows, C), BF),
         pltpu.VMEM((rows, C), F32), pltpu.SemaphoreType.DMA((5,)),
@@ -932,14 +942,16 @@
         pltpu.VMEM((DH, 256), F32),
         pltpu.VMEM((SM, 128), BF), pltpu.VMEM((SM, 128), BF), pltpu.VMEM((4, SM, 128), BF), pltpu.VMEM((zs, SM, 128), BF),
         pltpu.VMEM((zs, ZO, CL, 128), BF), pltpu.VMEM((8, 8, 128), F32),
-        pltpu.SemaphoreType.DMA((2, 9)), pltpu.SemaphoreType.DMA((2, line)), pltpu.SemaphoreType.DMA((2, 2, ZO)),
-        pltpu.SemaphoreType.DMA((12, line)),
+        pltpu.SemaphoreType.DMA((2, 9)), pltpu.SemaphoreType.DMA((2, max(zs, 4))), pltpu.SemaphoreType.DMA((2, 2, ZO)),
+        pltpu.SemaphoreType.DMA((6, max(zs, 4))), pltpu.SemaphoreType.DMA((2, 8)),
     ]
     for _ in range(4):
-        scratch += Direct.scratch(UN, zs)
+        scratch += Direct.scratch(UN, zs)[0:3]
+    for _ in range(2):
+        scratch += Direct.scratch(UN, zs)[3:5]
     for depth in (CB, CL):
         scratch += Reduce.scratch(depth, zs)
-    for _ in range(4):
+    for _ in range(2):
         scratch += Gather.scratch(zs)
     mixed_p, grad_p, big, late, small_sum, norm = pl.pallas_call(
         functools.partial(main_kernel, zs),
@@ -961,13 +973,13 @@
     outs = pl.pallas_call(
         last_kernel,
         out_shape=[sd((rows, C), BF), sd((rows, C), F32)] + everything,
-        in_specs=[smem, smem, smem, vmem, hbm, vmem, vmem, vmem] + [hbm] * 16,
+        in_specs=[smem, smem, smem, hbm, hbm, vmem, vmem, vmem] + [hbm] * 16,
         out_specs=[hbm] * 22,
         scratch_shapes=[pltpu.VMEM(v.shape, v.dtype) for v in state]
         + [pltpu.VMEM(v.shape, v.dtype) for v in everything]
         + [
-            pltpu.VMEM((rows, C), F32), pltpu.VMEM((rows + T, C), F32), pltpu.VMEM((rows, C), BF),
-            pltpu.VMEM((rows + T, C), F32), pltpu.SemaphoreType.DMA((17,)), pltpu.SemaphoreType.DMA((22,)),
+            pltpu.VMEM((rows, C), F32), pltpu.VMEM((rows, C), BF), pltpu.VMEM((rows + T, C), F32), pltpu.VMEM((rows, C), BF),
+            pltpu.VMEM((rows + T, C), F32), pltpu.SemaphoreType.DMA((18,)), pltpu.SemaphoreType.DMA((22,)),
         ],
         compiler_params=pltpu.CompilerParams(vmem_limit_bytes=60 << 20),
         name="last",

time: 109 us -> 101 us (0.927)
  Pallas kernels: 107 us -> 98.4 us
    pallas_call x1, Pallas kernels: 95.7 us -> 91.5 us  [body(): pl.pallas_call(functools.partial(main_kernel, zs), out_shape=[sd((rows, C...]
    pallas_call x1, Pallas kernels: 10.9 us -> 6.86 us  [body(): pl.pallas_call(last_kernel, out_shape=[sd((rows, C), BF), sd((rows, C), F...]
where the time goes in v4:
time: 101 us
  Pallas kernels  98.4 us (97%)
  between operations  2.42 us (2%)
    pallas_call x1, Pallas kernels, body(): pl.pallas_call(functools.partial(main_kernel, zs), out_shape=[sd((rows, C...  91.5 us
    pallas_call x1, Pallas kernels, body(): pl.pallas_call(last_kernel, out_shape=[sd((rows, C), BF), sd((rows, C), F...  6.86 us

profile of v4, /device:TPU:0, one launch (start us, length us, event | category | flops | bytes accessed | tf_op | source)
XLA Modules:
  0.0 100.8 jit_solution(7669314462907096551)
XLA Ops:
  0.7 91.5 %main.1 = (bf16[2048,256]{1,0:T(8,128)(2,1)}, f32[2048,256]{1,0:T(8,128)}, bf16[4,2,144,128]{3,2,1,0:T(8,128)(2,1)}, bf16[4,2,32,128]{3,2,1,0:T(8,128)(2,1)}, f32[80,128]{1,0:T(8,128)}, /*index=5*/f32[1,1]{1,0:T(1,128)}) custom-call(s32[1,16]{1,0:T(1,128)} %surface.3, s32[1,16]{1,0:T(1,128)} %volume.3, bf16[16,128,256]{2,1,0:T(8,128)(2,1)} %bitcast.3, ...), custom_call_target="tpu_custom_call" | custom-call | tf_op jit(solution)/shard_map/main/pallas_call | solution.py:956
  92.2 6.9 %last.1 = (bf16[2048,256]{1,0:T(8,128)(2,1)}, f32[2048,256]{1,0:T(8,128)}, f32[3,64,256]{2,1,0:T(8,128)}, f32[3,64,256]{2,1,0:T(8,128)}, f32[3,64,256]{2,1,0:T(8...) custom-call(s32[1,16]{1,0:T(1,128)} %surface.3, ...), custom_call_target="tpu_custom_call" | custom-call | tf_op jit(solution)/shard_map/last/pallas_call | solution.py:973

commit v5 on v4

--- a/solution.py
+++ b/solution.py
@@ -613,6 +613,8 @@
         for p in range(8):
             lo = f * 64 + (p % 4) * 16
             put(f, p, 128, grad[lo : lo + 16, (p // 4) * 128 : (p // 4) * 128 + 128])
+    for k in (1, 2, 3, 0):
+        red_big.core(k)
     gat[2].done()
     block = iota((1, 2 * T), 1)
     block = jnp.where(block < T, block // DH % 2, jnp.where(block == T, 0, jnp.where(block == T + 16, 1, 2)))
@@ -669,8 +671,6 @@
 
     lax.fori_loop(0, 4, back_item, 0, unroll=4)
     attend_back(1)
-    for k in (1, 2, 3, 0):
-        red_big.core(k)
     lax.fori_loop(4, BATCH, back_item, 0, unroll=4)
     for k in (1, 2, 3):
         red_big.square(k)
@@ -685,14 +685,18 @@
         stores.append(c)
 
     store_half(0)
-    def copies(ref, base):
+    def copies(ref):
         part = ref.at[g.zown, g.y]
-        cz = []
-        for k in range(1, zs):
-            c = rcopy(part, part, big_sem.at[base, k], big_sem.at[base + 1, k], g.zl(k)[1])
-            g.owned(g.z, c.start)
-            cz.append(c)
-        return cz
+        out = []
+        for j in range(zs - 1, -1, -1):
+            zz = (g.z + j) % zs
+            for i in range(2):
+                if i or j:
+                    dev = (zz * 2 + (1 - g.y if i else g.y), g.f)
+                    c = rcopy(part, part, big_sem.at[0, i, j], big_sem.at[1, i, j], dev)
+                    g.owned(g.z, c.start)
+                    out.append(((g.z - j + zs) % zs, c))
+        return out
 
     def to_y(ref, sem):
         cy = []
@@ -723,13 +727,10 @@
         fold = fold + jnp.where(iota((DH, 128), 1) < G, part[0:DH], part[DH : 2 * DH])
     fold = jnp.where(iota((32, 128), 1) < G, fold + pltpu.roll(fold, G, 1), 0.0)
     big[g.zown, g.y] = red_big.result().astype(BF)
-    big_z = copies(big, 0)
+    big_c = copies(big)
     for k in (1, 2, 3):
         red_late.square(k)
     lax.fori_loop(4, 8, back_tile, 0, unroll=4)
-    for k in range(1, zs):
-        g.owned((g.z - k + zs) % zs, big_z[k - 1].wait_recv)
-    big_y = to_y(big, y_sem.at[0])
     store_half(1)
 
     ones = jnp.ones((8, 128), F32)
@@ -758,6 +759,8 @@
         c = rcopy(sr2.at[g.m], sr2.at[g.m], sem.at[0, k], sem.at[1, k], g.xy(k)[1])
         c.start()
         cs.append(c)
+    for z, c in big_c:
+        g.owned(z, c.wait_recv)
     bigs = big[:, g.y].astype(F32).reshape(ZO * CB // 8, 8, 128)
     squares = jnp.sum(bigs * bigs, axis=0)
     for c in line_copies:
@@ -776,7 +779,7 @@
         c = rcopy(sqb.at[here], sqb.at[here], sq_sem.at[0, k], sq_sem.at[1, k], dev)
         c.start()
         sq_copies.append(c)
-    late_y = to_y(late, y_sem.at[1])
+    late_y = to_y(late, y_sem)
     for c in cs[1:4]:
         c.wait_recv()
     total = sr2[0].astype(F32)
@@ -787,7 +790,7 @@
         c = rcopy(sr3.at[g.z], sr3.at[g.z], sem.at[2, k], sem.at[3, k], g.zl(k)[1])
         c.start()
         cs.append(c)
-    for c in big_y + late_y + cs[4:]:
+    for c in late_y + cs[4:]:
         c.wait_recv()
     total = sr3[0].astype(F32)
     for z in range(1, zs):
@@ -800,11 +803,11 @@
         sq = sq + sqb[i]
     norm_out[0, 0] = jnp.sqrt(jnp.sum(sq) + jnp.sum(total * total))
 
-    for c in cs + line_copies + sq_copies + big_y + late_y + [a_x, a_c, a_f, o_x, o_c, o_f, m_x, m_c, m_f]:
+    for c in cs + line_copies + sq_copies + late_y + [a_x, a_c, a_f, o_x, o_c, o_f, m_x, m_c, m_f]:
         c.wait_send()
     for c in stores:
         c.wait()
-    for c in big_z:
+    for _, c in big_c:
         g.owned(g.z, c.wait_send)
     for c in red_late.c1.values():
         c.wait_send()
@@ -942,7 +945,7 @@
         pltpu.VMEM((DH, 256), F32),
         pltpu.VMEM((SM, 128), BF), pltpu.VMEM((SM, 128), BF), pltpu.VMEM((4, SM, 128), BF), pltpu.VMEM((zs, SM, 128), BF),
         pltpu.VMEM((zs, ZO, CL, 128), BF), pltpu.VMEM((8, 8, 128), F32),
-        pltpu.SemaphoreType.DMA((2, 9)), pltpu.SemaphoreType.DMA((2, max(zs, 4))), pltpu.SemaphoreType.DMA((2, 2, ZO)),
+        pltpu.SemaphoreType.DMA((2, 9)), pltpu.SemaphoreType.DMA((2, 2, zs)), pltpu.SemaphoreType.DMA((2, ZO)),
         pltpu.SemaphoreType.DMA((6, max(zs, 4))), pltpu.SemaphoreType.DMA((2, 8)),
     ]
     for _ in range(4):

time: 101 us -> 100 us (0.990)
  no operation moved by 1% of the time
where the time goes in v5:
time: 100 us
  Pallas kernels  97.8 us (98%)
  between operations  2.42 us (2%)
    pallas_call x1, Pallas kernels, body(): pl.pallas_call(functools.partial(main_kernel, zs), out_shape=[sd((rows, C...  90.9 us
    pallas_call x1, Pallas kernels, body(): pl.pallas_call(last_kernel, out_shape=[sd((rows, C), BF), sd((rows, C), F...  6.86 us

profile of v5, /device:TPU:0, one launch (start us, length us, event | category | flops | bytes accessed | tf_op | source)
XLA Modules:
  0.0 100.2 jit_solution(16182000805109950663)
XLA Ops:
  0.7 90.9 %main.1 = (bf16[2048,256]{1,0:T(8,128)(2,1)}, f32[2048,256]{1,0:T(8,128)}, bf16[4,2,144,128]{3,2,1,0:T(8,128)(2,1)}, bf16[4,2,32,128]{3,2,1,0:T(8,128)(2,1)}, f32[80,128]{1,0:T(8,128)}, /*index=5*/f32[1,1]{1,0:T(1,128)}) custom-call(s32[1,16]{1,0:T(1,128)} %surface.3, s32[1,16]{1,0:T(1,128)} %volume.3, bf16[16,128,256]{2,1,0:T(8,128)(2,1)} %bitcast.3, ...), custom_call_target="tpu_custom_call" | custom-call | tf_op jit(solution)/shard_map/main/pallas_call | solution.py:959
  91.6 6.9 %last.1 = (bf16[2048,256]{1,0:T(8,128)(2,1)}, f32[2048,256]{1,0:T(8,128)}, f32[3,64,256]{2,1,0:T(8,128)}, f32[3,64,256]{2,1,0:T(8,128)}, f32[3,64,256]{2,1,0:T(8...) custom-call(s32[1,16]{1,0:T(1,128)} %surface.3, ...), custom_call_target="tpu_custom_call" | custom-call | tf_op jit(solution)/shard_map/last/pallas_call | solution.py:976
